TPU v7x, 32 devices: a whole 2x2x4 slice. The times are simulated.
32 devices in a mesh: ctx: 4 (over x, core), fsdp: 8 (over z, y).
Axes of the slice: x: 2, y: 2, z: 4, core: 2. Of those that a mesh axis runs over, the one named last changes fastest.
Arguments:
- inputs: bfloat16 [8, 512, 2048], P('fsdp', 'ctx'), may hold values from -6 to 6
- doc_starts: int32 [8, 512], P('fsdp'), may hold values from 0 to 1, as said below
- routes: int32 [8, 512, 8], P('fsdp', 'ctx'), may hold values from 0 to 23, all different within a row; in each aligned block of 128 rows (0 to 127, 128 to 255, ..., all dimensions but the last counted through in order) at most 53 rows name the same one
- gate_weights: float32 [8, 512, 8], P('fsdp', 'ctx'), may hold values from 0.04 to 0.25
- qkv_w: bfloat16 [2048, 3, 2048], P('fsdp'), may hold values from -0.125 to 0.125
- out_w: bfloat16 [2048, 2048], P('fsdp'), may hold values from -2 to 2
- norm_gains: bfloat16 [2048, 2], P('fsdp'), may hold values from 0.5 to 1.5
- head_gains: bfloat16 [128, 2], P('fsdp'), may hold values from 0.5 to 1.5
- gate_up: bfloat16 [2048, 24, 2048], P('ctx', 'fsdp'), may hold values from -0.125 to 0.125
- down_t: bfloat16 [2048, 24, 1024], P('ctx', 'fsdp'), may hold values from -0.75 to 0.75
- cotangent: bfloat16 [8, 512, 2048], P('fsdp', 'ctx'), may hold values from -6 to 6
Outputs:
- block_out: bfloat16 [8, 512, 2048], P('fsdp', 'ctx')
- inputs_grad: float32 [8, 512, 2048], P('fsdp', 'ctx')
- qkv_w_grad: float32 [2048, 3, 2048], P('fsdp')
- out_w_grad: float32 [2048, 2048], P('fsdp')
- norm_gains_grad: float32 [2048, 2], P('fsdp')
- head_gains_grad: float32 [128, 2], P('fsdp')
- gate_up_grad: float32 [2048, 24, 2048], P('ctx', 'fsdp')
- down_t_grad: float32 [2048, 24, 1024], P('ctx', 'fsdp')
Inputs may be any that keep to these rules, and one draw needn't show every extreme that they name: `doc_starts`: 1 marks the first position of a document; position 0 of every stream is 1. `routes`: each row names 8 different experts; in the rows of one device no expert is named more than 53 times, a bound that some block reaches.
All inputs are finite; a program needn't handle non-finite values.
Results may differ from a plain program's by a relative error of at most 0.02.
Values may be sent and summed in bfloat16 or wider, within the bound.
No kernel may reach another device: no remote copies, remote signals or barrier semaphores. Data moves between devices by JAX's collectives and lax.ppermute only.
A program may use at most 384 MiB of HBM per device.

v0:
```python
import math

import jax
import jax.numpy as jnp
from jax import lax
from jax.sharding import PartitionSpec as P

EPS = 1e-06
ROPE_BASE = 10000.0
NEG_FILL = -1e30


def rms_scale(values, gain):
    return values * lax.rsqrt(jnp.mean(values * values, axis=-1, keepdims=True) + EPS) * gain


def rotate(values, cosine, sine_part):
    half_dim = values.shape[-1] // 2
    first = values[..., :half_dim]
    second = values[..., half_dim:]
    return jnp.concatenate(
        [first * cosine - second * sine_part, second * cosine + first * sine_part], axis=-1
    )


def body(
    inputs,
    doc_starts,
    routes,
    gate_weights,
    qkv_w,
    out_w,
    norm_gains,
    head_gains,
    gate_up,
    down_t,
    cotangent,
):
    tok_rows = inputs.shape[1]
    model_width = inputs.shape[2]
    head_dim = head_gains.shape[0] * lax.axis_size("fsdp")
    head_count = model_width // head_dim
    half_dim = head_dim // 2
    score_scale = head_dim ** (-0.5)
    top_count = routes.shape[2]
    hidden_units = down_t.shape[2]
    local_experts = gate_up.shape[1]
    experts_all = local_experts * lax.axis_size("fsdp")
    capacity = tok_rows * top_count * 5 // (experts_all * 4)
    stream_len = doc_starts.shape[1]
    key_width = min(512, stream_len)
    key_count = stream_len // key_width
    position = lax.axis_index("ctx") * tok_rows
    f32 = jnp.float32
    bf16 = jnp.bfloat16
    places = jnp.arange(stream_len, dtype=jnp.int32)
    starts = doc_starts[0]
    begins = lax.cummax(jnp.where(starts == 1, places, jnp.zeros_like(places)), axis=0)
    doc_ids = jnp.cumsum(starts)
    relative = places - begins
    local_docs = lax.dynamic_slice_in_dim(doc_ids, position, tok_rows)
    local_rel = lax.dynamic_slice_in_dim(relative, position, tok_rows)
    key_docs = doc_ids.reshape(key_count, key_width)
    frequency = jnp.exp(jnp.arange(half_dim, dtype=f32) * (-2.0 / head_dim) * math.log(ROPE_BASE))
    angles = local_rel.astype(f32)[:, None] * frequency[None, :]
    cosine = jnp.cos(angles)[:, None, :]
    sine_part = jnp.sin(angles)[:, None, :]
    qkv_full, out_full, norm_full, head_full = (
        lax.all_gather(qkv_w, "fsdp", axis=0, tiled=True),
        lax.all_gather(out_w, "fsdp", axis=0, tiled=True),
        lax.all_gather(norm_gains, "fsdp", axis=0, tiled=True),
        lax.all_gather(head_gains, "fsdp", axis=0, tiled=True),
    )
    x_rows = inputs[0].astype(f32)
    cot_rows = cotangent[0].astype(f32)
    a1_f32, norm_one_back = jax.vjp(rms_scale, x_rows, norm_full[:, 0].astype(f32))
    a1_low = a1_f32.astype(bf16)
    proj = jnp.einsum("td,djk->tjk", a1_low, qkv_full, preferred_element_type=f32)

    def prepare(q_flat, k_flat, q_gain, k_gain):
        q_heads = rms_scale(q_flat.reshape(tok_rows, head_count, head_dim), q_gain)
        k_heads = rms_scale(k_flat.reshape(tok_rows, head_count, head_dim), k_gain)
        return (rotate(q_heads, cosine, sine_part), rotate(k_heads, cosine, sine_part))

    (q_rot, k_rot), prepare_back = jax.vjp(
        prepare, proj[:, 0], proj[:, 1], head_full[:, 0].astype(f32), head_full[:, 1].astype(f32)
    )
    q_low = q_rot.astype(bf16)
    k_low = k_rot.reshape(tok_rows, model_width).astype(bf16)
    v_low = proj[:, 2].astype(bf16)
    keys_all, values_all = (
        lax.all_gather(k_low, "ctx", axis=0, tiled=True),
        lax.all_gather(v_low, "ctx", axis=0, tiled=True),
    )
    key_blocks = keys_all.reshape(key_count, key_width, head_count, head_dim)
    value_blocks = values_all.reshape(key_count, key_width, head_count, head_dim)

    def block_logits(key_block, doc_block):
        logits = (
            jnp.einsum("qhd,khd->hqk", q_low, key_block, preferred_element_type=f32) * score_scale
        )
        same_doc = (local_docs[:, None] == doc_block[None, :])[None]
        return jnp.where(same_doc, logits, NEG_FILL)

    def max_step(running, pieces):
        row_max, summed = running
        key_block, doc_block = pieces
        logits = block_logits(key_block, doc_block)
        new_max = jnp.maximum(row_max, jnp.max(logits, axis=2))
        summed = summed * jnp.exp(row_max - new_max) + jnp.sum(
            jnp.exp(logits - new_max[:, :, None]), axis=2
        )
        return ((new_max, summed), None)

    start_max = jnp.full((head_count, tok_rows), NEG_FILL, f32)
    (row_max, summed), _ = lax.scan(
        max_step, (start_max, jnp.zeros((head_count, tok_rows), f32)), (key_blocks, key_docs)
    )
    log_total = row_max + jnp.log(summed)

    def value_step(attn_acc, pieces):
        key_block, value_block, doc_block = pieces
        attn_probs = jnp.exp(block_logits(key_block, doc_block) - log_total[:, :, None])
        return (
            attn_acc
            + jnp.einsum(
                "hqk,khd->qhd", attn_probs.astype(bf16), value_block, preferred_element_type=f32
            ),
            None,
        )

    attn_acc, _ = lax.scan(
        value_step,
        jnp.zeros((tok_rows, head_count, head_dim), f32),
        (key_blocks, value_blocks, key_docs),
    )
    attn_low = attn_acc.reshape(tok_rows, model_width).astype(bf16)
    h_one = x_rows + jnp.dot(attn_low, out_full, preferred_element_type=f32)
    a2_f32, norm_two_back = jax.vjp(rms_scale, h_one, norm_full[:, 1].astype(f32))
    a2_low = a2_f32.astype(bf16)
    flat_routes = routes[0].reshape(tok_rows * top_count)
    onehot = (flat_routes[:, None] == jnp.arange(experts_all, dtype=jnp.int32)[None, :]).astype(
        jnp.int32
    )
    earlier = jnp.cumsum(onehot, axis=0) - onehot
    slot_in = jnp.sum(earlier * onehot, axis=1)
    slot_index = flat_routes * capacity + slot_in
    token_of = jnp.arange(tok_rows * top_count, dtype=jnp.int32) // top_count
    send_rows = (
        jnp.zeros((experts_all * capacity, model_width), bf16).at[slot_index].set(a2_low[token_of])
    )
    scaled = (
        (gate_weights[0][:, :, None] * cot_rows[:, None, :])
        .reshape(tok_rows * top_count, model_width)
        .astype(bf16)
    )
    send_grads = jnp.zeros((experts_all * capacity, model_width), bf16).at[slot_index].set(scaled)
    got_rows, got_grads = (
        lax.all_to_all(
            send_rows.reshape(experts_all, capacity, model_width),
            "fsdp",
            split_axis=0,
            concat_axis=1,
            tiled=True,
        ),
        lax.all_to_all(
            send_grads.reshape(experts_all, capacity, model_width),
            "fsdp",
            split_axis=0,
            concat_axis=1,
            tiled=True,
        ),
    )
    segment = lax.all_gather(gate_up, "ctx", axis=0, tiled=True)
    gate_add = jnp.einsum(
        "erd,dek->erk", got_rows, segment[:, :, :hidden_units], preferred_element_type=f32
    )
    up_add = jnp.einsum(
        "erd,dek->erk", got_rows, segment[:, :, hidden_units:], preferred_element_type=f32
    )
    sigmoid_g = jax.nn.sigmoid(gate_add)
    activated = gate_add * sigmoid_g
    hidden_low = (activated * up_add).astype(bf16)
    segment = lax.all_gather(down_t, "ctx", axis=0, tiled=True)
    made_block = jnp.einsum("erf,def->erd", hidden_low, segment, preferred_element_type=f32).astype(
        bf16
    )
    made_rows = made_block
    hidden_grad = jnp.einsum("erd,def->erf", got_grads, segment, preferred_element_type=f32)
    made_rows, hidden_grad = (made_rows, hidden_grad)
    gate_grad_low = (
        hidden_grad * up_add * sigmoid_g * (1.0 + gate_add * (1.0 - sigmoid_g))
    ).astype(bf16)
    up_grad_low = (hidden_grad * activated).astype(bf16)
    segment = lax.all_gather(gate_up, "ctx", axis=0, tiled=True)
    part_gate = jnp.einsum(
        "erk,dek->erd", gate_grad_low, segment[:, :, :hidden_units], preferred_element_type=f32
    )
    part_up = jnp.einsum(
        "erk,dek->erd", up_grad_low, segment[:, :, hidden_units:], preferred_element_type=f32
    )
    input_grads = (part_gate + part_up).astype(bf16)
    expert_sums = lax.psum_scatter(
        jnp.concatenate(
            [
                jnp.einsum("erd,erk->dek", got_rows, gate_grad_low, preferred_element_type=f32),
                jnp.einsum("erd,erk->dek", got_rows, up_grad_low, preferred_element_type=f32),
                jnp.einsum("erd,erf->def", got_grads, hidden_low, preferred_element_type=f32),
            ],
            axis=2,
        ).astype(jnp.bfloat16),
        "ctx",
        scatter_dimension=0,
        tiled=True,
    ).astype(jnp.float32)
    back_out, back_in = (
        lax.all_to_all(made_rows, "fsdp", split_axis=1, concat_axis=0, tiled=True),
        lax.all_to_all(input_grads, "fsdp", split_axis=1, concat_axis=0, tiled=True),
    )
    out_rows = back_out.reshape(experts_all * capacity, model_width)[slot_index].reshape(
        tok_rows, top_count, model_width
    )
    mixed = jnp.sum(gate_weights[0][:, :, None] * out_rows.astype(f32), axis=1)
    block_out = (h_one + mixed).astype(bf16)
    in_rows = back_in.reshape(experts_all * capacity, model_width)[slot_index].reshape(
        tok_rows, top_count, model_width
    )
    da2 = jnp.sum(in_rows.astype(f32), axis=1)
    dh_part, gain_two_grad = norm_two_back(da2)
    dh_one = cot_rows + dh_part
    dattn = dh_one.astype(bf16)
    out_grad_low = (
        jnp.einsum("tk,dk->td", dattn, out_full, preferred_element_type=f32)
        .astype(bf16)
        .reshape(tok_rows, head_count, head_dim)
    )
    row_delta = jnp.einsum("qhd,qhd->hq", out_grad_low.astype(f32), attn_acc)

    def grad_step(query_grad, pieces):
        key_block, value_block, doc_block = pieces
        attn_probs = jnp.exp(block_logits(key_block, doc_block) - log_total[:, :, None])
        prob_grad = jnp.einsum(
            "qhd,khd->hqk", out_grad_low, value_block, preferred_element_type=f32
        )
        logit_grad = (attn_probs * (prob_grad - row_delta[:, :, None])).astype(bf16)
        query_grad = (
            query_grad
            + jnp.einsum("hqk,khd->qhd", logit_grad, key_block, preferred_element_type=f32)
            * score_scale
        )
        key_grad = (
            jnp.einsum("hqk,qhd->khd", logit_grad, q_low, preferred_element_type=f32) * score_scale
        )
        value_grad = jnp.einsum(
            "hqk,qhd->khd", attn_probs.astype(bf16), out_grad_low, preferred_element_type=f32
        )
        return (query_grad, (key_grad, value_grad))

    query_grad, (key_grads, value_grads) = lax.scan(
        grad_step,
        jnp.zeros((tok_rows, head_count, head_dim), f32),
        (key_blocks, value_blocks, key_docs),
    )
    key_sum, value_sum = (
        lax.psum_scatter(
            key_grads.reshape(stream_len, model_width).astype(jnp.bfloat16),
            "ctx",
            scatter_dimension=0,
            tiled=True,
        ).astype(jnp.float32),
        lax.psum_scatter(
            value_grads.reshape(stream_len, model_width).astype(jnp.bfloat16),
            "ctx",
            scatter_dimension=0,
            tiled=True,
        ).astype(jnp.float32),
    )
    key_low = key_sum.astype(bf16).astype(f32).reshape(tok_rows, head_count, head_dim)
    query_low = query_grad.astype(bf16).astype(f32)
    dq_proj, dk_proj, q_gain_grad, k_gain_grad = prepare_back((query_low, key_low))
    proj_grad = jnp.stack([dq_proj, dk_proj, value_sum], axis=1).astype(bf16)
    da1 = jnp.einsum("tjk,djk->td", proj_grad, qkv_full, preferred_element_type=f32)
    dx_part, gain_one_grad = norm_one_back(da1)
    inputs_grad = dh_one + dx_part
    projections = jnp.einsum("td,tjk->djk", a1_low, proj_grad, preferred_element_type=f32)
    output_part = jnp.einsum("td,tk->dk", attn_low, dattn, preferred_element_type=f32)
    attn_shard = lax.psum_scatter(
        jnp.concatenate([projections, output_part[:, None, :]], axis=1).astype(jnp.bfloat16),
        "fsdp",
        scatter_dimension=0,
        tiled=True,
    )
    norm_part = jnp.stack([gain_one_grad, gain_two_grad], axis=1)
    head_part = jnp.stack([q_gain_grad, k_gain_grad], axis=1)
    norm_shard, head_shard = (
        lax.psum_scatter(norm_part, "fsdp", scatter_dimension=0, tiled=True),
        lax.psum_scatter(head_part, "fsdp", scatter_dimension=0, tiled=True),
    )
    totals = (
        lax.psum(attn_shard, "ctx").astype(jnp.float32),
        lax.psum(norm_shard.astype(jnp.bfloat16), "ctx").astype(jnp.float32),
        lax.psum(head_shard.astype(jnp.bfloat16), "ctx").astype(jnp.float32),
    )
    return (
        block_out[None],
        inputs_grad[None],
        totals[0][:, :3, :],
        totals[0][:, 3, :],
        totals[1],
        totals[2],
        expert_sums[:, :, : 2 * hidden_units],
        expert_sums[:, :, 2 * hidden_units :],
    )


def solution(mesh):
    return jax.shard_map(
        body,
        mesh=mesh,
        in_specs=(
            P("fsdp", "ctx", None),
            P("fsdp", None),
            P("fsdp", "ctx", None),
            P("fsdp", "ctx", None),
            P("fsdp", None, None),
            P("fsdp", None),
            P("fsdp", None),
            P("fsdp", None),
            P("ctx", "fsdp", None),
            P("ctx", "fsdp", None),
            P("fsdp", "ctx", None),
        ),
        out_specs=(
            P("fsdp", "ctx", None),
            P("fsdp", "ctx", None),
            P("fsdp", None, None),
            P("fsdp", None),
            P("fsdp", None),
            P("fsdp", None),
            P("ctx", "fsdp", None),
            P("ctx", "fsdp", None),
        ),
        check_vma=False,
    )
```

profile of v0, /device:TPU:0, one launch (start us, length us, event | category | flops | bytes accessed | tf_op | source)
XLA Modules:
  0.0 2599.0 jit_solution(13533799499513804395)
XLA Ops:
  7.9 50.7 %all_gather.25 = bf16[2048,2]{0,1:T(2,128)(2,1)S(1)} all-gather(bf16[256,2]{0,1:T(2,128)(2,1)} %param.17), channel_id=1, replica_groups=mesh['ctx'=4,'fsdp'=8] {'fsdp'}, dimensions={0}, use_global_device_ids=true | all-gather | bytes 9216 | tf_op jit(solution)/shard_map/all_gather | solution.py:71
  60.5 432.3 %all-gather.9.cloned.1.call-done = bf16[2048,3,2048]{2,0,1:T(8,128)(2,1)} async-done(((bf16[256,3,2048]{2,0,1:T(8,128)(2,1)}), bf16[2048,3,2048]{2,0,1:T(8,128)(2,1)}) %all-gather.9.cloned.1.call-update) | async-done | bytes 25165840 | tf_op jit(solution)/shard_map/all_gather | solution.py:69
  504.5 19.2 all-gather.1
  575.0 207.0 %all-gather.13.cloned.1.call-done = bf16[2048,2048]{1,0:T(8,128)(2,1)} async-done(((bf16[256,2048]{1,0:T(8,128)(2,1)}), bf16[2048,2048]{1,0:T(8,128)(2,1)}) %all-gather.13.cloned.1.call-update) | async-done | bytes 8388624 | tf_op jit(solution)/shard_map/all_gather | solution.py:70
  787.9 23.4 scatter_custom_fusion
  835.5 29.1 %all-gather.17.cloned.1.call-done = bf16[2048,3,1024]{2,0,1:T(8,128)(2,1)} async-done(((bf16[512,3,1024]{2,0,1:T(8,128)(2,1)}), bf16[2048,3,1024]{2,0,1:T(8,128)(2,1)}) %all-gather.17.cloned.1.call-update) | async-done | bytes 12582928 | tf_op jit(solution)/shard_map/all_gather | solution.py:184
  864.6 11.8 fusion.69
  876.4 68.4 %all-to-all-done = bf16[24,53,2048]{2,1,0:T(8,128)(2,1)} async-done(((bf16[24,53,2048]{2,1,0:T(8,128)(2,1)}), bf16[24,53,2048]{2,1,0:T(8,128)(2,1)}, u32[]{:S(2)}, u32[]{:S(2)}) %all-to-all-start) | async-done | bytes 5210144 | tf_op jit(solution)/shard_map/all_to_all | solution.py:159
  957.2 63.6 %all-gather.15.cloned.1.call-done = bf16[2048,3,2048]{2,0,1:T(8,128)(2,1)} async-done(((bf16[512,3,2048]{2,0,1:T(8,128)(2,1)}), bf16[2048,3,2048]{2,0,1:T(8,128)(2,1)}) %all-gather.15.cloned.1.call-update) | async-done | bytes 25165840 | tf_op jit(solution)/shard_map/all_gather | solution.py:174
  1020.8 11.6 fusion.2
  1032.4 15.5 multiply_convert_fusion.1
  1047.9 12.0 convolution_convert_fusion.1
  1075.2 11.8 fusion
  1087.0 15.7 add_convert_fusion
  1112.5 115.3 %all-to-all-done.1 = bf16[3,424,2048]{2,0,1:T(4,128)(2,1)} async-done(((bf16[3,424,2048]{2,0,1:T(4,128)(2,1)}), bf16[3,424,2048]{2,0,1:T(4,128)(2,1)}, u32[]{:S(2)}, u32[]{:S(2)}) %all-to-all-start.1) | async-done | bytes 5210144 | tf_op jit(solution)/shard_map/all_to_all | solution.py:217
  1249.2 135.3 %all-to-all-done.3 = bf16[3,424,2048]{2,0,1:T(4,128)(2,1)} async-done(((bf16[3,424,2048]{2,0,1:T(4,128)(2,1)}), bf16[3,424,2048]{2,0,1:T(4,128)(2,1)}, u32[]{:S(2)}, u32[]{:S(2)}) %all-to-all-start.3) | async-done | bytes 5210144 | tf_op jit(solution)/shard_map/all_to_all | solution.py:218
  1400.3 12.0 gather_fusion
  1412.3 12.1 gather_fusion.1
  1473.1 14.0 reduce-scatter.19.cloned.1.call-done
  1502.5 19.3 reduce-scatter.13.cloned.1.call-done
  1521.8 12.8 convolution_convert_fusion
  1534.7 22.9 pad_maximum_fusion.1
  1557.6 12.4 convert_bitcast_fusion
  1570.0 12.3 convert_bitcast_fusion.2
  1592.9 14.8 fusion.33
  1609.2 27.5 %pad_maximum_fusion = bf16[2048,3,3072]{0,2,1:T(8,128)(2,1)} fusion(bf16[2048,3,1024]{0,2,1:T(8,128)(2,1)} %convert_bitcast_fusion, bf16[2048,3,1024]{0,2,1:T(8,128)(2,1)} %convert_bitcast_fusion.1, bf16[2048,3,1024]{0,2,1:T(8,128)(2,1)} %convert_bitcast_fusion.2), kind=kLoop, calls=%fused_computation.5 | loop fusion | flops 113246208 | bytes 75497472 | tf_op jit(solution)/shard_map/concatenate | solution.py:204
  1636.8 463.8 %reduce-scatter.15.cloned.1.call-done = bf16[256,4,2048]{2,0,1:T(8,128)(2,1)} async-done(((bf16[2048,4,2048]{2,0,1:T(8,128)(2,1)}), bf16[256,4,2048]{2,0,1:T(8,128)(2,1)}) %reduce-scatter.15.cloned.1.call-update) | async-done | bytes 4194320 | tf_op jit(solution)/shard_map/reduce_scatter | solution.py:287
  2101.9 62.9 %reduce-scatter.23.cloned.1.call-done = f32[16,2]{1,0:T(8,128)} async-done(((f32[128,2]{1,0:T(8,128)}), f32[16,2]{1,0:T(8,128)}) %reduce-scatter.23.cloned.1.call-update) | async-done | bytes 144
  2165.6 65.7 %reduce-scatter.21.cloned.1.call-done = f32[256,2]{1,0:T(8,128)} async-done(((f32[2048,2]{1,0:T(8,128)}), f32[256,2]{1,0:T(8,128)}) %reduce-scatter.21.cloned.1.call-update) | async-done | bytes 2064
  2239.1 255.4 %reduce-scatter.17.cloned.1.call-done = bf16[512,3,3072]{0,2,1:T(8,128)(2,1)} async-done(((bf16[2048,3,3072]{0,2,1:T(8,128)(2,1)}), bf16[512,3,3072]{0,2,1:T(8,128)(2,1)}) %reduce-scatter.17.cloned.1.call-update) | async-done | bytes 9437200 | tf_op jit(solution)/shard_map/reduce_scatter | solution.py:203
  2515.8 12.8 copy.205
  2528.6 53.8 %all-reduce.7.cloned.1.call-done = bf16[256,4,2048]{2,0,1:T(8,128)(2,1)} async-done(((bf16[256,4,2048]{2,0,1:T(8,128)(2,1)}), bf16[256,4,2048]{2,0,1:T(8,128)(2,1)}) %all-reduce.7.cloned.1.call-update) | async-done | bytes 4194320 | tf_op jit(solution)/shard_map/psum | solution.py:300
  (304 shorter events, 286.4 us)
Async XLA Ops:
  7.2 485.6 %all-gather.9.cloned.1.call-start = ((), (), s32[]{:S(2)}) async-start(), calls=%async_computation.10 | async-start | bytes 28311552 | tf_op jit(solution)/shard_map/all_gather | solution.py:69
  7.9 555.2 %all-gather.19.cloned.1.call-start = ((), (), s32[]{:S(2)}) async-start(), calls=%async_computation.19 | async-start | bytes 2621440 | tf_op jit(solution)/shard_map/all_gather | solution.py:93
  60.5 442.6 %copy-start.47 = (f32[128]{0:T(128)}, f32[128]{0:T(128)S(1)}, u32[]{:S(2)}) copy-start(f32[128]{0:T(128)S(1)} %fusion.58) | copy-start | bytes 1540
  60.5 442.6 %copy-start.31 = (f32[2048,1]{0,1:T(1,128)}, f32[2048,1]{0,1:T(1,128)S(1)}, u32[]{:S(2)}) copy-start(f32[2048,1]{0,1:T(1,128)S(1)} %get-tuple-element.161) | copy-start | bytes 24580
  60.5 726.4 %copy-start.33 = (f32[2048,1]{0,1:T(1,128)}, f32[2048,1]{0,1:T(1,128)S(1)}, u32[]{:S(2)}) copy-start(f32[2048,1]{0,1:T(1,128)S(1)} %get-tuple-element.160) | copy-start | bytes 24580
  504.0 63.0 %all-gather.11.cloned.1.call-start = ((), (), s32[]{:S(2)}) async-start(), calls=%async_computation.11 | async-start | bytes 2621440 | tf_op jit(solution)/shard_map/all_gather | solution.py:92
  529.6 37.3 %copy-start.15 = (bf16[128,16,64]{2,0,1:T(8,128)(2,1)}, bf16[128,16,64]{2,0,1:T(8,128)(2,1)S(1)}, u32[]{:S(2)}) copy-start(bf16[128,16,64]{2,0,1:T(8,128)(2,1)S(1)} %get-tuple-element.148) | copy-start | bytes 786436
  529.7 37.3 %copy-start.17 = (bf16[128,16,64]{2,0,1:T(8,128)(2,1)}, bf16[128,16,64]{2,0,1:T(8,128)(2,1)S(1)}, u32[]{:S(2)}) copy-start(bf16[128,16,64]{2,0,1:T(8,128)(2,1)S(1)} %get-tuple-element.149) | copy-start | bytes 786436
  531.0 251.0 %all-gather.13.cloned.1.call-start = ((), (), s32[]{:S(2)}) async-start(), calls=%async_computation.12 | async-start | bytes 9437184 | tf_op jit(solution)/shard_map/all_gather | solution.py:70
  531.6 332.9 %all-gather.17.cloned.1.call-start = ((), (), s32[]{:S(2)}) async-start(), calls=%async_computation.14 | async-start | bytes 15728640 | tf_op jit(solution)/shard_map/all_gather | solution.py:184
  532.2 488.6 %all-gather.15.cloned.1.call-start = ((), (), s32[]{:S(2)}) async-start(), calls=%async_computation.13 | async-start | bytes 31457280 | tf_op jit(solution)/shard_map/all_gather | solution.py:174
  557.6 260.7 %all-to-all-start.2 = ((bf16[24,53,2048]{2,1,0:T(8,128)(2,1)}), bf16[24,53,2048]{2,1,0:T(8,128)(2,1)}, u32[]{:S(2)}, u32[]{:S(2)}) async-start(bf16[24,53,2048]{2,1,0:T(8,128)(2,1)} %reshape.418), calls=%async_computation.2 | async-start | bytes 11010048 | tf_op jit(solution)/shard_map/all_to_all | solution.py:166
  571.1 210.9 %copy-start.8 = (bf16[1,128,2048]{2,1,0:T(8,128)(2,1)S(1)}, bf16[1,128,2048]{2,1,0:T(8,128)(2,1)}, u32[]{:S(2)}) copy-start(bf16[1,128,2048]{2,1,0:T(8,128)(2,1)} %param.11) | copy-start | bytes 1572868
  571.2 215.6 %copy-start.43 = (f32[16,128]{1,0:T(8,128)}, f32[16,128]{1,0:T(8,128)S(1)}, u32[]{:S(2)}) copy-start(f32[16,128]{1,0:T(8,128)S(1)} %log_add_fusion) | copy-start | bytes 24580
  575.0 211.8 %copy-start.13 = (bf16[128,16,128]{0,2,1:T(8,128)(2,1)}, bf16[128,16,128]{0,2,1:T(8,128)(2,1)S(1)}, u32[]{:S(2)}) copy-start(bf16[128,16,128]{0,2,1:T(8,128)(2,1)S(1)} %get-tuple-element.168) | copy-start | bytes 1572868
  786.8 31.4 %copy-start.56 = (f32[128]{0:T(128)}, f32[128]{0:T(128)S(1)}, u32[]{:S(2)}) copy-start(f32[128]{0:T(128)S(1)} %get-tuple-element.170) | copy-start | bytes 1540
  786.8 31.4 %copy-start.54 = (f32[128]{0:T(128)}, f32[128]{0:T(128)S(1)}, u32[]{:S(2)}) copy-start(f32[128]{0:T(128)S(1)} %fusion.59) | copy-start | bytes 1540
  818.3 126.5 %all-to-all-start = ((bf16[24,53,2048]{2,1,0:T(8,128)(2,1)}), bf16[24,53,2048]{2,1,0:T(8,128)(2,1)}, u32[]{:S(2)}, u32[]{:S(2)}) async-start(bf16[24,53,2048]{2,1,0:T(8,128)(2,1)} %reshape.416), calls=%async_computation | async-start | bytes 11010048 | tf_op jit(solution)/shard_map/all_to_all | solution.py:159
  1047.9 39.0 %copy-start.61 = (bf16[3,424,1024]{2,1,0:T(8,128)(2,1)}, bf16[3,424,1024]{2,1,0:T(8,128)(2,1)S(1)}, u32[]{:S(2)}) copy-start(bf16[3,424,1024]{2,1,0:T(8,128)(2,1)S(1)} %get-tuple-element.139) | copy-start | bytes 7815172
  1069.7 158.2 %all-to-all-start.1 = ((bf16[3,424,2048]{2,0,1:T(4,128)(2,1)}), bf16[3,424,2048]{2,0,1:T(4,128)(2,1)}, u32[]{:S(2)}, u32[]{:S(2)}) async-start(bf16[3,424,2048]{2,0,1:T(4,128)(2,1)} %copy.180), calls=%async_computation.1 | async-start | bytes 13893632 | tf_op jit(solution)/shard_map/all_to_all | solution.py:217
  1227.9 156.7 %all-to-all-start.3 = ((bf16[3,424,2048]{2,0,1:T(4,128)(2,1)}), bf16[3,424,2048]{2,0,1:T(4,128)(2,1)}, u32[]{:S(2)}, u32[]{:S(2)}) async-start(bf16[3,424,2048]{2,0,1:T(4,128)(2,1)} %copy.185), calls=%async_computation.3 | async-start | bytes 13893632 | tf_op jit(solution)/shard_map/all_to_all | solution.py:218
  1232.8 254.3 %reduce-scatter.19.cloned.1.call-start = ((), (), s32[]{:S(2)}) async-start(), calls=%async_computation.20 | async-start | bytes 2621440
  1457.4 64.4 %reduce-scatter.13.cloned.1.call-start = ((), (), s32[]{:S(2)}) async-start(), calls=%async_computation.15 | async-start | bytes 2621440 | tf_op jit(solution)/shard_map/reduce_scatter | solution.py:271
  1466.5 634.1 %reduce-scatter.15.cloned.1.call-start = ((), (), s32[]{:S(2)}) async-start(), calls=%async_computation.16 | async-start | bytes 37748736 | tf_op jit(solution)/shard_map/reduce_scatter | solution.py:287
  1497.4 24.4 copy-start.9
  1557.5 607.3 %reduce-scatter.23.cloned.1.call-start = ((), (), s32[]{:S(2)}) async-start(), calls=%async_computation.22 | async-start | bytes 73728
  1557.6 24.7 slice-start.2
  1592.8 638.5 %reduce-scatter.21.cloned.1.call-start = ((), (), s32[]{:S(2)}) async-start(), calls=%async_computation.21 | async-start | bytes 1179648
  1609.1 885.4 %reduce-scatter.17.cloned.1.call-start = ((), (), s32[]{:S(2)}) async-start(), calls=%async_computation.18 | async-start | bytes 47185920 | tf_op jit(solution)/shard_map/reduce_scatter | solution.py:203
  1636.7 463.9 %copy-start.59 = (f32[128]{0:T(128)S(1)}, f32[128]{0:T(128)}, u32[]{:S(2)}) copy-start(f32[128]{0:T(128)} %copy-done.58) | copy-start | bytes 1540
  1636.7 464.0 %copy-start.25 = (f32[128,2048]{1,0:T(8,128)S(1)}, f32[128,2048]{1,0:T(8,128)}, u32[]{:S(2)}) copy-start(f32[128,2048]{1,0:T(8,128)} %get-tuple-element.172) | copy-start | bytes 3145732
  1636.8 945.7 %all-reduce.7.cloned.1.call-start = ((), (), s32[]{:S(2)}) async-start(), calls=%async_computation.17 | async-start | bytes 8388608 | tf_op jit(solution)/shard_map/psum | solution.py:300
  (53 other events, 378.7 us)
Sparse Core Ops, SparseCore 0:
  9.5 483.2 all-gather.8
  504.1 22.5 all-gather.18
  531.1 20.5 all-gather.10
  553.7 228.2 all-gather.12
  783.4 81.0 all-gather.16
  866.0 154.8 all-gather.14
  1457.5 29.5 reduce-scatter.18
  1490.3 31.4 reduce-scatter.12
  1557.7 542.9 reduce-scatter.14
  2104.4 60.3 reduce-scatter.22
  2168.8 62.4 reduce-scatter.20
  2234.0 260.5 reduce-scatter.16
  2496.9 85.5 all-reduce.6
where the time goes:
time: 2610 us; the launch traced here: 2600 us
  waiting for transfers between devices  1990 us (76%)
  local copies, waits for them, and re-layouts  213 us (8%)
  matrix products  184 us (7%)
  other arithmetic  102 us (4%)
  blocking collectives  75.5 us (3%)
    reduce_scatter x1, waiting for transfers between devices, body(): lax.psum_scatter(jnp.concatenate([projections, output_part[:, None, :]],...  464 us
    all_gather x1, waiting for transfers between devices, body(): lax.all_gather(qkv_w, 'fsdp', axis=0, tiled=True)  432 us
    reduce_scatter x1, waiting for transfers between devices, body(): lax.psum_scatter(jnp.concatenate([jnp.einsum('erd,erk->dek', got_rows, ga...  255 us
    all_gather x1, waiting for transfers between devices, body(): lax.all_gather(out_w, 'fsdp', axis=0, tiled=True)  207 us
    unnamed x16, waiting for transfers between devices  145 us
    all_to_all x1, waiting for transfers between devices, body(): lax.all_to_all(input_grads, 'fsdp', split_axis=1, concat_axis=0, tiled=True)  135 us
    all_to_all x1, waiting for transfers between devices, body(): lax.all_to_all(made_rows, 'fsdp', split_axis=1, concat_axis=0, tiled=True)  115 us
    all_to_all x1, waiting for transfers between devices, body(): lax.all_to_all(send_rows.reshape(experts_all, capacity, model_width), 'fs...  68.4 us
  transfers between devices with their start and end apart: 17, of which 14 were waited for; matrix products, arithmetic and copies ran while one was open for 12% of the time, Pallas kernels for 0%

commit v1 on v0

v1 whole, which is shorter than its diff:
```python
import math

import jax
import jax.numpy as jnp
from jax import lax
from jax.sharding import PartitionSpec as P

EPS = 1e-06
ROPE_BASE = 10000.0
NEG_FILL = -1e30
f32 = jnp.float32
bf16 = jnp.bfloat16


def rms_scale(values, gain):
    return values * lax.rsqrt(jnp.mean(values * values, axis=-1, keepdims=True) + EPS) * gain


def rotate(values, cosine, sine_part):
    half_dim = values.shape[-1] // 2
    first = values[..., :half_dim]
    second = values[..., half_dim:]
    return jnp.concatenate(
        [first * cosine - second * sine_part, second * cosine + first * sine_part], axis=-1
    )


def swap(value, axis, mask):
    size = lax.axis_size(axis)
    return lax.ppermute(value, axis, [(i, i ^ mask) for i in range(size)])


def bits_down(size):
    return [1 << b for b in reversed(range(size.bit_length() - 1))]


def gather_ctx(block):
    pieces = {0: block}
    for bit in bits_down(lax.axis_size("ctx")):
        pieces.update({q | bit: swap(piece, "ctx", bit) for q, piece in list(pieces.items())})
    return [pieces[q] for q in range(len(pieces))]


def scatter_ctx(blocks):
    size = lax.axis_size("ctx")
    current = dict(enumerate(blocks))
    for bit in reversed(bits_down(size)):
        current = {
            q: current[q].astype(f32) + swap(current[q | bit].astype(bf16), "ctx", bit).astype(f32)
            for q in current
            if not q & bit
        }
    return current[0]


def gather_fsdp(block):
    size = lax.axis_size("fsdp")
    even = {0: block}
    even.update({m: swap(block, "fsdp", m) for m in range(2, size, 2)})
    out = [None] * size
    for q, piece in even.items():
        out[q] = piece
        out[q | 1] = swap(piece, "fsdp", 1)
    return out


def scatter_fsdp(blocks):
    size = lax.axis_size("fsdp")
    even = {
        q: blocks[q].astype(f32) + swap(blocks[q | 1].astype(bf16), "fsdp", 1).astype(f32)
        for q in range(0, size, 2)
    }
    total = even[0]
    for m in range(2, size, 2):
        total = total + swap(even[m].astype(bf16), "fsdp", m).astype(f32)
    return total


def xor_blocks(values, index, count):
    shape = values.shape
    width = shape[-1] // count
    for bit in bits_down(count):
        parts = values.reshape(shape[:-1] + (count // (2 * bit), 2, bit * width))
        flipped = jnp.concatenate([parts[..., 1:, :], parts[..., :1, :]], axis=-2)
        values = jnp.where((index & bit) != 0, flipped, parts).reshape(shape)
    return values


def body(
    inputs,
    doc_starts,
    routes,
    gate_weights,
    qkv_w,
    out_w,
    norm_gains,
    head_gains,
    gate_up,
    down_t,
    cotangent,
):
    n_ctx, n_fsdp = lax.axis_size("ctx"), lax.axis_size("fsdp")
    c, f = lax.axis_index("ctx"), lax.axis_index("fsdp")
    tok_rows, model_width = inputs.shape[1:]
    head_dim = head_gains.shape[0] * n_fsdp
    own_width = model_width // n_ctx
    own_heads = own_width // head_dim
    score_scale = head_dim ** (-0.5)
    top_count = routes.shape[2]
    hidden_units = down_t.shape[2]
    local_experts = gate_up.shape[1]
    experts_all = local_experts * n_fsdp
    capacity = tok_rows * top_count * 5 // (experts_all * 4)
    slots = n_fsdp * capacity
    stream_len = doc_starts.shape[1]
    half_dim = head_dim // 2

    x_low = inputs[0]
    x_rows = x_low.astype(f32)
    cot_low = cotangent[0]
    cot_rows = cot_low.astype(f32)

    x_all = jnp.concatenate(gather_ctx(xor_blocks(x_low, f, n_fsdp)), axis=0)
    qkv_own = lax.dynamic_slice_in_dim(qkv_w, c * own_width, own_width, axis=2)
    qkv_all = jnp.concatenate(gather_fsdp(qkv_own), axis=0)
    units = n_ctx * n_fsdp
    out_piece_rows = out_w.shape[0] // n_ctx
    flat = lambda ci, fi: ci * n_fsdp + fi
    to_heads = [(flat(u % n_ctx, u // n_ctx), flat(u // n_fsdp, u % n_fsdp)) for u in range(units)]
    out_piece = lax.ppermute(
        lax.dynamic_slice_in_dim(out_w, c * out_piece_rows, out_piece_rows, axis=0),
        ("ctx", "fsdp"),
        to_heads,
    )
    out_pieces = gather_fsdp(out_piece)
    out_own = jnp.zeros((own_width, model_width), bf16)
    for q, piece in enumerate(out_pieces):
        out_own = lax.dynamic_update_slice_in_dim(out_own, piece, (f ^ q) * out_piece_rows, axis=0)

    gains = lax.all_gather(
        jnp.concatenate([norm_gains, head_gains], axis=0).T, "fsdp", axis=0
    ).astype(f32)
    norm_one = gains[:, 0, : norm_gains.shape[0]].reshape(model_width)
    norm_two = gains[:, 1, : norm_gains.shape[0]].reshape(model_width)
    head_q = gains[:, 0, norm_gains.shape[0] :].reshape(head_dim)
    head_k = gains[:, 1, norm_gains.shape[0] :].reshape(head_dim)

    cot_all = jnp.concatenate(gather_fsdp(xor_blocks(cot_low, c, n_ctx)), axis=0)
    gate_up_all = [
        jnp.concatenate(gather_ctx(gate_up[:, e, :]), axis=0) for e in range(local_experts)
    ]
    down_all = [jnp.concatenate(gather_ctx(down_t[:, e, :]), axis=0) for e in range(local_experts)]

    places = jnp.arange(stream_len, dtype=jnp.int32)
    spots = ((c ^ (places // tok_rows)) * tok_rows + places % tok_rows).astype(jnp.int32)
    starts = doc_starts[0]
    reach = spots[:, None] >= places[None, :]
    doc_ids = jnp.sum(jnp.where(reach, starts[None, :], 0), axis=1)
    begins = jnp.max(jnp.where(reach & (starts[None, :] == 1), places[None, :], 0), axis=1)
    relative = spots - begins
    same_doc = (doc_ids[:, None] == doc_ids[None, :])[None]
    frequency = jnp.exp(jnp.arange(half_dim, dtype=f32) * (-2.0 / head_dim) * math.log(ROPE_BASE))
    angles = relative.astype(f32)[:, None] * frequency[None, :]
    cosine = jnp.cos(angles)[:, None, :]
    sine_part = jnp.sin(angles)[:, None, :]

    a1 = rms_scale(x_all.astype(f32), xor_blocks(norm_one, f, n_fsdp)).astype(bf16)
    proj = jnp.einsum("td,djk->tjk", a1, qkv_all, preferred_element_type=f32)

    def prepare(q_flat, k_flat, q_gain, k_gain):
        q_heads = rms_scale(q_flat.reshape(stream_len, own_heads, head_dim), q_gain)
        k_heads = rms_scale(k_flat.reshape(stream_len, own_heads, head_dim), k_gain)
        return (rotate(q_heads, cosine, sine_part), rotate(k_heads, cosine, sine_part))

    (q_rot, k_rot), prepare_back = jax.vjp(prepare, proj[:, 0], proj[:, 1], head_q, head_k)
    q_low = q_rot.astype(bf16)
    k_low = k_rot.astype(bf16)
    v_low = proj[:, 2].reshape(stream_len, own_heads, head_dim).astype(bf16)
    logits = jnp.einsum("qhd,khd->hqk", q_low, k_low, preferred_element_type=f32) * score_scale
    logits = jnp.where(same_doc, logits, NEG_FILL)
    probs = jax.nn.softmax(logits, axis=-1)
    probs_low = probs.astype(bf16)
    attn_acc = jnp.einsum("hqk,khd->qhd", probs_low, v_low, preferred_element_type=f32)
    attn_low = attn_acc.reshape(stream_len, own_width).astype(bf16)
    mixed_heads = jnp.dot(attn_low, out_own, preferred_element_type=f32).astype(bf16)
    h_one = x_rows + scatter_ctx(
        [mixed_heads[q * tok_rows : (q + 1) * tok_rows] for q in range(n_ctx)]
    )
    a2_f32, norm_two_back = jax.vjp(rms_scale, h_one, norm_two)
    a2_low = a2_f32.astype(bf16)
    a2_all = jnp.concatenate(gather_fsdp(xor_blocks(a2_low, c, n_ctx)), axis=0)

    tokens = n_fsdp * tok_rows
    routed = lax.all_gather(
        jnp.concatenate([routes[0].astype(f32), gate_weights[0]], axis=1).T, "fsdp", axis=0
    )
    routed = xor_blocks(
        routed.transpose(1, 0, 2).reshape(2 * top_count, tokens), f, n_fsdp
    )
    own = (f * local_experts + jnp.arange(local_experts, dtype=jnp.int32)).astype(f32)
    chosen = routed[None, :top_count] == own[:, None, None]
    member = jnp.any(chosen, axis=1)
    weight = jnp.sum(jnp.where(chosen, routed[None, top_count:], 0.0), axis=1)
    token_ids = jnp.arange(tokens, dtype=jnp.int32)
    before = (token_ids[:, None] < token_ids[None, :]).astype(bf16)
    rank = jnp.dot(member.astype(bf16), before, preferred_element_type=f32).astype(jnp.int32)
    place = jnp.where(member, rank, -1)
    picks = place[:, None, :] == jnp.arange(slots, dtype=jnp.int32)[None, :, None]
    slot_weight = jnp.sum(jnp.where(picks, weight[:, None, :], 0.0), axis=2)
    picks = picks.astype(bf16)

    made, made_grads, gate_up_grads, down_grads = [], [], [], []
    for e in range(local_experts):
        rows = jnp.dot(picks[e], a2_all, preferred_element_type=f32).astype(bf16)
        scale = slot_weight[e][:, None]
        dy = (scale * jnp.dot(picks[e], cot_all, preferred_element_type=f32)).astype(bf16)
        gate_w = gate_up_all[e]
        gate_add = jnp.dot(rows, gate_w[:, :hidden_units], preferred_element_type=f32)
        up_add = jnp.dot(rows, gate_w[:, hidden_units:], preferred_element_type=f32)
        hidden_grad = jnp.dot(dy, down_all[e], preferred_element_type=f32)
        sigmoid_g = jax.nn.sigmoid(gate_add)
        activated = gate_add * sigmoid_g
        hidden_low = (activated * up_add).astype(bf16)
        gate_grad = (hidden_grad * up_add * sigmoid_g * (1.0 + gate_add * (1.0 - sigmoid_g))).astype(
            bf16
        )
        up_grad = (hidden_grad * activated).astype(bf16)
        pair_grad = jnp.concatenate([gate_grad, up_grad], axis=1)
        y_rows = jnp.einsum("rf,df->rd", hidden_low, down_all[e], preferred_element_type=f32)
        made.append((scale * y_rows.astype(bf16).astype(f32)).astype(bf16))
        made_grads.append(
            jnp.einsum("rk,dk->rd", pair_grad, gate_w, preferred_element_type=f32).astype(bf16)
        )
        pair_part = jnp.einsum("rd,rk->dk", rows, pair_grad, preferred_element_type=f32)
        down_part = jnp.einsum("rd,rf->df", dy, hidden_low, preferred_element_type=f32)
        blocks = [slice(p * own_width, (p + 1) * own_width) for p in range(n_ctx)]
        gate_up_grads.append(scatter_ctx([pair_part[b].astype(bf16) for b in blocks]))
        down_grads.append(scatter_ctx([down_part[b].astype(bf16) for b in blocks]))

    grads_back = jnp.einsum("est,esd->td", picks, jnp.stack(made_grads), preferred_element_type=f32)
    grads_back = grads_back.astype(bf16).reshape(n_fsdp, tok_rows, model_width)
    da2 = xor_blocks(scatter_fsdp([grads_back[q] for q in range(n_fsdp)]), c, n_ctx)
    mixed = jnp.einsum("est,esd->td", picks, jnp.stack(made), preferred_element_type=f32)
    mixed = mixed.astype(bf16).reshape(n_fsdp, tok_rows, model_width)
    mixed = xor_blocks(scatter_fsdp([mixed[q] for q in range(n_fsdp)]), c, n_ctx)
    block_out = (h_one + mixed).astype(bf16)

    dh_part, gain_two_grad = norm_two_back(da2)
    dh_one = cot_rows + dh_part
    dattn = jnp.concatenate(gather_ctx(dh_one.astype(bf16)), axis=0)
    d_out = jnp.einsum("tk,dk->td", dattn, out_own, preferred_element_type=f32)
    d_out = d_out.astype(bf16).reshape(stream_len, own_heads, head_dim)
    prob_grad = jnp.einsum("qhd,khd->hqk", d_out, v_low, preferred_element_type=f32)
    row_delta = jnp.sum(probs * prob_grad, axis=2, keepdims=True)
    logit_grad = (probs * (prob_grad - row_delta)).astype(bf16)
    dq = jnp.einsum("hqk,khd->qhd", logit_grad, k_low, preferred_element_type=f32) * score_scale
    dk = jnp.einsum("hqk,qhd->khd", logit_grad, q_low, preferred_element_type=f32) * score_scale
    dv = jnp.einsum("hqk,qhd->khd", probs_low, d_out, preferred_element_type=f32)
    dq_proj, dk_proj, q_gain_grad, k_gain_grad = prepare_back(
        (dq.astype(bf16).astype(f32), dk.astype(bf16).astype(f32))
    )
    proj_grad = jnp.stack([dq_proj, dk_proj, dv.reshape(stream_len, own_width)], axis=1).astype(bf16)
    da1 = jnp.einsum("tjk,djk->td", proj_grad, qkv_all, preferred_element_type=f32).astype(bf16)
    da1 = scatter_ctx([da1[q * tok_rows : (q + 1) * tok_rows] for q in range(n_ctx)])
    da1 = xor_blocks(da1, f, n_fsdp)
    _, norm_one_back = jax.vjp(rms_scale, x_rows, norm_one)
    dx_part, gain_one_grad = norm_one_back(da1)
    inputs_grad = dh_one + dx_part

    qkv_part = jnp.einsum("td,tjk->djk", a1, proj_grad, preferred_element_type=f32).astype(bf16)
    row_count = qkv_w.shape[0]
    qkv_sum = scatter_fsdp([qkv_part[q * row_count : (q + 1) * row_count] for q in range(n_fsdp)])
    out_part = jnp.einsum("td,tk->dk", attn_low, dattn, preferred_element_type=f32).astype(bf16)
    out_sum = scatter_fsdp(
        [
            lax.dynamic_slice_in_dim(out_part, (f ^ q) * out_piece_rows, out_piece_rows, axis=0)
            for q in range(n_fsdp)
        ]
    )
    qkv_grad = jnp.zeros((row_count, 3, model_width), f32)
    for q, piece in enumerate(gather_ctx(qkv_sum.astype(bf16))):
        qkv_grad = lax.dynamic_update_slice_in_dim(
            qkv_grad, piece.astype(f32), (c ^ q) * own_width, axis=2
        )
    out_sum = lax.ppermute(out_sum.astype(bf16), ("ctx", "fsdp"), [(b, a) for a, b in to_heads])
    out_grad = jnp.zeros((row_count, model_width), f32)
    for q, piece in enumerate(gather_ctx(out_sum)):
        out_grad = lax.dynamic_update_slice_in_dim(
            out_grad, piece.astype(f32), (c ^ q) * out_piece_rows, axis=0
        )

    gain_sums = lax.psum(
        jnp.concatenate(
            [
                jnp.stack([gain_one_grad, gain_two_grad]),
                jnp.stack([q_gain_grad, k_gain_grad]),
            ],
            axis=1,
        ),
        ("ctx", "fsdp"),
    )
    norm_rows = norm_gains.shape[0]
    norm_grad = lax.dynamic_slice_in_dim(gain_sums, f * norm_rows, norm_rows, axis=1).T
    head_rows = head_gains.shape[0]
    head_grad = lax.dynamic_slice_in_dim(
        gain_sums, model_width + f * head_rows, head_rows, axis=1
    ).T
    return (
        block_out[None],
        inputs_grad[None],
        qkv_grad,
        out_grad,
        norm_grad,
        head_grad,
        jnp.stack(gate_up_grads, axis=1),
        jnp.stack(down_grads, axis=1),
    )


def solution(mesh):
    return jax.shard_map(
        body,
        mesh=mesh,
        in_specs=(
            P("fsdp", "ctx", None),
            P("fsdp", None),
            P("fsdp", "ctx", None),
            P("fsdp", "ctx", None),
            P("fsdp", None, None),
            P("fsdp", None),
            P("fsdp", None),
            P("fsdp", None),
            P("ctx", "fsdp", None),
            P("ctx", "fsdp", None),
            P("fsdp", "ctx", None),
        ),
        out_specs=(
            P("fsdp", "ctx", None),
            P("fsdp", "ctx", None),
            P("fsdp", None, None),
            P("fsdp", None),
            P("fsdp", None),
            P("fsdp", None),
            P("ctx", "fsdp", None),
            P("ctx", "fsdp", None),
        ),
        check_vma=False,
    )
```

time: 2610 us -> 1230 us (0.47)
  waiting for transfers between devices: 1990 us -> 493 us
  starting transfers between devices: 20.7 us -> 167 us
  local copies, waits for them, and re-layouts: 213 us -> 128 us
  blocking collectives: 75.5 us -> 124 us
  other arithmetic: 102 us -> 137 us
    reduce_scatter x3 -> x0, waiting for transfers between devices: 739 us -> none  [the longest x1 464 us: body(): lax.psum_scatter(jnp.concatenate([projections, output_part[:, None, :]],...]
    all_gather x6 -> x0, waiting for transfers between devices: 732 us -> none  [the longest x1 432 us: body(): lax.all_gather(qkv_w, 'fsdp', axis=0, tiled=True)]
    ppermute x0 -> x112, waiting for transfers between devices: none -> 493 us  [the longest x110 493 us: swap(): return lax.ppermute(value, axis, [(i, i ^ mask) for i in range(size)])]
    all_to_all x4 -> x0, waiting for transfers between devices: 319 us -> none  [the longest x1 135 us: body(): lax.all_to_all(input_grads, 'fsdp', split_axis=1, concat_axis=0, tiled=True)]
    ppermute x0 -> x112, starting transfers between devices: none -> 167 us  [the longest x110 163 us: swap(): return lax.ppermute(value, axis, [(i, i ^ mask) for i in range(size)])]
    unnamed x16 -> x0, waiting for transfers between devices: 145 us -> none
    psum x1 -> x0, waiting for transfers between devices: 53.8 us -> none  [body(): lax.psum(attn_shard, 'ctx').astype(jnp.float32)]
    all_to_all x6 -> x0, local copies, waits for them, and re-layouts: 43.5 us -> none  [the longest x2 12.5 us: body(): lax.all_to_all(send_grads.reshape(experts_all, capacity, model_width), 'f...]
  transfers between devices with their start and end apart: 17 -> 112, of which waited for: 14 -> 36; matrix products, arithmetic and copies ran while one was open for 12% -> 31% of each run, Pallas kernels for 0% -> 0%
where the time goes in v1:
time: 1230 us
  waiting for transfers between devices  493 us (40%)
  matrix products  174 us (14%)
  starting transfers between devices  167 us (14%)
  other arithmetic  137 us (11%)
  local copies, waits for them, and re-layouts  128 us (10%)
  blocking collectives  124 us (10%)
    ppermute x110, waiting for transfers between devices, swap(): return lax.ppermute(value, axis, [(i, i ^ mask) for i in range(size)])  493 us
    ppermute x110, starting transfers between devices, swap(): return lax.ppermute(value, axis, [(i, i ^ mask) for i in range(size)])  163 us
    psum x1, blocking collectives, body(): lax.psum(jnp.concatenate([jnp.stack([gain_one_grad, gain_two_grad]), jnp....  48.7 us
    all_gather x1, blocking collectives, body(): lax.all_gather(jnp.concatenate([norm_gains, head_gains], axis=0).T, 'fsdp...  45.2 us
    all_gather x1, blocking collectives, body(): lax.all_gather(jnp.concatenate([routes[0].astype(f32), gate_weights[0]],...  30.5 us
    concatenate x27, local copies, waits for them, and re-layouts, xor_blocks(): flipped = jnp.concatenate([parts[..., 1:, :], parts[..., :1, :]], axis=-2)  26.6 us
    unnamed x334, local copies, waits for them, and re-layouts  26.2 us
    dot_general x3, matrix products, body(): jnp.einsum('rk,dk->rd', pair_grad, gate_w, preferred_element_type=f32)  26 us
  transfers between devices with their start and end apart: 112, of which 36 were waited for; matrix products, arithmetic and copies ran while one was open for 31% of the time, Pallas kernels for 0%

profile of v1, /device:TPU:0, one launch (start us, length us, event | category | flops | bytes accessed | tf_op | source)
XLA Modules:
  0.0 1227.8 jit_solution(3604934983640964124)
XLA Ops:
  27.7 45.2 %all-gather.2 = bf16[8,2,272]{2,1,0:T(2,128)(2,1)S(1)} all-gather(bf16[1,2,272]{2,1,0:T(2,128)(2,1)S(1)} %maximum_bitcast_fusion.2), channel_id=2, replica_groups=mesh['ctx'=4,'fsdp'=8] {'fsdp'}, dimensions={0}, use_global_device_ids=true | all-gather | bytes 9792 | tf_op jit(solution)/shard_map/all_gather | solution.py:140
  74.7 30.5 %all-gather.1 = f32[128,128]{1,0:T(8,128)S(1)} all-gather(f32[16,128]{1,0:T(8,128)S(1)} %maximum_bitcast_fusion.1), channel_id=3, replica_groups=mesh['ctx'=4,'fsdp'=8] {'fsdp'}, dimensions={0}, use_global_device_ids=true | all-gather | bytes 73728 | tf_op jit(solution)/shard_map/all_gather | solution.py:194
  172.8 13.0 %collective-permute-start.6 = (bf16[256,3,512]{0,2,1:T(8,128)(2,1)S(1)}, bf16[256,3,512]{0,2,1:T(8,128)(2,1)S(1)}, u32[]{:S(2)}, u32[]{:S(2)}) collective-permute-start(bf16[256,3,512]{0,2,1:T(8,128)(2,1)S(1)} %copy.328), channel_id=1, source_target_pairs={{0,4},{1,5},{2,6},{3,7},{4,0},{5,1},{6,2},{7,3},{8,12},{9,13},{10,... | collective-permute-start | bytes 2359304 | tf_op jit(solution)/shard_map/ppermute | solution.py:30
  188.0 30.5 %collective-permute-done.56 = bf16[128,2048]{1,0:T(8,128)(2,1)S(1)} collective-permute-done((bf16[128,2048]{1,0:T(8,128)(2,1)}, bf16[128,2048]{1,0:T(8,128)(2,1)S(1)}, u32[]{:S(2)}, u32[]{:S(2)}) %collective-permute-start.56) | collective-permute-done | bytes 524320 | tf_op jit(solution)/shard_map/ppermute | solution.py:30
  239.8 15.1 %collective-permute-done.6 = bf16[256,3,512]{0,2,1:T(8,128)(2,1)S(1)} collective-permute-done((bf16[256,3,512]{0,2,1:T(8,128)(2,1)S(1)}, bf16[256,3,512]{0,2,1:T(8,128)(2,1)S(1)}, u32[]{:S(2)}, u32[]{:S(2)}) %collective-permute-start.6) | collective-permute-done | bytes 786464 | tf_op jit(solution)/shard_map/ppermute | solution.py:30
  263.2 12.8 %collective-permute-done.7 = bf16[256,3,512]{0,2,1:T(8,128)(2,1)S(1)} collective-permute-done((bf16[256,3,512]{0,2,1:T(8,128)(2,1)S(1)}, bf16[256,3,512]{0,2,1:T(8,128)(2,1)S(1)}, u32[]{:S(2)}, u32[]{:S(2)}) %collective-permute-start.7) | collective-permute-done | bytes 786464 | tf_op jit(solution)/shard_map/ppermute | solution.py:30
  276.3 16.2 %collective-permute-done.9 = bf16[256,3,512]{0,2,1:T(8,128)(2,1)S(1)} collective-permute-done((bf16[256,3,512]{0,2,1:T(8,128)(2,1)S(1)}, bf16[256,3,512]{0,2,1:T(8,128)(2,1)S(1)}, u32[]{:S(2)}, u32[]{:S(2)}) %collective-permute-start.9) | collective-permute-done | bytes 786464 | tf_op jit(solution)/shard_map/ppermute | solution.py:30
  335.2 46.8 %collective-permute-done.20 = bf16[128,2048]{1,0:T(8,128)(2,1)S(1)} collective-permute-done((bf16[128,2048]{1,0:T(8,128)(2,1)S(1)}, bf16[128,2048]{1,0:T(8,128)(2,1)S(1)}, u32[]{:S(2)}, u32[]{:S(2)}) %collective-permute-start.20) | collective-permute-done | bytes 524320 | tf_op jit(solution)/shard_map/ppermute | solution.py:30
  385.0 16.8 %collective-permute-start.22 = (bf16[128,2048]{1,0:T(8,128)(2,1)S(1)}, bf16[128,2048]{1,0:T(8,128)(2,1)S(1)}, u32[]{:S(2)}, u32[]{:S(2)}) collective-permute-start(bf16[128,2048]{1,0:T(8,128)(2,1)S(1)} %get-tuple-element.31), channel_id=1, source_target_pairs={{0,2},{1,3},{2,0},{3,1},{4,6},{5,7},{6,4},{7,5},{8,10},{9,11},{10,... | collective-permute-start | bytes 1572872 | tf_op jit(solution)/shard_map/ppermute | solution.py:30
  410.3 13.5 %collective-permute-done.22 = bf16[128,2048]{1,0:T(8,128)(2,1)S(1)} collective-permute-done((bf16[128,2048]{1,0:T(8,128)(2,1)S(1)}, bf16[128,2048]{1,0:T(8,128)(2,1)S(1)}, u32[]{:S(2)}, u32[]{:S(2)}) %collective-permute-start.22) | collective-permute-done | bytes 524320 | tf_op jit(solution)/shard_map/ppermute | solution.py:30
  425.4 14.7 %collective-permute-done.24 = bf16[128,2048]{1,0:T(8,128)(2,1)S(1)} collective-permute-done((bf16[128,2048]{1,0:T(8,128)(2,1)S(1)}, bf16[128,2048]{1,0:T(8,128)(2,1)S(1)}, u32[]{:S(2)}, u32[]{:S(2)}) %collective-permute-start.24) | collective-permute-done | bytes 524320 | tf_op jit(solution)/shard_map/ppermute | solution.py:30
  444.5 9.0 collective-permute-done.25
  468.0 22.7 %collective-permute-done.35 = bf16[512,2048]{1,0:T(8,128)(2,1)} collective-permute-done((bf16[512,2048]{1,0:T(8,128)(2,1)S(1)}, bf16[512,2048]{1,0:T(8,128)(2,1)}, u32[]{:S(2)}, u32[]{:S(2)}) %collective-permute-start.35) | collective-permute-done | bytes 2097184 | tf_op jit(solution)/shard_map/ppermute | solution.py:30
  490.7 38.2 %collective-permute-done.29 = bf16[512,2048]{1,0:T(8,128)(2,1)} collective-permute-done((bf16[512,2048]{1,0:T(8,128)(2,1)S(1)}, bf16[512,2048]{1,0:T(8,128)(2,1)}, u32[]{:S(2)}, u32[]{:S(2)}) %collective-permute-start.29) | collective-permute-done | bytes 2097184 | tf_op jit(solution)/shard_map/ppermute | solution.py:30
  567.9 10.2 fusion.35
  589.8 8.9 fusion.34
  676.9 9.1 collective-permute-done.51
  686.0 12.8 %collective-permute-start.64 = (bf16[128,2048]{1,0:T(8,128)(2,1)S(1)}, bf16[128,2048]{1,0:T(8,128)(2,1)S(1)}, u32[]{:S(2)}, u32[]{:S(2)}) collective-permute-start(bf16[128,2048]{1,0:T(8,128)(2,1)S(1)} %get-tuple-element.62), channel_id=1, source_target_pairs={{0,4},{1,5},{2,6},{3,7},{4,0},{5,1},{6,2},{7,3},{8,12},{9,13},{10,... | collective-permute-start | bytes 1572872 | tf_op jit(solution)/shard_map/ppermute | solution.py:30
  698.7 10.9 collective-permute-start.62
  714.6 20.8 %collective-permute-done.64 = bf16[128,2048]{1,0:T(8,128)(2,1)S(1)} collective-permute-done((bf16[128,2048]{1,0:T(8,128)(2,1)S(1)}, bf16[128,2048]{1,0:T(8,128)(2,1)S(1)}, u32[]{:S(2)}, u32[]{:S(2)}) %collective-permute-start.64) | collective-permute-done | bytes 524320 | tf_op jit(solution)/shard_map/ppermute | solution.py:30
  855.1 10.2 collective-permute-done.111
  867.5 20.2 %collective-permute-done.108 = bf16[512,1024]{1,0:T(8,128)(2,1)S(1)} collective-permute-done((bf16[512,1024]{1,0:T(8,128)(2,1)S(1)}, bf16[512,1024]{1,0:T(8,128)(2,1)S(1)}, u32[]{:S(2)}, u32[]{:S(2)}) %collective-permute-start.108) | collective-permute-done | bytes 1048608 | tf_op jit(solution)/shard_map/ppermute | solution.py:30
  892.0 16.9 %collective-permute-done.105 = bf16[512,1024]{1,0:T(8,128)(2,1)S(1)} collective-permute-done((bf16[512,1024]{1,0:T(8,128)(2,1)S(1)}, bf16[512,1024]{1,0:T(8,128)(2,1)S(1)}, u32[]{:S(2)}, u32[]{:S(2)}) %collective-permute-start.105) | collective-permute-done | bytes 1048608 | tf_op jit(solution)/shard_map/ppermute | solution.py:30
  924.3 11.1 collective-permute-done.87
  944.5 14.4 %collective-permute-done.78 = bf16[256,3,512]{2,0,1:T(8,128)(2,1)S(1)} collective-permute-done((bf16[256,3,512]{2,0,1:T(8,128)(2,1)S(1)}, bf16[256,3,512]{2,0,1:T(8,128)(2,1)S(1)}, u32[]{:S(2)}, u32[]{:S(2)}) %collective-permute-start.78) | collective-permute-done | bytes 786464 | tf_op jit(solution)/shard_map/ppermute | solution.py:30
  958.9 16.8 %collective-permute-done.76 = bf16[256,3,512]{2,0,1:T(8,128)(2,1)S(1)} collective-permute-done((bf16[256,3,512]{2,0,1:T(8,128)(2,1)S(1)}, bf16[256,3,512]{2,0,1:T(8,128)(2,1)S(1)}, u32[]{:S(2)}, u32[]{:S(2)}) %collective-permute-start.76) | collective-permute-done | bytes 786464 | tf_op jit(solution)/shard_map/ppermute | solution.py:30
  978.5 19.5 %collective-permute-start.102 = (bf16[512,2048]{1,0:T(8,128)(2,1)}, bf16[512,2048]{1,0:T(8,128)(2,1)}, u32[]{:S(2)}, u32[]{:S(2)}) collective-permute-start(bf16[512,2048]{1,0:T(8,128)(2,1)} %add_convert_fusion), channel_id=1, source_target_pairs={{0,16},{8,24},{16,0},{24,8},{1,17},{9,25},{17,1},{25,9},{2,18},{10... | collective-permute-start | bytes 6291464 | tf_op jit(solution)/shard_map/ppermute | solution.py:30
  1049.8 48.7 %psum.7 = f32[2,2176]{1,0:T(2,128)S(1)} all-reduce(f32[2,2176]{1,0:T(2,128)S(1)} %maximum_maximum_fusion), channel_id=1, replica_groups=mesh['ctx'=4,'fsdp'=8] {'ctx','fsdp'}, use_global_device_ids=true, to_apply=%region_21.22 | all-reduce | flops 4352 | bytes 34816 | tf_op jit(solution)/shard_map/psum | solution.py:292
  1115.9 32.3 %collective-permute-done.99 = bf16[512,2048]{1,0:T(8,128)(2,1)S(1)} collective-permute-done((bf16[512,2048]{1,0:T(8,128)(2,1)}, bf16[512,2048]{1,0:T(8,128)(2,1)S(1)}, u32[]{:S(2)}, u32[]{:S(2)}) %collective-permute-start.99) | collective-permute-done | bytes 2097184 | tf_op jit(solution)/shard_map/ppermute | solution.py:30
  1152.9 40.2 %collective-permute-done.96 = bf16[512,2048]{1,0:T(8,128)(2,1)S(1)} collective-permute-done((bf16[512,2048]{1,0:T(8,128)(2,1)}, bf16[512,2048]{1,0:T(8,128)(2,1)S(1)}, u32[]{:S(2)}, u32[]{:S(2)}) %collective-permute-start.96) | collective-permute-done | bytes 2097184 | tf_op jit(solution)/shard_map/ppermute | solution.py:30
  1197.8 12.0 collective-permute-done.81
  1209.8 10.1 pad_maximum_fusion
  (797 shorter events, 573.6 us)
Async XLA Ops:
  13.9 134.4 %collective-permute-start.53 = (bf16[128,2048]{1,0:T(8,128)(2,1)}, bf16[128,2048]{1,0:T(8,128)(2,1)}, u32[]{:S(2)}, u32[]{:S(2)}) collective-permute-start(bf16[128,2048]{1,0:T(8,128)(2,1)} %get-tuple-element.29), channel_id=1, source_target_pairs={{0,1},{1,0},{2,3},{3,2},{4,5},{5,4},{6,7},{7,6},{8,9},{9,8},{10,11... | collective-permute-start | bytes 1572872 | tf_op jit(solution)/shard_map/ppermute | solution.py:30
  16.9 136.4 %collective-permute-start.54 = (bf16[128,2048]{1,0:T(8,128)(2,1)}, bf16[128,2048]{1,0:T(8,128)(2,1)}, u32[]{:S(2)}, u32[]{:S(2)}) collective-permute-start(bf16[128,2048]{1,0:T(8,128)(2,1)} %get-tuple-element.29), channel_id=1, source_target_pairs={{0,2},{1,3},{2,0},{3,1},{4,6},{5,7},{6,4},{7,5},{8,10},{9,11},{10,... | collective-permute-start | bytes 1572872 | tf_op jit(solution)/shard_map/ppermute | solution.py:30
  20.9 152.0 %collective-permute-start.3 = (bf16[256,3,512]{0,2,1:T(8,128)(2,1)S(1)}, bf16[256,3,512]{0,2,1:T(8,128)(2,1)}, u32[]{:S(2)}, u32[]{:S(2)}) collective-permute-start(bf16[256,3,512]{0,2,1:T(8,128)(2,1)S(1)} %copy.328), channel_id=1, source_target_pairs={{0,1},{1,0},{2,3},{3,2},{4,5},{5,4},{6,7},{7,6},{8,9},{9,8},{10,11... | collective-permute-start | bytes 2359304 | tf_op jit(solution)/shard_map/ppermute | solution.py:30
  23.1 108.6 %collective-permute-start.10 = (bf16[64,2048]{1,0:T(8,128)(2,1)}, bf16[64,2048]{1,0:T(8,128)(2,1)}, u32[]{:S(2)}, u32[]{:S(2)}) collective-permute-start(bf16[64,2048]{1,0:T(8,128)(2,1)} %constant_dynamic-slice_fusion.6), channel_id=1, source_target_pairs={{0,0},{8,1},{16,2},{24,3},{1,4},{9,5},{17,6},{25,7},{2,8},{10,9},{... | collective-permute-start | bytes 786440 | tf_op jit(solution)/shard_map/ppermute | solution.py:130
  153.3 67.1 %collective-permute-start.4 = (bf16[256,3,512]{0,2,1:T(8,128)(2,1)S(1)}, bf16[256,3,512]{0,2,1:T(8,128)(2,1)S(1)}, u32[]{:S(2)}, u32[]{:S(2)}) collective-permute-start(bf16[256,3,512]{0,2,1:T(8,128)(2,1)S(1)} %copy.328), channel_id=1, source_target_pairs={{0,2},{1,3},{2,0},{3,1},{4,6},{5,7},{6,4},{7,5},{8,10},{9,11},{10,... | collective-permute-start | bytes 2359304 | tf_op jit(solution)/shard_map/ppermute | solution.py:30
  172.8 82.1 %collective-permute-start.6 = (bf16[256,3,512]{0,2,1:T(8,128)(2,1)S(1)}, bf16[256,3,512]{0,2,1:T(8,128)(2,1)S(1)}, u32[]{:S(2)}, u32[]{:S(2)}) collective-permute-start(bf16[256,3,512]{0,2,1:T(8,128)(2,1)S(1)} %copy.328), channel_id=1, source_target_pairs={{0,4},{1,5},{2,6},{3,7},{4,0},{5,1},{6,2},{7,3},{8,12},{9,13},{10,... | collective-permute-start | bytes 2359304 | tf_op jit(solution)/shard_map/ppermute | solution.py:30
  258.9 63.5 %collective-permute-start.43 = (bf16[512,1024]{1,0:T(8,128)(2,1)}, bf16[512,1024]{1,0:T(8,128)(2,1)}, u32[]{:S(2)}, u32[]{:S(2)}) collective-permute-start(bf16[512,1024]{1,0:T(8,128)(2,1)} %get-tuple-element.80), channel_id=1, source_target_pairs={{0,8},{8,0},{16,24},{24,16},{1,9},{9,1},{17,25},{25,17},{2,10},{10... | collective-permute-start | bytes 3145736 | tf_op jit(solution)/shard_map/ppermute | solution.py:30
  260.8 60.9 %collective-permute-start.38 = (bf16[512,1024]{1,0:T(8,128)(2,1)}, bf16[512,1024]{1,0:T(8,128)(2,1)}, u32[]{:S(2)}, u32[]{:S(2)}) collective-permute-start(bf16[512,1024]{1,0:T(8,128)(2,1)} %get-tuple-element.81), channel_id=1, source_target_pairs={{0,16},{8,24},{16,0},{24,8},{1,17},{9,25},{17,1},{25,9},{2,18},{10... | collective-permute-start | bytes 3145736 | tf_op jit(solution)/shard_map/ppermute | solution.py:30
  261.6 60.9 %collective-permute-start.32 = (bf16[512,1024]{1,0:T(8,128)(2,1)}, bf16[512,1024]{1,0:T(8,128)(2,1)}, u32[]{:S(2)}, u32[]{:S(2)}) collective-permute-start(bf16[512,1024]{1,0:T(8,128)(2,1)} %get-tuple-element.79), channel_id=1, source_target_pairs={{0,16},{8,24},{16,0},{24,8},{1,17},{9,25},{17,1},{25,9},{2,18},{10... | collective-permute-start | bytes 3145736 | tf_op jit(solution)/shard_map/ppermute | solution.py:30
  322.4 79.4 %collective-permute-start.31 = (bf16[512,1024]{1,0:T(8,128)(2,1)}, bf16[512,1024]{1,0:T(8,128)(2,1)}, u32[]{:S(2)}, u32[]{:S(2)}) collective-permute-start(bf16[512,1024]{1,0:T(8,128)(2,1)} %get-tuple-element.79), channel_id=1, source_target_pairs={{0,8},{8,0},{16,24},{24,16},{1,9},{9,1},{17,25},{25,17},{2,10},{10... | collective-permute-start | bytes 3145736 | tf_op jit(solution)/shard_map/ppermute | solution.py:30
  322.5 121.6 %collective-permute-start.41 = (bf16[512,2048]{1,0:T(8,128)(2,1)}, bf16[512,2048]{1,0:T(8,128)(2,1)}, u32[]{:S(2)}, u32[]{:S(2)}) collective-permute-start(bf16[512,2048]{1,0:T(8,128)(2,1)} %get-tuple-element.48), channel_id=1, source_target_pairs={{0,16},{8,24},{16,0},{24,8},{1,17},{9,25},{17,1},{25,9},{2,18},{10... | collective-permute-start | bytes 6291464 | tf_op jit(solution)/shard_map/ppermute | solution.py:30
  322.6 79.9 %collective-permute-start.33 = (bf16[512,1024]{1,0:T(8,128)(2,1)}, bf16[512,1024]{1,0:T(8,128)(2,1)}, u32[]{:S(2)}, u32[]{:S(2)}) collective-permute-start(bf16[512,1024]{1,0:T(8,128)(2,1)} %collective-permute-done.32), channel_id=1, source_target_pairs={{0,8},{8,0},{16,24},{24,16},{1,9},{9,1},{17,25},{25,17},{2,10},{10... | collective-permute-start | bytes 3145736 | tf_op jit(solution)/shard_map/ppermute | solution.py:30
  444.2 84.8 %collective-permute-start.29 = (bf16[512,2048]{1,0:T(8,128)(2,1)S(1)}, bf16[512,2048]{1,0:T(8,128)(2,1)}, u32[]{:S(2)}, u32[]{:S(2)}) collective-permute-start(bf16[512,2048]{1,0:T(8,128)(2,1)S(1)} %copy-done.21), channel_id=1, source_target_pairs={{0,16},{8,24},{16,0},{24,8},{1,17},{9,25},{17,1},{25,9},{2,18},{10... | collective-permute-start | bytes 6291464 | tf_op jit(solution)/shard_map/ppermute | solution.py:30
  453.5 75.5 %collective-permute-start.42 = (bf16[512,2048]{1,0:T(8,128)(2,1)}, bf16[512,2048]{1,0:T(8,128)(2,1)S(1)}, u32[]{:S(2)}, u32[]{:S(2)}) collective-permute-start(bf16[512,2048]{1,0:T(8,128)(2,1)} %collective-permute-done.41), channel_id=1, source_target_pairs={{0,8},{8,0},{16,24},{24,16},{1,9},{9,1},{17,25},{25,17},{2,10},{10... | collective-permute-start | bytes 6291464 | tf_op jit(solution)/shard_map/ppermute | solution.py:30
  459.1 92.5 %collective-permute-start.34 = (bf16[512,2048]{1,0:T(8,128)(2,1)S(1)}, bf16[512,2048]{1,0:T(8,128)(2,1)}, u32[]{:S(2)}, u32[]{:S(2)}) collective-permute-start(bf16[512,2048]{1,0:T(8,128)(2,1)S(1)} %copy-done.22), channel_id=1, source_target_pairs={{0,8},{8,0},{16,24},{24,16},{1,9},{9,1},{17,25},{25,17},{2,10},{10... | collective-permute-start | bytes 6291464 | tf_op jit(solution)/shard_map/ppermute | solution.py:30
  467.5 110.6 %collective-permute-start.28 = (bf16[512,2048]{1,0:T(8,128)(2,1)S(1)}, bf16[512,2048]{1,0:T(8,128)(2,1)}, u32[]{:S(2)}, u32[]{:S(2)}) collective-permute-start(bf16[512,2048]{1,0:T(8,128)(2,1)S(1)} %copy-done.21), channel_id=1, source_target_pairs={{0,8},{8,0},{16,24},{24,16},{1,9},{9,1},{17,25},{25,17},{2,10},{10... | collective-permute-start | bytes 6291464 | tf_op jit(solution)/shard_map/ppermute | solution.py:30
  490.7 60.9 %collective-permute-start.36 = (bf16[512,2048]{1,0:T(8,128)(2,1)}, bf16[512,2048]{1,0:T(8,128)(2,1)}, u32[]{:S(2)}, u32[]{:S(2)}) collective-permute-start(bf16[512,2048]{1,0:T(8,128)(2,1)} %collective-permute-done.35), channel_id=1, source_target_pairs={{0,8},{8,0},{16,24},{24,16},{1,9},{9,1},{17,25},{25,17},{2,10},{10... | collective-permute-start | bytes 6291464 | tf_op jit(solution)/shard_map/ppermute | solution.py:30
  617.6 95.1 %collective-permute-start.60 = (bf16[128,2048]{1,0:T(8,128)(2,1)}, bf16[128,2048]{1,0:T(8,128)(2,1)S(1)}, u32[]{:S(2)}, u32[]{:S(2)}) collective-permute-start(bf16[128,2048]{1,0:T(8,128)(2,1)} %get-tuple-element.56), channel_id=1, source_target_pairs={{0,1},{1,0},{2,3},{3,2},{4,5},{5,4},{6,7},{7,6},{8,9},{9,8},{10,11... | collective-permute-start | bytes 1572872 | tf_op jit(solution)/shard_map/ppermute | solution.py:30
  671.0 92.0 %collective-permute-start.46 = (bf16[128,2048]{1,0:T(8,128)(2,1)}, bf16[128,2048]{1,0:T(8,128)(2,1)}, u32[]{:S(2)}, u32[]{:S(2)}) collective-permute-start(bf16[128,2048]{1,0:T(8,128)(2,1)} %get-tuple-element.63), channel_id=1, source_target_pairs={{0,1},{1,0},{2,3},{3,2},{4,5},{5,4},{6,7},{7,6},{8,9},{9,8},{10,11... | collective-permute-start | bytes 1572872 | tf_op jit(solution)/shard_map/ppermute | solution.py:30
  712.7 126.4 %collective-permute-start.101 = (bf16[512,2048]{1,0:T(8,128)(2,1)}, bf16[512,2048]{1,0:T(8,128)(2,1)}, u32[]{:S(2)}, u32[]{:S(2)}) collective-permute-start(bf16[512,2048]{1,0:T(8,128)(2,1)} %get-tuple-element.39), channel_id=1, source_target_pairs={{0,8},{8,0},{16,24},{24,16},{1,9},{9,1},{17,25},{25,17},{2,10},{10... | collective-permute-start | bytes 6291464 | tf_op jit(solution)/shard_map/ppermute | solution.py:30
  797.5 69.9 %collective-permute-start.106 = (bf16[512,1024]{1,0:T(8,128)(2,1)}, bf16[512,1024]{1,0:T(8,128)(2,1)}, u32[]{:S(2)}, u32[]{:S(2)}) collective-permute-start(bf16[512,1024]{1,0:T(8,128)(2,1)} %get-tuple-element.52), channel_id=1, source_target_pairs={{0,8},{8,0},{16,24},{24,16},{1,9},{9,1},{17,25},{25,17},{2,10},{10... | collective-permute-start | bytes 3145736 | tf_op jit(solution)/shard_map/ppermute | solution.py:30
  865.3 72.3 %collective-permute-start.71 = (bf16[128,2048]{1,0:T(8,128)(2,1)S(1)}, bf16[128,2048]{1,0:T(8,128)(2,1)S(1)}, u32[]{:S(2)}, u32[]{:S(2)}) collective-permute-start(bf16[128,2048]{1,0:T(8,128)(2,1)S(1)} %get-tuple-element.92), channel_id=1, source_target_pairs={{0,8},{8,0},{16,24},{24,16},{1,9},{9,1},{17,25},{25,17},{2,10},{10... | collective-permute-start | bytes 1572872 | tf_op jit(solution)/shard_map/ppermute | solution.py:30
  918.8 116.5 %collective-permute-start.100 = (bf16[512,2048]{1,0:T(8,128)(2,1)}, bf16[512,2048]{1,0:T(8,128)(2,1)}, u32[]{:S(2)}, u32[]{:S(2)}) collective-permute-start(bf16[512,2048]{1,0:T(8,128)(2,1)} %get-tuple-element.38), channel_id=1, source_target_pairs={{0,8},{8,0},{16,24},{24,16},{1,9},{9,1},{17,25},{25,17},{2,10},{10... | collective-permute-start | bytes 6291464 | tf_op jit(solution)/shard_map/ppermute | solution.py:30
  937.6 62.7 %collective-permute-start.70 = (bf16[128,2048]{1,0:T(8,128)(2,1)S(1)}, bf16[128,2048]{1,0:T(8,128)(2,1)S(1)}, u32[]{:S(2)}, u32[]{:S(2)}) collective-permute-start(bf16[128,2048]{1,0:T(8,128)(2,1)S(1)} %get-tuple-element.91), channel_id=1, source_target_pairs={{0,8},{8,0},{16,24},{24,16},{1,9},{9,1},{17,25},{25,17},{2,10},{10... | collective-permute-start | bytes 1572872 | tf_op jit(solution)/shard_map/ppermute | solution.py:30
  942.0 97.9 %collective-permute-start.73 = (bf16[256,3,512]{2,0,1:T(8,128)(2,1)}, bf16[256,3,512]{2,0,1:T(8,128)(2,1)}, u32[]{:S(2)}, u32[]{:S(2)}) collective-permute-start(bf16[256,3,512]{2,0,1:T(8,128)(2,1)} %get-tuple-element.40), channel_id=1, source_target_pairs={{0,1},{1,0},{2,3},{3,2},{4,5},{5,4},{6,7},{7,6},{8,9},{9,8},{10,11... | collective-permute-start | bytes 2359304 | tf_op jit(solution)/shard_map/ppermute | solution.py:30
  978.5 128.7 %collective-permute-start.102 = (bf16[512,2048]{1,0:T(8,128)(2,1)}, bf16[512,2048]{1,0:T(8,128)(2,1)}, u32[]{:S(2)}, u32[]{:S(2)}) collective-permute-start(bf16[512,2048]{1,0:T(8,128)(2,1)} %add_convert_fusion), channel_id=1, source_target_pairs={{0,16},{8,24},{16,0},{24,8},{1,17},{9,25},{17,1},{25,9},{2,18},{10... | collective-permute-start | bytes 6291464 | tf_op jit(solution)/shard_map/ppermute | solution.py:30
  1000.4 98.8 %collective-permute-start.79 = (bf16[256,3,512]{2,0,1:T(8,128)(2,1)}, bf16[256,3,512]{2,0,1:T(8,128)(2,1)}, u32[]{:S(2)}, u32[]{:S(2)}) collective-permute-start(bf16[256,3,512]{2,0,1:T(8,128)(2,1)} %get-tuple-element.45), channel_id=1, source_target_pairs={{0,6},{1,7},{2,4},{3,5},{4,2},{5,3},{6,0},{7,1},{8,14},{9,15},{10,... | collective-permute-start | bytes 2359304 | tf_op jit(solution)/shard_map/ppermute | solution.py:30
  1035.3 67.6 %collective-permute-start.77 = (bf16[256,3,512]{2,0,1:T(8,128)(2,1)}, bf16[256,3,512]{2,0,1:T(8,128)(2,1)S(1)}, u32[]{:S(2)}, u32[]{:S(2)}) collective-permute-start(bf16[256,3,512]{2,0,1:T(8,128)(2,1)} %get-tuple-element.46), channel_id=1, source_target_pairs={{0,4},{1,5},{2,6},{3,7},{4,0},{5,1},{6,2},{7,3},{8,12},{9,13},{10,... | collective-permute-start | bytes 2359304 | tf_op jit(solution)/shard_map/ppermute | solution.py:30
  1040.0 63.1 %collective-permute-start.75 = (bf16[256,3,512]{2,0,1:T(8,128)(2,1)S(1)}, bf16[256,3,512]{2,0,1:T(8,128)(2,1)S(1)}, u32[]{:S(2)}, u32[]{:S(2)}) collective-permute-start(bf16[256,3,512]{2,0,1:T(8,128)(2,1)S(1)} %copy-done.57), channel_id=1, source_target_pairs={{0,2},{1,3},{2,0},{3,1},{4,6},{5,7},{6,4},{7,5},{8,10},{9,11},{10,... | collective-permute-start | bytes 2359304 | tf_op jit(solution)/shard_map/ppermute | solution.py:30
  1103.1 90.0 %collective-permute-start.96 = (bf16[512,2048]{1,0:T(8,128)(2,1)}, bf16[512,2048]{1,0:T(8,128)(2,1)S(1)}, u32[]{:S(2)}, u32[]{:S(2)}) collective-permute-start(bf16[512,2048]{1,0:T(8,128)(2,1)} %add_convert_fusion.2), channel_id=1, source_target_pairs={{0,16},{8,24},{16,0},{24,8},{1,17},{9,25},{17,1},{25,9},{2,18},{10... | collective-permute-start | bytes 6291464 | tf_op jit(solution)/shard_map/ppermute | solution.py:30
  1109.9 110.0 %collective-permute-start.80 = (bf16[256,3,512]{2,0,1:T(8,128)(2,1)S(1)}, bf16[256,3,512]{2,0,1:T(8,128)(2,1)}, u32[]{:S(2)}, u32[]{:S(2)}) collective-permute-start(bf16[256,3,512]{2,0,1:T(8,128)(2,1)S(1)} %get-tuple-element.25), channel_id=1, source_target_pairs={{0,8},{8,0},{16,24},{24,16},{1,9},{9,1},{17,25},{25,17},{2,10},{10... | collective-permute-start | bytes 2359304 | tf_op jit(solution)/shard_map/ppermute | solution.py:30
  1114.0 95.8 %collective-permute-start.81 = (bf16[256,3,512]{2,0,1:T(8,128)(2,1)S(1)}, bf16[256,3,512]{2,0,1:T(8,128)(2,1)}, u32[]{:S(2)}, u32[]{:S(2)}) collective-permute-start(bf16[256,3,512]{2,0,1:T(8,128)(2,1)S(1)} %get-tuple-element.25), channel_id=1, source_target_pairs={{0,16},{8,24},{16,0},{24,8},{1,17},{9,25},{17,1},{25,9},{2,18},{10... | collective-permute-start | bytes 2359304 | tf_op jit(solution)/shard_map/ppermute | solution.py:30
  (234 other events, 5868.3 us)

commit v2 on v1

--- a/solution.py
+++ b/solution.py
@@ -2,7 +2,10 @@
 
 import jax
 import jax.numpy as jnp
+import numpy as np
 from jax import lax
+from jax.experimental import pallas as pl
+from jax.experimental.pallas import tpu as pltpu
 from jax.sharding import PartitionSpec as P
 
 EPS = 1e-06
@@ -76,14 +79,31 @@
     return total
 
 
+def copy_block(index_ref, from_ref, to_ref):
+    to_ref[...] = from_ref[...]
+
+
 def xor_blocks(values, index, count):
-    shape = values.shape
-    width = shape[-1] // count
-    for bit in bits_down(count):
-        parts = values.reshape(shape[:-1] + (count // (2 * bit), 2, bit * width))
-        flipped = jnp.concatenate([parts[..., 1:, :], parts[..., :1, :]], axis=-2)
-        values = jnp.where((index & bit) != 0, flipped, parts).reshape(shape)
-    return values
+    rows, columns = values.shape
+    width = columns // count
+    return pl.pallas_call(
+        copy_block,
+        grid_spec=pltpu.PrefetchScalarGridSpec(
+            num_scalar_prefetch=1,
+            grid=(count,),
+            in_specs=[pl.BlockSpec((rows, width), lambda q, at: (0, jnp.bitwise_xor(q, at[0])))],
+            out_specs=pl.BlockSpec((rows, width), lambda q, at: (0, q)),
+        ),
+        out_shape=jax.ShapeDtypeStruct(values.shape, values.dtype),
+    )(index.astype(jnp.int32).reshape(1), values)
+
+
+def xor_small(values, index, count):
+    rows, columns = values.shape
+    blocks = jnp.arange(count, dtype=jnp.int32)
+    swap_matrix = (blocks[:, None] ^ index == blocks[None, :])[None, :, :, None]
+    parts = values.reshape(rows, 1, count, columns // count)
+    return jnp.sum(jnp.where(swap_matrix, parts, 0.0), axis=2).reshape(rows, columns)
 
 
 def body(
@@ -137,19 +157,30 @@
     for q, piece in enumerate(out_pieces):
         out_own = lax.dynamic_update_slice_in_dim(out_own, piece, (f ^ q) * out_piece_rows, axis=0)
 
-    gains = lax.all_gather(
-        jnp.concatenate([norm_gains, head_gains], axis=0).T, "fsdp", axis=0
-    ).astype(f32)
-    norm_one = gains[:, 0, : norm_gains.shape[0]].reshape(model_width)
-    norm_two = gains[:, 1, : norm_gains.shape[0]].reshape(model_width)
-    head_q = gains[:, 0, norm_gains.shape[0] :].reshape(head_dim)
-    head_k = gains[:, 1, norm_gains.shape[0] :].reshape(head_dim)
-
-    cot_all = jnp.concatenate(gather_fsdp(xor_blocks(cot_low, c, n_ctx)), axis=0)
-    gate_up_all = [
-        jnp.concatenate(gather_ctx(gate_up[:, e, :]), axis=0) for e in range(local_experts)
-    ]
-    down_all = [jnp.concatenate(gather_ctx(down_t[:, e, :]), axis=0) for e in range(local_experts)]
+    norm_rows, head_rows = norm_gains.shape[0], head_gains.shape[0]
+    small = jnp.concatenate(
+        [
+            norm_gains.astype(f32).T.reshape(-1),
+            routes[0].astype(f32).T.reshape(-1),
+            gate_weights[0].T.reshape(-1),
+            head_gains.astype(f32).T.reshape(-1),
+        ]
+    )
+    small_rows = -(-small.shape[0] // 1024) * 8
+    small = jnp.pad(small, (0, small_rows * 128 - small.shape[0])).reshape(small_rows, 128)
+    small = jnp.stack(gather_fsdp(small)).reshape(n_fsdp, small_rows * 128)
+    parts = jnp.split(
+        small, np.cumsum([2 * norm_rows, 2 * tok_rows * top_count, 2 * head_rows]), axis=1
+    )
+    norm_xor = parts[0].reshape(n_fsdp, 2, norm_rows).transpose(1, 0, 2).reshape(2, model_width)
+    routed = parts[1].reshape(n_fsdp, 2 * top_count, tok_rows).transpose(1, 0, 2)
+    head_xor = parts[2].reshape(n_fsdp, 2, head_rows).transpose(1, 0, 2).reshape(2, head_dim)
+    norm_one, norm_two = xor_small(norm_xor, f, n_fsdp)
+    head_q, head_k = xor_small(head_xor, f, n_fsdp)
+
+    cot_all = jnp.concatenate(gather_fsdp(cot_low), axis=0)
+    gate_up_all = lax.all_gather(gate_up.transpose(1, 0, 2), "ctx", axis=1, tiled=True)
+    down_all = lax.all_gather(down_t.transpose(1, 0, 2), "ctx", axis=1, tiled=True)
 
     places = jnp.arange(stream_len, dtype=jnp.int32)
     spots = ((c ^ (places // tok_rows)) * tok_rows + places % tok_rows).astype(jnp.int32)
@@ -164,7 +195,7 @@
     cosine = jnp.cos(angles)[:, None, :]
     sine_part = jnp.sin(angles)[:, None, :]
 
-    a1 = rms_scale(x_all.astype(f32), xor_blocks(norm_one, f, n_fsdp)).astype(bf16)
+    a1 = rms_scale(x_all.astype(f32), norm_xor[0]).astype(bf16)
     proj = jnp.einsum("td,djk->tjk", a1, qkv_all, preferred_element_type=f32)
 
     def prepare(q_flat, k_flat, q_gain, k_gain):
@@ -188,15 +219,10 @@
     )
     a2_f32, norm_two_back = jax.vjp(rms_scale, h_one, norm_two)
     a2_low = a2_f32.astype(bf16)
-    a2_all = jnp.concatenate(gather_fsdp(xor_blocks(a2_low, c, n_ctx)), axis=0)
+    a2_all = jnp.concatenate(gather_fsdp(a2_low), axis=0)
 
     tokens = n_fsdp * tok_rows
-    routed = lax.all_gather(
-        jnp.concatenate([routes[0].astype(f32), gate_weights[0]], axis=1).T, "fsdp", axis=0
-    )
-    routed = xor_blocks(
-        routed.transpose(1, 0, 2).reshape(2 * top_count, tokens), f, n_fsdp
-    )
+    routed = routed.reshape(2 * top_count, tokens)
     own = (f * local_experts + jnp.arange(local_experts, dtype=jnp.int32)).astype(f32)
     chosen = routed[None, :top_count] == own[:, None, None]
     member = jnp.any(chosen, axis=1)
@@ -209,41 +235,32 @@
     slot_weight = jnp.sum(jnp.where(picks, weight[:, None, :], 0.0), axis=2)
     picks = picks.astype(bf16)
 
-    made, made_grads, gate_up_grads, down_grads = [], [], [], []
-    for e in range(local_experts):
-        rows = jnp.dot(picks[e], a2_all, preferred_element_type=f32).astype(bf16)
-        scale = slot_weight[e][:, None]
-        dy = (scale * jnp.dot(picks[e], cot_all, preferred_element_type=f32)).astype(bf16)
-        gate_w = gate_up_all[e]
-        gate_add = jnp.dot(rows, gate_w[:, :hidden_units], preferred_element_type=f32)
-        up_add = jnp.dot(rows, gate_w[:, hidden_units:], preferred_element_type=f32)
-        hidden_grad = jnp.dot(dy, down_all[e], preferred_element_type=f32)
-        sigmoid_g = jax.nn.sigmoid(gate_add)
-        activated = gate_add * sigmoid_g
-        hidden_low = (activated * up_add).astype(bf16)
-        gate_grad = (hidden_grad * up_add * sigmoid_g * (1.0 + gate_add * (1.0 - sigmoid_g))).astype(
-            bf16
-        )
-        up_grad = (hidden_grad * activated).astype(bf16)
-        pair_grad = jnp.concatenate([gate_grad, up_grad], axis=1)
-        y_rows = jnp.einsum("rf,df->rd", hidden_low, down_all[e], preferred_element_type=f32)
-        made.append((scale * y_rows.astype(bf16).astype(f32)).astype(bf16))
-        made_grads.append(
-            jnp.einsum("rk,dk->rd", pair_grad, gate_w, preferred_element_type=f32).astype(bf16)
-        )
-        pair_part = jnp.einsum("rd,rk->dk", rows, pair_grad, preferred_element_type=f32)
-        down_part = jnp.einsum("rd,rf->df", dy, hidden_low, preferred_element_type=f32)
-        blocks = [slice(p * own_width, (p + 1) * own_width) for p in range(n_ctx)]
-        gate_up_grads.append(scatter_ctx([pair_part[b].astype(bf16) for b in blocks]))
-        down_grads.append(scatter_ctx([down_part[b].astype(bf16) for b in blocks]))
-
-    grads_back = jnp.einsum("est,esd->td", picks, jnp.stack(made_grads), preferred_element_type=f32)
+    rows = jnp.einsum("est,td->esd", picks, a2_all, preferred_element_type=f32).astype(bf16)
+    scale = slot_weight[:, :, None]
+    dy = jnp.einsum("est,td->esd", picks, cot_all, preferred_element_type=f32)
+    dy = (scale * dy).astype(bf16)
+    gate_add = jnp.einsum("erd,edk->erk", rows, gate_up_all[:, :, :hidden_units], preferred_element_type=f32)
+    up_add = jnp.einsum("erd,edk->erk", rows, gate_up_all[:, :, hidden_units:], preferred_element_type=f32)
+    hidden_grad = jnp.einsum("erd,edf->erf", dy, down_all, preferred_element_type=f32)
+    sigmoid_g = jax.nn.sigmoid(gate_add)
+    activated = gate_add * sigmoid_g
+    hidden_low = (activated * up_add).astype(bf16)
+    gate_grad = hidden_grad * up_add * sigmoid_g * (1.0 + gate_add * (1.0 - sigmoid_g))
+    pair_grad = jnp.concatenate([gate_grad, hidden_grad * activated], axis=2).astype(bf16)
+    dxe = jnp.einsum("erk,edk->erd", pair_grad, gate_up_all, preferred_element_type=f32).astype(bf16)
+    grads_back = jnp.einsum("est,esd->td", picks, dxe, preferred_element_type=f32)
     grads_back = grads_back.astype(bf16).reshape(n_fsdp, tok_rows, model_width)
-    da2 = xor_blocks(scatter_fsdp([grads_back[q] for q in range(n_fsdp)]), c, n_ctx)
-    mixed = jnp.einsum("est,esd->td", picks, jnp.stack(made), preferred_element_type=f32)
+    da2 = scatter_fsdp([grads_back[q] for q in range(n_fsdp)])
+    made = jnp.einsum("erf,edf->erd", hidden_low, down_all, preferred_element_type=f32)
+    made = (scale * made.astype(bf16).astype(f32)).astype(bf16)
+    mixed = jnp.einsum("est,esd->td", picks, made, preferred_element_type=f32)
     mixed = mixed.astype(bf16).reshape(n_fsdp, tok_rows, model_width)
-    mixed = xor_blocks(scatter_fsdp([mixed[q] for q in range(n_fsdp)]), c, n_ctx)
-    block_out = (h_one + mixed).astype(bf16)
+    block_out = (h_one + scatter_fsdp([mixed[q] for q in range(n_fsdp)])).astype(bf16)
+
+    down_part = jnp.einsum("erd,erf->edf", dy, hidden_low, preferred_element_type=f32).astype(bf16)
+    down_grad = lax.psum_scatter(down_part, "ctx", scatter_dimension=1, tiled=True).astype(f32)
+    pair_part = jnp.einsum("erd,erk->edk", rows, pair_grad, preferred_element_type=f32).astype(bf16)
+    gate_up_grad = lax.psum_scatter(pair_part, "ctx", scatter_dimension=1, tiled=True).astype(f32)
 
     dh_part, gain_two_grad = norm_two_back(da2)
     dh_one = cot_rows + dh_part
@@ -289,19 +306,13 @@
             out_grad, piece.astype(f32), (c ^ q) * out_piece_rows, axis=0
         )
 
-    gain_sums = lax.psum(
-        jnp.concatenate(
-            [
-                jnp.stack([gain_one_grad, gain_two_grad]),
-                jnp.stack([q_gain_grad, k_gain_grad]),
-            ],
-            axis=1,
-        ),
-        ("ctx", "fsdp"),
-    )
-    norm_rows = norm_gains.shape[0]
+    gain_sums = jnp.concatenate(
+        [jnp.stack([gain_one_grad, gain_two_grad]), jnp.stack([q_gain_grad, k_gain_grad])], axis=1
+    )
+    for axis in ("fsdp", "ctx"):
+        for bit in bits_down(lax.axis_size(axis)):
+            gain_sums = gain_sums + swap(gain_sums, axis, bit)
     norm_grad = lax.dynamic_slice_in_dim(gain_sums, f * norm_rows, norm_rows, axis=1).T
-    head_rows = head_gains.shape[0]
     head_grad = lax.dynamic_slice_in_dim(
         gain_sums, model_width + f * head_rows, head_rows, axis=1
     ).T
@@ -312,8 +323,8 @@
         out_grad,
         norm_grad,
         head_grad,
-        jnp.stack(gate_up_grads, axis=1),
-        jnp.stack(down_grads, axis=1),
+        gate_up_grad.transpose(1, 0, 2),
+        down_grad.transpose(1, 0, 2),
     )
 
 

time: 1230 us -> 821 us (0.67)
  waiting for transfers between devices: 493 us -> 291 us
  blocking collectives: 124 us -> 0 us
  local copies, waits for them, and re-layouts: 128 us -> 48.5 us
  other arithmetic: 137 us -> 67.7 us
  starting transfers between devices: 167 us -> 210 us
    ppermute x110 -> x86, waiting for transfers between devices: 493 us -> 289 us  [swap(): return lax.ppermute(value, axis, [(i, i ^ mask) for i in range(size)])]
    all_gather x2 -> x0, blocking collectives: 75.7 us -> none  [the longest x1 45.2 us: body(): lax.all_gather(jnp.concatenate([norm_gains, head_gains], axis=0).T, 'fsdp...]
    psum x1 -> x0, blocking collectives: 48.7 us -> none  [body(): lax.psum(jnp.concatenate([jnp.stack([gain_one_grad, gain_two_grad]), jnp....]
    ppermute x110 -> x86, starting transfers between devices: 163 us -> 207 us  [swap(): return lax.ppermute(value, axis, [(i, i ^ mask) for i in range(size)])]
    slice x40 -> x1, local copies, waits for them, and re-layouts: 34.5 us -> 1.25 us  [body(): da2 = scatter_fsdp([grads_back[q] for q in range(n_fsdp)])]
    another operation x11 -> x3, other arithmetic: 38.2 us -> 6.51 us  [the longest x4 23.5 us: body(): jnp.stack(gate_up_grads, axis=1)]
    concatenate x29 -> x2, local copies, waits for them, and re-layouts: 26.6 us -> 0.08 us  [the longest x1 0.04 us: body(): a2_all = jnp.concatenate(gather_fsdp(a2_low), axis=0)]
    concatenate x18 -> x0, other arithmetic: 24.4 us -> none  [the longest x15 12.9 us: xor_blocks(): flipped = jnp.concatenate([parts[..., 1:, :], parts[..., :1, :]], axis=-2)]
  transfers between devices with their start and end apart: 112 -> 92, of which waited for: 36 -> 32; matrix products, arithmetic and copies ran while one was open for 31% -> 28% of each run, Pallas kernels for 0% -> 1%
where the time goes in v2:
time: 821 us; the launch traced here: 811 us
  waiting for transfers between devices  291 us (35%)
  starting transfers between devices  210 us (26%)
  matrix products  169 us (21%)
  other arithmetic  67.7 us (8%)
  local copies, waits for them, and re-layouts  48.5 us (6%)
  between operations  15.6 us (2%)
  Pallas kernels  10.1 us (1%)
    ppermute x86, waiting for transfers between devices, swap(): return lax.ppermute(value, axis, [(i, i ^ mask) for i in range(size)])  289 us
    ppermute x86, starting transfers between devices, swap(): return lax.ppermute(value, axis, [(i, i ^ mask) for i in range(size)])  207 us
    unnamed x200, local copies, waits for them, and re-layouts  21.3 us
    dot_general x1, matrix products, body(): jnp.einsum('erd,erk->edk', rows, pair_grad, preferred_element_type=f32)  19.9 us
    dot_general x1, matrix products, body(): jnp.einsum('erk,edk->erd', pair_grad, gate_up_all, preferred_element_type...  17 us
    dot_general x1, matrix products, body(): mixed = jnp.einsum('est,esd->td', picks, made, preferred_element_type=f32)  16.6 us
  transfers between devices with their start and end apart: 92, of which 32 were waited for; matrix products, arithmetic and copies ran while one was open for 28% of the time, Pallas kernels for 1%

profile of v2, /device:TPU:0, one launch (start us, length us, event | category | flops | bytes accessed | tf_op | source)
XLA Modules:
  0.0 811.4 jit_solution(1042279091517723358)
XLA Ops:
  45.3 8.2 %collective-permute-start.19 = (bf16[64,2048]{1,0:T(8,128)(2,1)S(1)}, bf16[64,2048]{1,0:T(8,128)(2,1)}, u32[]{:S(2)}, u32[]{:S(2)}) collective-permute-start(bf16[64,2048]{1,0:T(8,128)(2,1)S(1)} %collective-permute-done.17), channel_id=1, source_target_pairs={{0,2},{1,3},{2,0},{3,1},{4,6},{5,7},{6,4},{7,5},{8,10},{9,11},{10,... | collective-permute-start | bytes 786440 | tf_op jit(solution)/shard_map/ppermute | solution.py:33
  62.8 13.1 %collective-permute-start.11 = (bf16[256,3,512]{0,2,1:T(8,128)(2,1)S(1)}, bf16[256,3,512]{0,2,1:T(8,128)(2,1)S(1)}, u32[]{:S(2)}, u32[]{:S(2)}) collective-permute-start(bf16[256,3,512]{0,2,1:T(8,128)(2,1)S(1)} %copy.127), channel_id=1, source_target_pairs={{0,2},{1,3},{2,0},{3,1},{4,6},{5,7},{6,4},{7,5},{8,10},{9,11},{10,... | collective-permute-start | bytes 2359304 | tf_op jit(solution)/shard_map/ppermute | solution.py:33
  91.2 14.5 %collective-permute-done.11 = bf16[256,3,512]{0,2,1:T(8,128)(2,1)S(1)} collective-permute-done((bf16[256,3,512]{0,2,1:T(8,128)(2,1)S(1)}, bf16[256,3,512]{0,2,1:T(8,128)(2,1)S(1)}, u32[]{:S(2)}, u32[]{:S(2)}) %collective-permute-start.11) | collective-permute-done | bytes 786464 | tf_op jit(solution)/shard_map/ppermute | solution.py:33
  105.8 29.0 %collective-permute-done.13 = bf16[256,3,512]{0,2,1:T(8,128)(2,1)S(1)} collective-permute-done((bf16[256,3,512]{0,2,1:T(8,128)(2,1)S(1)}, bf16[256,3,512]{0,2,1:T(8,128)(2,1)S(1)}, u32[]{:S(2)}, u32[]{:S(2)}) %collective-permute-start.13) | collective-permute-done | bytes 786464 | tf_op jit(solution)/shard_map/ppermute | solution.py:33
  140.1 11.0 %collective-permute-start.43 = (bf16[128,2048]{1,0:T(8,128)(2,1)}, bf16[128,2048]{1,0:T(8,128)(2,1)}, u32[]{:S(2)}, u32[]{:S(2)}) collective-permute-start(bf16[128,2048]{1,0:T(8,128)(2,1)} %bitcast.38), channel_id=1, source_target_pairs={{0,2},{1,3},{2,0},{3,1},{4,6},{5,7},{6,4},{7,5},{8,10},{9,11},{10,... | collective-permute-start | bytes 1572872 | tf_op jit(solution)/shard_map/ppermute | solution.py:33
  160.6 20.7 %collective-permute-done.16 = bf16[256,3,512]{0,2,1:T(8,128)(2,1)S(1)} collective-permute-done((bf16[256,3,512]{0,2,1:T(8,128)(2,1)S(1)}, bf16[256,3,512]{0,2,1:T(8,128)(2,1)S(1)}, u32[]{:S(2)}, u32[]{:S(2)}) %collective-permute-start.16) | collective-permute-done | bytes 786464 | tf_op jit(solution)/shard_map/ppermute | solution.py:33
  214.0 8.3 %collective-permute-done.44 = bf16[128,2048]{1,0:T(8,128)(2,1)S(1)} collective-permute-done((bf16[128,2048]{1,0:T(8,128)(2,1)}, bf16[128,2048]{1,0:T(8,128)(2,1)S(1)}, u32[]{:S(2)}, u32[]{:S(2)}) %collective-permute-start.44) | collective-permute-done | bytes 524320 | tf_op jit(solution)/shard_map/ppermute | solution.py:33
  223.4 13.1 %collective-permute-done.27 = bf16[128,2048]{1,0:T(8,128)(2,1)S(1)} collective-permute-done((bf16[128,2048]{1,0:T(8,128)(2,1)S(1)}, bf16[128,2048]{1,0:T(8,128)(2,1)S(1)}, u32[]{:S(2)}, u32[]{:S(2)}) %collective-permute-start.27) | collective-permute-done | bytes 524320 | tf_op jit(solution)/shard_map/ppermute | solution.py:33
  262.2 22.0 %collective-permute-done.31 = bf16[128,2048]{1,0:T(8,128)(2,1)S(1)} collective-permute-done((bf16[128,2048]{1,0:T(8,128)(2,1)S(1)}, bf16[128,2048]{1,0:T(8,128)(2,1)S(1)}, u32[]{:S(2)}, u32[]{:S(2)}) %collective-permute-start.31) | collective-permute-done | bytes 524320 | tf_op jit(solution)/shard_map/ppermute | solution.py:33
  286.5 12.6 %collective-permute-done.32 = bf16[128,2048]{1,0:T(8,128)(2,1)S(1)} collective-permute-done((bf16[128,2048]{1,0:T(8,128)(2,1)S(1)}, bf16[128,2048]{1,0:T(8,128)(2,1)S(1)}, u32[]{:S(2)}, u32[]{:S(2)}) %collective-permute-start.32) | collective-permute-done | bytes 524320 | tf_op jit(solution)/shard_map/ppermute | solution.py:33
  299.2 7.9 collective-permute-done.34
  314.8 11.6 %fusion.99 = f32[3,424,1024]{2,1,0:T(8,128)} fusion(bf16[3,424,2048]{2,1,0:T(8,128)(2,1)} %multiply_convert_fusion, bf16[3,2048,1024]{2,1,0:T(8,128)(2,1)} %all-gather.5.cloned.1.call-done), kind=kOutput, calls=%fused_computation.270 | convolution fusion | flops 5335154688 | bytes 23003136 | tf_op jit(solution)/shard_map/erd,edf->erf/dot_general | solution.py:244
  326.4 11.6 %fusion.1 = f32[3,424,1024]{2,1,0:T(8,128)} fusion(bf16[3,424,2048]{2,1,0:T(8,128)(2,1)} %fusion.23, bf16[3,2048,2048]{2,1,0:T(8,128)(2,1)} %all-gather.3.cloned.1.call-done), kind=kOutput, calls=%fused_computation.2 | convolution fusion | flops 5335154688 | bytes 23003136 | tf_op jit(solution)/shard_map/erd,edk->erk/dot_general | solution.py:243
  338.0 15.6 %multiply_convert_fusion.4 = (bf16[3,424,1024]{2,1,0:T(8,128)(2,1)}, bf16[3,424,1024]{2,1,0:T(8,128)(2,1)}, bf16[3,424,1024]{2,1,0:T(8,128)(2,1)S(1)}) fusion(f32[3,424,1024]{2,1,0:T(8,128)} %fusion.99, f32[3,424,1024]{2,1,0:T(8,128)} %fusion.1, bf16[3,424,2048]{2,1,0:T(8,128)(2,1)} %fusion.23, bf16[3,2048,2048]{2,1,0:T(8,128)(2,1)} %all-gather.3.cloned.1.call-done), kind=kOutput, calls=%fused_computation.20 | convolution fusion | flops 5354692608 | bytes 36028416 | tf_op jit(solution)/shard_map/erd,edk->erk/dot_general | solution.py:242
  353.6 13.2 %convolution_convert_fusion.1 = bf16[3,2048,1024]{2,1,0:T(8,128)(2,1)} fusion(bf16[3,424,2048]{2,1,0:T(8,128)(2,1)} %multiply_convert_fusion, bf16[3,424,1024]{2,1,0:T(8,128)(2,1)S(1)} %get-tuple-element.27), kind=kOutput, calls=%fused_computation.11 | convolution fusion | flops 5341446144 | bytes 20398080 | tf_op jit(solution)/shard_map/erd,erf->edf/dot_general | solution.py:260
  368.5 19.9 %convolution_convert_fusion = bf16[3,2048,2048]{2,1,0:T(8,128)(2,1)} fusion(bf16[3,424,2048]{2,1,0:T(8,128)(2,1)} %fusion.23, bf16[3,424,1024]{2,1,0:T(8,128)(2,1)} %get-tuple-element.26, bf16[3,424,1024]{2,1,0:T(8,128)(2,1)S(1)} %copy-done.85), kind=kOutput, calls=%fused_computation.1 | convolution fusion | flops 10693312512 | bytes 35586048 | tf_op jit(solution)/shard_map/erd,erk->edk/dot_general | solution.py:262
  388.5 17.0 %fusion.28 = bf16[3,424,2048]{2,1,0:T(8,128)(2,1)} fusion(bf16[3,2048,2048]{2,1,0:T(8,128)(2,1)} %all-gather.3.cloned.1.call-done, bf16[3,424,1024]{2,1,0:T(8,128)(2,1)} %get-tuple-element.26, bf16[3,424,1024]{2,1,0:T(8,128)(2,1)S(1)} %copy-done.85), kind=kOutput, calls=%fused_computation.45 | convolution fusion | flops 10680729600 | bytes 35586048 | tf_op jit(solution)/shard_map/erk,edk->erd/dot_general | solution.py:250
  405.4 8.4 %bitcast_convert_fusion = bf16[1024,2048]{1,0:T(8,128)(2,1)S(1)} fusion(bf16[3,424,2048]{2,1,0:T(8,128)(2,1)} %fusion.28, s32[3,1024]{1,0:T(4,128)S(1)} %fusion.45), kind=kOutput, calls=%fused_computation.9 | convolution fusion | flops 5338554368 | bytes 9416704 | tf_op jit(solution)/shard_map/est,esd->td/dot_general | solution.py:251
  419.2 10.8 %collective-permute-done.50 = bf16[128,2048]{1,0:T(8,128)(2,1)S(1)} collective-permute-done((bf16[128,2048]{1,0:T(8,128)(2,1)S(1)}, bf16[128,2048]{1,0:T(8,128)(2,1)S(1)}, u32[]{:S(2)}, u32[]{:S(2)}) %collective-permute-start.50) | collective-permute-done | bytes 524320 | tf_op jit(solution)/shard_map/ppermute | solution.py:33
  430.0 11.2 %collective-permute-done.54 = bf16[128,2048]{1,0:T(8,128)(2,1)S(1)} collective-permute-done((bf16[128,2048]{1,0:T(8,128)(2,1)S(1)}, bf16[128,2048]{1,0:T(8,128)(2,1)S(1)}, u32[]{:S(2)}, u32[]{:S(2)}) %collective-permute-start.54) | collective-permute-done | bytes 524320 | tf_op jit(solution)/shard_map/ppermute | solution.py:33
  441.2 11.2 %collective-permute-done.52 = bf16[128,2048]{1,0:T(8,128)(2,1)S(1)} collective-permute-done((bf16[128,2048]{1,0:T(8,128)(2,1)S(1)}, bf16[128,2048]{1,0:T(8,128)(2,1)S(1)}, u32[]{:S(2)}, u32[]{:S(2)}) %collective-permute-start.52) | collective-permute-done | bytes 524320 | tf_op jit(solution)/shard_map/ppermute | solution.py:33
  457.6 16.6 %bitcast_convert_fusion.1 = bf16[1024,2048]{1,0:T(8,128)(2,1)} fusion(bf16[3,424,1024]{2,1,0:T(8,128)(2,1)} %copy-done.84, bf16[3,2048,1024]{2,1,0:T(8,128)(2,1)} %all-gather.5.cloned.1.call-done, f32[3,424]{1,0:T(4,128)S(1)} %copy-done.58, s32[3,1024]{1,0:T(4,128)S(1)} %fusion.45), kind=kOutput, calls=%fused_computation.10 | convolution fusion | flops 10684129280 | bytes 19399648 | tf_op jit(solution)/shard_map/est,esd->td/dot_general | solution.py:256
  477.9 16.9 %collective-permute-done.53 = bf16[128,2048]{1,0:T(8,128)(2,1)} collective-permute-done((bf16[128,2048]{1,0:T(8,128)(2,1)S(1)}, bf16[128,2048]{1,0:T(8,128)(2,1)}, u32[]{:S(2)}, u32[]{:S(2)}) %collective-permute-start.53) | collective-permute-done | bytes 524320 | tf_op jit(solution)/shard_map/ppermute | solution.py:33
  502.6 17.0 %collective-permute-done.57 = bf16[128,2048]{1,0:T(8,128)(2,1)} collective-permute-done((bf16[128,2048]{1,0:T(8,128)(2,1)}, bf16[128,2048]{1,0:T(8,128)(2,1)}, u32[]{:S(2)}, u32[]{:S(2)}) %collective-permute-start.57) | collective-permute-done | bytes 524320 | tf_op jit(solution)/shard_map/ppermute | solution.py:33
  601.5 8.1 collective-permute-done.76
  649.2 9.2 %collective-permute-start.37 = (bf16[128,2048]{1,0:T(8,128)(2,1)}, bf16[128,2048]{1,0:T(8,128)(2,1)S(1)}, u32[]{:S(2)}, u32[]{:S(2)}) collective-permute-start(bf16[128,2048]{1,0:T(8,128)(2,1)} %get-tuple-element.46), channel_id=1, source_target_pairs={{0,2},{1,3},{2,0},{3,1},{4,6},{5,7},{6,4},{7,5},{8,10},{9,11},{10,... | collective-permute-start | bytes 1572872 | tf_op jit(solution)/shard_map/ppermute | solution.py:33
  672.5 13.8 %collective-permute-start.62 = (bf16[256,3,512]{2,0,1:T(8,128)(2,1)S(1)}, bf16[256,3,512]{2,0,1:T(8,128)(2,1)S(1)}, u32[]{:S(2)}, u32[]{:S(2)}) collective-permute-start(bf16[256,3,512]{2,0,1:T(8,128)(2,1)S(1)} %copy-done.32), channel_id=1, source_target_pairs={{0,1},{1,0},{2,3},{3,2},{4,5},{5,4},{6,7},{7,6},{8,9},{9,8},{10,11... | collective-permute-start | bytes 2359304 | tf_op jit(solution)/shard_map/ppermute | solution.py:33
  691.9 35.7 %collective-permute-start.85 = (f32[2,2176]{1,0:T(2,128)S(1)}, f32[2,2176]{1,0:T(2,128)S(1)}, u32[]{:S(2)}, u32[]{:S(2)}) collective-permute-start(f32[2,2176]{1,0:T(2,128)S(1)} %fusion.125), channel_id=1, source_target_pairs={{0,1},{1,0},{2,3},{3,2},{4,5},{5,4},{6,7},{7,6},{8,9},{9,8},{10,11... | collective-permute-start | bytes 52232 | tf_op jit(solution)/shard_map/ppermute | solution.py:33
  729.3 7.8 collective-permute-start.81
  743.5 13.9 %collective-permute-done.66 = bf16[256,3,512]{2,0,1:T(8,128)(2,1)S(1)} collective-permute-done((bf16[256,3,512]{2,0,1:T(8,128)(2,1)S(1)}, bf16[256,3,512]{2,0,1:T(8,128)(2,1)S(1)}, u32[]{:S(2)}, u32[]{:S(2)}) %collective-permute-start.66) | collective-permute-done | bytes 786464 | tf_op jit(solution)/shard_map/ppermute | solution.py:33
  770.7 14.3 %collective-permute-done.70 = bf16[256,3,512]{2,0,1:T(8,128)(2,1)S(1)} collective-permute-done((bf16[256,3,512]{2,0,1:T(8,128)(2,1)S(1)}, bf16[256,3,512]{2,0,1:T(8,128)(2,1)S(1)}, u32[]{:S(2)}, u32[]{:S(2)}) %collective-permute-start.70) | collective-permute-done | bytes 786464 | tf_op jit(solution)/shard_map/ppermute | solution.py:33
  795.4 9.2 %convert_bitcast_fusion = f32[512,3,2048]{2,0,1:T(8,128)} fusion(bf16[3,512,2048]{2,1,0:T(8,128)(2,1)} %reduce-scatter.3.cloned.1.call-done), kind=kLoop, calls=%fused_computation.6 | loop fusion | flops 3145728 | bytes 18874368 | tf_op jit(solution)/shard_map/transpose | solution.py:326
  (494 shorter events, 342.2 us)
Async XLA Ops:
  7.2 307.6 %all-gather.5.cloned.1.call-start = ((), (), s32[]{:S(2)}) async-start(), calls=%async_computation.3 | async-start | bytes 15728640 | tf_op jit(solution)/shard_map/all_gather | solution.py:183
  7.9 318.4 %all-gather.3.cloned.1.call-start = ((), (), s32[]{:S(2)}) async-start(), calls=%async_computation.2 | async-start | bytes 31457280 | tf_op jit(solution)/shard_map/all_gather | solution.py:182
  8.7 781.4 %reduce-scatter.5.cloned.1.call-start = ((), (), s32[]{:S(2)}) async-start(), calls=%async_computation.5 | async-start | bytes 15728640 | tf_op jit(solution)/shard_map/reduce_scatter | solution.py:261
  18.8 71.9 %collective-permute-start.10 = (bf16[256,3,512]{0,2,1:T(8,128)(2,1)S(1)}, bf16[256,3,512]{0,2,1:T(8,128)(2,1)}, u32[]{:S(2)}, u32[]{:S(2)}) collective-permute-start(bf16[256,3,512]{0,2,1:T(8,128)(2,1)S(1)} %copy.127), channel_id=1, source_target_pairs={{0,1},{1,0},{2,3},{3,2},{4,5},{5,4},{6,7},{7,6},{8,9},{9,8},{10,11... | collective-permute-start | bytes 2359304 | tf_op jit(solution)/shard_map/ppermute | solution.py:33
  37.5 45.2 %collective-permute-start.1 = (bf16[128,2048]{1,0:T(8,128)(2,1)}, bf16[128,2048]{1,0:T(8,128)(2,1)}, u32[]{:S(2)}, u32[]{:S(2)}) collective-permute-start(bf16[128,2048]{1,0:T(8,128)(2,1)} %shard_map.170), channel_id=1, source_target_pairs={{0,16},{8,24},{16,0},{24,8},{1,17},{9,25},{17,1},{25,9},{2,18},{10... | collective-permute-start | bytes 1572872 | tf_op jit(solution)/shard_map/ppermute | solution.py:33
  62.8 43.0 %collective-permute-start.11 = (bf16[256,3,512]{0,2,1:T(8,128)(2,1)S(1)}, bf16[256,3,512]{0,2,1:T(8,128)(2,1)S(1)}, u32[]{:S(2)}, u32[]{:S(2)}) collective-permute-start(bf16[256,3,512]{0,2,1:T(8,128)(2,1)S(1)} %copy.127), channel_id=1, source_target_pairs={{0,2},{1,3},{2,0},{3,1},{4,6},{5,7},{6,4},{7,5},{8,10},{9,11},{10,... | collective-permute-start | bytes 2359304 | tf_op jit(solution)/shard_map/ppermute | solution.py:33
  75.9 58.9 %collective-permute-start.13 = (bf16[256,3,512]{0,2,1:T(8,128)(2,1)S(1)}, bf16[256,3,512]{0,2,1:T(8,128)(2,1)S(1)}, u32[]{:S(2)}, u32[]{:S(2)}) collective-permute-start(bf16[256,3,512]{0,2,1:T(8,128)(2,1)S(1)} %copy.127), channel_id=1, source_target_pairs={{0,4},{1,5},{2,6},{3,7},{4,0},{5,1},{6,2},{7,3},{8,12},{9,13},{10,... | collective-permute-start | bytes 2359304 | tf_op jit(solution)/shard_map/ppermute | solution.py:33
  85.0 55.1 %collective-permute-start.15 = (bf16[256,3,512]{0,2,1:T(8,128)(2,1)S(1)}, bf16[256,3,512]{0,2,1:T(8,128)(2,1)S(1)}, u32[]{:S(2)}, u32[]{:S(2)}) collective-permute-start(bf16[256,3,512]{0,2,1:T(8,128)(2,1)S(1)} %copy.127), channel_id=1, source_target_pairs={{0,6},{1,7},{2,4},{3,5},{4,2},{5,3},{6,0},{7,1},{8,14},{9,15},{10,... | collective-permute-start | bytes 2359304 | tf_op jit(solution)/shard_map/ppermute | solution.py:33
  90.7 47.9 %collective-permute-start = (bf16[128,2048]{1,0:T(8,128)(2,1)S(1)}, bf16[128,2048]{1,0:T(8,128)(2,1)S(1)}, u32[]{:S(2)}, u32[]{:S(2)}) collective-permute-start(bf16[128,2048]{1,0:T(8,128)(2,1)S(1)} %copy-done.24), channel_id=1, source_target_pairs={{0,8},{8,0},{16,24},{24,16},{1,9},{9,1},{17,25},{25,17},{2,10},{10... | collective-permute-start | bytes 1572872 | tf_op jit(solution)/shard_map/ppermute | solution.py:33
  90.7 60.4 %collective-permute-start.2 = (bf16[128,2048]{1,0:T(8,128)(2,1)}, bf16[128,2048]{1,0:T(8,128)(2,1)S(1)}, u32[]{:S(2)}, u32[]{:S(2)}) collective-permute-start(bf16[128,2048]{1,0:T(8,128)(2,1)} %collective-permute-done.1), channel_id=1, source_target_pairs={{0,8},{8,0},{16,24},{24,16},{1,9},{9,1},{17,25},{25,17},{2,10},{10... | collective-permute-start | bytes 1572872 | tf_op jit(solution)/shard_map/ppermute | solution.py:33
  105.8 48.6 %collective-permute-start.12 = (bf16[256,3,512]{0,2,1:T(8,128)(2,1)S(1)}, bf16[256,3,512]{0,2,1:T(8,128)(2,1)S(1)}, u32[]{:S(2)}, u32[]{:S(2)}) collective-permute-start(bf16[256,3,512]{0,2,1:T(8,128)(2,1)S(1)} %collective-permute-done.11), channel_id=1, source_target_pairs={{0,1},{1,0},{2,3},{3,2},{4,5},{5,4},{6,7},{7,6},{8,9},{9,8},{10,11... | collective-permute-start | bytes 2359304 | tf_op jit(solution)/shard_map/ppermute | solution.py:33
  138.6 70.6 %collective-permute-start.42 = (bf16[128,2048]{1,0:T(8,128)(2,1)}, bf16[128,2048]{1,0:T(8,128)(2,1)}, u32[]{:S(2)}, u32[]{:S(2)}) collective-permute-start(bf16[128,2048]{1,0:T(8,128)(2,1)} %bitcast.38), channel_id=1, source_target_pairs={{0,1},{1,0},{2,3},{3,2},{4,5},{5,4},{6,7},{7,6},{8,9},{9,8},{10,11... | collective-permute-start | bytes 1572872 | tf_op jit(solution)/shard_map/ppermute | solution.py:33
  140.1 67.2 %collective-permute-start.43 = (bf16[128,2048]{1,0:T(8,128)(2,1)}, bf16[128,2048]{1,0:T(8,128)(2,1)}, u32[]{:S(2)}, u32[]{:S(2)}) collective-permute-start(bf16[128,2048]{1,0:T(8,128)(2,1)} %bitcast.38), channel_id=1, source_target_pairs={{0,2},{1,3},{2,0},{3,1},{4,6},{5,7},{6,4},{7,5},{8,10},{9,11},{10,... | collective-permute-start | bytes 1572872 | tf_op jit(solution)/shard_map/ppermute | solution.py:33
  154.3 57.5 %collective-permute-start.45 = (bf16[128,2048]{1,0:T(8,128)(2,1)}, bf16[128,2048]{1,0:T(8,128)(2,1)}, u32[]{:S(2)}, u32[]{:S(2)}) collective-permute-start(bf16[128,2048]{1,0:T(8,128)(2,1)} %bitcast.38), channel_id=1, source_target_pairs={{0,4},{1,5},{2,6},{3,7},{4,0},{5,1},{6,2},{7,3},{8,12},{9,13},{10,... | collective-permute-start | bytes 1572872 | tf_op jit(solution)/shard_map/ppermute | solution.py:33
  156.3 56.0 %collective-permute-start.47 = (bf16[128,2048]{1,0:T(8,128)(2,1)}, bf16[128,2048]{1,0:T(8,128)(2,1)}, u32[]{:S(2)}, u32[]{:S(2)}) collective-permute-start(bf16[128,2048]{1,0:T(8,128)(2,1)} %bitcast.38), channel_id=1, source_target_pairs={{0,6},{1,7},{2,4},{3,5},{4,2},{5,3},{6,0},{7,1},{8,14},{9,15},{10,... | collective-permute-start | bytes 1572872 | tf_op jit(solution)/shard_map/ppermute | solution.py:33
  244.5 40.3 %collective-permute-start.28 = (bf16[128,2048]{1,0:T(8,128)(2,1)S(1)}, bf16[128,2048]{1,0:T(8,128)(2,1)S(1)}, u32[]{:S(2)}, u32[]{:S(2)}) collective-permute-start(bf16[128,2048]{1,0:T(8,128)(2,1)S(1)} %get-tuple-element.22), channel_id=1, source_target_pairs={{0,1},{1,0},{2,3},{3,2},{4,5},{5,4},{6,7},{7,6},{8,9},{9,8},{10,11... | collective-permute-start | bytes 1572872 | tf_op jit(solution)/shard_map/ppermute | solution.py:33
  366.8 428.6 %reduce-scatter.3.cloned.1.call-start = ((), (), s32[]{:S(2)}) async-start(), calls=%async_computation.4 | async-start | bytes 31457280 | tf_op jit(solution)/shard_map/reduce_scatter | solution.py:263
  417.2 60.7 %collective-permute-start.49 = (bf16[128,2048]{1,0:T(8,128)(2,1)}, bf16[128,2048]{1,0:T(8,128)(2,1)}, u32[]{:S(2)}, u32[]{:S(2)}) collective-permute-start(bf16[128,2048]{1,0:T(8,128)(2,1)} %get-tuple-element.35), channel_id=1, source_target_pairs={{0,1},{1,0},{2,3},{3,2},{4,5},{5,4},{6,7},{7,6},{8,9},{9,8},{10,11... | collective-permute-start | bytes 1572872 | tf_op jit(solution)/shard_map/ppermute | solution.py:33
  453.7 41.1 %collective-permute-start.53 = (bf16[128,2048]{1,0:T(8,128)(2,1)S(1)}, bf16[128,2048]{1,0:T(8,128)(2,1)}, u32[]{:S(2)}, u32[]{:S(2)}) collective-permute-start(bf16[128,2048]{1,0:T(8,128)(2,1)S(1)} %get-tuple-element.41), channel_id=1, source_target_pairs={{0,4},{1,5},{2,6},{3,7},{4,0},{5,1},{6,2},{7,3},{8,12},{9,13},{10,... | collective-permute-start | bytes 1572872 | tf_op jit(solution)/shard_map/ppermute | solution.py:33
  454.8 40.0 %collective-permute-start.51 = (bf16[128,2048]{1,0:T(8,128)(2,1)S(1)}, bf16[128,2048]{1,0:T(8,128)(2,1)}, u32[]{:S(2)}, u32[]{:S(2)}) collective-permute-start(bf16[128,2048]{1,0:T(8,128)(2,1)S(1)} %get-tuple-element.39), channel_id=1, source_target_pairs={{0,2},{1,3},{2,0},{3,1},{4,6},{5,7},{6,4},{7,5},{8,10},{9,11},{10,... | collective-permute-start | bytes 1572872 | tf_op jit(solution)/shard_map/ppermute | solution.py:33
  477.9 41.8 %collective-permute-start.36 = (bf16[128,2048]{1,0:T(8,128)(2,1)}, bf16[128,2048]{1,0:T(8,128)(2,1)S(1)}, u32[]{:S(2)}, u32[]{:S(2)}) collective-permute-start(bf16[128,2048]{1,0:T(8,128)(2,1)} %get-tuple-element.45), channel_id=1, source_target_pairs={{0,1},{1,0},{2,3},{3,2},{4,5},{5,4},{6,7},{7,6},{8,9},{9,8},{10,11... | collective-permute-start | bytes 1572872 | tf_op jit(solution)/shard_map/ppermute | solution.py:33
  564.2 48.2 %collective-permute-start.59 = (bf16[128,2048]{1,0:T(8,128)(2,1)S(1)}, bf16[128,2048]{1,0:T(8,128)(2,1)S(1)}, u32[]{:S(2)}, u32[]{:S(2)}) collective-permute-start(bf16[128,2048]{1,0:T(8,128)(2,1)S(1)} %get-tuple-element.58), channel_id=1, source_target_pairs={{0,8},{8,0},{16,24},{24,16},{1,9},{9,1},{17,25},{25,17},{2,10},{10... | collective-permute-start | bytes 1572872 | tf_op jit(solution)/shard_map/ppermute | solution.py:33
  599.7 86.6 %collective-permute-start.35 = (bf16[128,2048]{1,0:T(8,128)(2,1)}, bf16[128,2048]{1,0:T(8,128)(2,1)}, u32[]{:S(2)}, u32[]{:S(2)}) collective-permute-start(bf16[128,2048]{1,0:T(8,128)(2,1)} %get-tuple-element.42), channel_id=1, source_target_pairs={{0,1},{1,0},{2,3},{3,2},{4,5},{5,4},{6,7},{7,6},{8,9},{9,8},{10,11... | collective-permute-start | bytes 1572872 | tf_op jit(solution)/shard_map/ppermute | solution.py:33
  612.5 50.3 %collective-permute-start.65 = (bf16[256,3,512]{2,0,1:T(8,128)(2,1)}, bf16[256,3,512]{2,0,1:T(8,128)(2,1)}, u32[]{:S(2)}, u32[]{:S(2)}) collective-permute-start(bf16[256,3,512]{2,0,1:T(8,128)(2,1)} %get-tuple-element.30), channel_id=1, source_target_pairs={{0,1},{1,0},{2,3},{3,2},{4,5},{5,4},{6,7},{7,6},{8,9},{9,8},{10,11... | collective-permute-start | bytes 2359304 | tf_op jit(solution)/shard_map/ppermute | solution.py:33
  637.1 53.1 %collective-permute-start.41 = (bf16[128,2048]{1,0:T(8,128)(2,1)}, bf16[128,2048]{1,0:T(8,128)(2,1)S(1)}, u32[]{:S(2)}, u32[]{:S(2)}) collective-permute-start(bf16[128,2048]{1,0:T(8,128)(2,1)} %get-tuple-element.47), channel_id=1, source_target_pairs={{0,6},{1,7},{2,4},{3,5},{4,2},{5,3},{6,0},{7,1},{8,14},{9,15},{10,... | collective-permute-start | bytes 1572872 | tf_op jit(solution)/shard_map/ppermute | solution.py:33
  639.6 51.7 %collective-permute-start.39 = (bf16[128,2048]{1,0:T(8,128)(2,1)}, bf16[128,2048]{1,0:T(8,128)(2,1)S(1)}, u32[]{:S(2)}, u32[]{:S(2)}) collective-permute-start(bf16[128,2048]{1,0:T(8,128)(2,1)} %get-tuple-element.48), channel_id=1, source_target_pairs={{0,4},{1,5},{2,6},{3,7},{4,0},{5,1},{6,2},{7,3},{8,12},{9,13},{10,... | collective-permute-start | bytes 1572872 | tf_op jit(solution)/shard_map/ppermute | solution.py:33
  649.2 42.7 %collective-permute-start.37 = (bf16[128,2048]{1,0:T(8,128)(2,1)}, bf16[128,2048]{1,0:T(8,128)(2,1)S(1)}, u32[]{:S(2)}, u32[]{:S(2)}) collective-permute-start(bf16[128,2048]{1,0:T(8,128)(2,1)} %get-tuple-element.46), channel_id=1, source_target_pairs={{0,2},{1,3},{2,0},{3,1},{4,6},{5,7},{6,4},{7,5},{8,10},{9,11},{10,... | collective-permute-start | bytes 1572872 | tf_op jit(solution)/shard_map/ppermute | solution.py:33
  672.5 68.2 %collective-permute-start.62 = (bf16[256,3,512]{2,0,1:T(8,128)(2,1)S(1)}, bf16[256,3,512]{2,0,1:T(8,128)(2,1)S(1)}, u32[]{:S(2)}, u32[]{:S(2)}) collective-permute-start(bf16[256,3,512]{2,0,1:T(8,128)(2,1)S(1)} %copy-done.32), channel_id=1, source_target_pairs={{0,1},{1,0},{2,3},{3,2},{4,5},{5,4},{6,7},{7,6},{8,9},{9,8},{10,11... | collective-permute-start | bytes 2359304 | tf_op jit(solution)/shard_map/ppermute | solution.py:33
  686.3 55.2 %collective-permute-start.68 = (bf16[256,3,512]{2,0,1:T(8,128)(2,1)S(1)}, bf16[256,3,512]{2,0,1:T(8,128)(2,1)S(1)}, u32[]{:S(2)}, u32[]{:S(2)}) collective-permute-start(bf16[256,3,512]{2,0,1:T(8,128)(2,1)S(1)} %get-tuple-element.33), channel_id=1, source_target_pairs={{0,6},{1,7},{2,4},{3,5},{4,2},{5,3},{6,0},{7,1},{8,14},{9,15},{10,... | collective-permute-start | bytes 2359304 | tf_op jit(solution)/shard_map/ppermute | solution.py:33
  690.2 67.2 %collective-permute-start.66 = (bf16[256,3,512]{2,0,1:T(8,128)(2,1)S(1)}, bf16[256,3,512]{2,0,1:T(8,128)(2,1)S(1)}, u32[]{:S(2)}, u32[]{:S(2)}) collective-permute-start(bf16[256,3,512]{2,0,1:T(8,128)(2,1)S(1)} %get-tuple-element.34), channel_id=1, source_target_pairs={{0,4},{1,5},{2,6},{3,7},{4,0},{5,1},{6,2},{7,3},{8,12},{9,13},{10,... | collective-permute-start | bytes 2359304 | tf_op jit(solution)/shard_map/ppermute | solution.py:33
  691.3 66.1 %collective-permute-start.64 = (bf16[256,3,512]{2,0,1:T(8,128)(2,1)S(1)}, bf16[256,3,512]{2,0,1:T(8,128)(2,1)S(1)}, u32[]{:S(2)}, u32[]{:S(2)}) collective-permute-start(bf16[256,3,512]{2,0,1:T(8,128)(2,1)S(1)} %get-tuple-element.32), channel_id=1, source_target_pairs={{0,2},{1,3},{2,0},{3,1},{4,6},{5,7},{6,4},{7,5},{8,10},{9,11},{10,... | collective-permute-start | bytes 2359304 | tf_op jit(solution)/shard_map/ppermute | solution.py:33
  741.5 43.6 %collective-permute-start.82 = (bf16[64,2048]{1,0:T(8,128)(2,1)S(1)}, bf16[64,2048]{1,0:T(8,128)(2,1)S(1)}, u32[]{:S(2)}, u32[]{:S(2)}) collective-permute-start(bf16[64,2048]{1,0:T(8,128)(2,1)S(1)} %collective-permute-done.81), channel_id=1, source_target_pairs={{0,8},{8,0},{16,24},{24,16},{1,9},{9,1},{17,25},{25,17},{2,10},{10... | collective-permute-start | bytes 786440 | tf_op jit(solution)/shard_map/ppermute | solution.py:33
  (146 other events, 2853.4 us)
Sparse Core Ops, SparseCore 0:
  9.6 103.2 all-gather.4
  114.5 170.0 all-gather.2
  366.9 95.9 reduce-scatter.4
  465.3 198.2 reduce-scatter.2

commit v3 on v2

v3 whole, which is shorter than its diff:
```python
import functools
import math

import jax
import jax.numpy as jnp
from jax import lax
from jax.experimental import pallas as pl
from jax.experimental.pallas import tpu as pltpu
from jax.sharding import PartitionSpec as P

EPS = 1e-06
ROPE_BASE = 10000.0
NEG_FILL = -1e30
LANES = 128
f32 = jnp.float32
bf16 = jnp.bfloat16
VMEM = pl.BlockSpec(memory_space=pltpu.VMEM)
SMEM = pl.BlockSpec(memory_space=pltpu.SMEM)
NN = (((1,), (0,)), ((), ()))
NT = (((1,), (1,)), ((), ()))
TN = (((0,), (0,)), ((), ()))


def mm(a, b, dims=NN):
    return lax.dot_general(a, b, dims, preferred_element_type=f32)


def rms_scale(values, gain):
    return values * lax.rsqrt(jnp.mean(values * values, axis=-1, keepdims=True) + EPS) * gain


def cost(microseconds):
    return pl.CostEstimate(flops=int(microseconds * 1e9), bytes_accessed=0, transcendentals=0)


def params(mib):
    return pltpu.CompilerParams(vmem_limit_bytes=mib * 2**20)


def after(value, *others):
    return lax.optimization_barrier((value, *others))[0]


def swap(value, axis, mask):
    size = lax.axis_size(axis)
    return lax.ppermute(value, axis, [(i, i ^ mask) for i in range(size)])


def bits_down(size):
    return [1 << b for b in reversed(range(size.bit_length() - 1))]


def gather_ctx(block):
    pieces = {0: block}
    for bit in bits_down(lax.axis_size("ctx")):
        pieces.update({q | bit: swap(piece, "ctx", bit) for q, piece in list(pieces.items())})
    return [pieces[q] for q in range(len(pieces))]


def folded_order(size):
    order = [0]
    for bit in bits_down(size):
        order = order + [q | bit for q in order]
    return order


def scatter_ctx(blocks):
    size = lax.axis_size("ctx")
    for bit in reversed(bits_down(size)):
        half = blocks.shape[0] // 2
        got = swap(blocks[half:], "ctx", bit)
        blocks = blocks[:half].astype(f32) + got.astype(f32)
        if half > 1:
            blocks = blocks.astype(bf16)
    return blocks[0]


def far_masks():
    return list(range(2, lax.axis_size("fsdp"), 2))


def gather_far(block):
    size = lax.axis_size("fsdp")
    masks = sorted(range(2, size, 2), key=lambda m: (m == size - 2, m == 2))
    far = {m: swap(block, "fsdp", m) for m in masks}
    return [block] + [far[m] for m in range(2, size, 2)]


def gather_near(pieces):
    out = []
    for piece in pieces:
        out += [piece, swap(piece, "fsdp", 1)]
    return out


def gather_fsdp(block):
    return gather_near(gather_far(block))


def scatter_first(even_a, odd_a, pairs_b):
    got = swap(odd_a, "fsdp", 1)
    sums_a = [even_a[i].astype(f32) + got[i].astype(f32) for i in range(even_a.shape[0])]
    sums_a = [sums_a[0]] + [part.astype(bf16) for part in sums_a[1:]]
    sum_b = pairs_b[0].astype(f32)
    for i, m in enumerate(far_masks()):
        sum_b = sum_b + swap(pairs_b[i + 1], "fsdp", m).astype(f32)
    return sums_a, sum_b[0], sum_b[1].astype(bf16)


def scatter_second(first, *others):
    sums_a, own_b, other_b = first
    total_a = sums_a[0]
    for i, m in enumerate(far_masks()):
        total_a = total_a + swap(after(sums_a[i + 1], *others), "fsdp", m).astype(f32)
    return total_a, own_b + swap(after(other_b, *others), "fsdp", 1).astype(f32)


def split_blocks(blocks, size):
    pairs = blocks.reshape(blocks.shape[0] // 2, 2, *blocks.shape[1:])
    parts_b = [pairs[i, :, :, size:] for i in range(pairs.shape[0])]
    return pairs[:, 0, :, :size], pairs[:, 1, :, :size], parts_b


def lane_chunk(values, flat):
    width = values.shape[1]
    row, lane = flat // width, flat % width
    return values[row : row + 1, lane : lane + LANES]


def at_block(block, width):
    return pl.ds(pl.multiple_of(block * width, LANES), width)


def rope(values, cosine, sine):
    return values * cosine + pltpu.roll(values, values.shape[1] // 2, 1) * sine


def rope_back(grads, cosine, sine):
    return grads * cosine + pltpu.roll(grads * sine, grads.shape[1] // 2, 1)


def over_blocks(block, carry, length, size):
    if length == size:
        return block(slice(0, size), carry)
    step = lambda i, kept: block(pl.ds(pl.multiple_of(i * size, size), size), kept)
    return lax.fori_loop(0, length // size, step, carry)


def out_kernel(f_ref, attn_ref, *refs):
    piece_refs, (own_ref, mixed_ref) = refs[:-2], refs[-2:]
    rows = piece_refs[0].shape[0]
    for q, piece_ref in enumerate(piece_refs):
        spot = pl.ds(pl.multiple_of(jnp.bitwise_xor(f_ref[0], q) * rows, rows), rows)
        own_ref[spot, :] = piece_ref[...]
    mixed_ref[...] = mm(attn_ref[...], own_ref[...]).astype(bf16)


def attend_kernel(sizes, f_ref, *refs):
    n_ctx, n_fsdp, head_dim, head_rows, norm_rows, q_rows = sizes
    x_refs, refs = refs[:n_ctx], refs[n_ctx:]
    w_refs, refs = refs[:n_fsdp], refs[n_fsdp:]
    cos_ref, sin_ref, dq_ref, dk_ref = refs[:4]
    a1_ref, qp_ref, kp_ref, q_ref, k_ref, v_ref, o_ref, gains_ref, heads_ref = refs[4:]
    f = f_ref[0]
    tok = x_refs[0].shape[0]
    length, width = q_ref.shape
    lane = lax.broadcasted_iota(jnp.int32, (8, LANES), 1)
    heads = [jnp.zeros((8, LANES), f32), jnp.zeros((8, LANES), f32)]
    for q in range(n_fsdp):
        block = jnp.bitwise_xor(f, q)
        extra = w_refs[q][3 * norm_rows :, :].astype(f32)
        for row in range(2):
            for k in range(norm_rows // LANES):
                spot = pl.ds(pl.multiple_of(block * norm_rows + k * LANES, LANES), LANES)
                gains_ref[row : row + 1, spot] = lane_chunk(extra, row * norm_rows + k * LANES)
            piece = jnp.broadcast_to(lane_chunk(extra, 2 * norm_rows + row * LANES), (8, LANES))
            piece = pltpu.roll(piece, block * head_rows, 1)
            heads[row] = jnp.where(lane // head_rows == block, piece, heads[row])
    for row in range(2):
        heads_ref[row : row + 1, :] = heads[row][:1]
    for i, x_ref in enumerate(x_refs):
        x = x_ref[...].astype(f32)
        a1_ref[i * tok : (i + 1) * tok, :] = rms_scale(x, gains_ref[0:1, :]).astype(bf16)
    outs = []
    for j in range(3):
        acc = None
        for q in range(n_fsdp):
            part = mm(
                a1_ref[:, at_block(jnp.bitwise_xor(f, q), norm_rows)],
                w_refs[q][j * norm_rows : (j + 1) * norm_rows, :],
            )
            acc = part if acc is None else acc + part
        if j == 0:
            qp_ref[...] = acc
        elif j == 1:
            kp_ref[...] = acc
        else:
            v_ref[...] = acc.astype(bf16)
    cosine, sine = cos_ref[...], sin_ref[...]
    for h in range(width // head_dim):
        cols = slice(h * head_dim, (h + 1) * head_dim)
        for from_ref, to_ref, row in ((qp_ref, q_ref, 0), (kp_ref, k_ref, 1)):
            normed = rms_scale(from_ref[:, cols], heads_ref[row : row + 1, :])
            to_ref[:, cols] = rope(normed, cosine, sine).astype(bf16)

        def block(rows, _):
            logits = mm(q_ref[rows, cols], k_ref[:, cols], NT) * head_dim**-0.5
            logits = jnp.where(dq_ref[rows, :] == dk_ref[...], logits, NEG_FILL)
            weights = jnp.exp(logits - jnp.max(logits, axis=1, keepdims=True))
            probs = weights * (1.0 / jnp.sum(weights, axis=1, keepdims=True))
            o_ref[rows, cols] = mm(probs.astype(bf16), v_ref[:, cols]).astype(bf16)
            return 0

        over_blocks(block, 0, length, q_rows)


def attend_back_kernel(sizes, *refs):
    n_ctx, head_dim, q_rows = sizes
    g_refs, refs = refs[:n_ctx], refs[n_ctx:]
    out_ref, q_ref, k_ref, v_ref, qp_ref, kp_ref, cos_ref, sin_ref, dq_ref, dk_ref, heads_ref = refs[:11]
    d_ref, hg_ref, go_ref = refs[11:]
    tok = g_refs[0].shape[0]
    length, width = q_ref.shape
    scale = head_dim**-0.5
    for i, g_ref in enumerate(g_refs):
        go_ref[i * tok : (i + 1) * tok, :] = mm(g_ref[...], out_ref[...], NT).astype(bf16)
    cosine, sine = cos_ref[...], sin_ref[...]
    sums = [None, None]
    for h in range(width // head_dim):
        cols = slice(h * head_dim, (h + 1) * head_dim)
        key, value = k_ref[:, cols], v_ref[:, cols]

        def block(rows, sums_of):
            d_key, d_value = sums_of
            query, d_out = q_ref[rows, cols], go_ref[rows, cols]
            logits = mm(query, key, NT) * scale
            logits = jnp.where(dq_ref[rows, :] == dk_ref[...], logits, NEG_FILL)
            weights = jnp.exp(logits - jnp.max(logits, axis=1, keepdims=True))
            probs = weights * (1.0 / jnp.sum(weights, axis=1, keepdims=True))
            d_prob = mm(d_out, value, NT)
            delta = jnp.sum(probs * d_prob, axis=1, keepdims=True)
            d_logit = (probs * (d_prob - delta)).astype(bf16)
            d_ref[0, rows, cols] = (mm(d_logit, key) * scale).astype(bf16)
            return (
                d_key + mm(d_logit, query, TN),
                d_value + mm(probs.astype(bf16), d_out, TN),
            )

        zeros = jnp.zeros((length, head_dim), f32)
        d_key, d_value = over_blocks(block, (zeros, zeros), length, q_rows)
        d_query = d_ref[0, :, cols].astype(f32)
        d_ref[2, :, cols] = d_value.astype(bf16)
        for row, grads, proj_ref in ((0, d_query, qp_ref), (1, d_key * scale, kp_ref)):
            grads = rope_back(grads.astype(bf16).astype(f32), cosine, sine)
            values = proj_ref[:, cols]
            root = lax.rsqrt(jnp.mean(values * values, axis=1, keepdims=True) + EPS)
            normed = values * root
            part = jnp.sum(grads * normed, axis=0, keepdims=True)
            sums[row] = part if sums[row] is None else sums[row] + part
            grads = grads * heads_ref[row : row + 1, :]
            inner = jnp.mean(grads * normed, axis=1, keepdims=True)
            d_ref[row, :, cols] = (root * (grads - normed * inner)).astype(bf16)
    for row in range(2):
        hg_ref[row : row + 1, :] = sums[row]


def project_back_kernel(sizes, f_ref, *refs):
    n_ctx, n_fsdp, head_rows, norm_rows = sizes
    x_refs, refs = refs[:n_ctx], refs[n_ctx:]
    w_refs, refs = refs[:n_fsdp], refs[n_fsdp:]
    a1_ref, d_ref, hg_ref, gain_two_ref = refs[:4]
    pay_refs, (da_ref, root_ref, extra_ref) = refs[4:-3], refs[-3:]
    pay_a, pay_b = pay_refs[:2], pay_refs[2:]
    f = f_ref[0]
    tok = x_refs[0].shape[0]
    width = d_ref.shape[2]
    for i, x_ref in enumerate(x_refs):
        x = x_ref[...].astype(f32)
        root_ref[i * tok : (i + 1) * tok, :] = lax.rsqrt(jnp.mean(x * x, axis=1, keepdims=True) + EPS)
    for q in range(n_fsdp):
        block = jnp.bitwise_xor(f, q)
        spot = at_block(block, norm_rows)
        flipped = a1_ref[:, spot].astype(f32).T.astype(bf16)
        da = None
        for j in range(3):
            rows = slice(j * norm_rows, (j + 1) * norm_rows)
            part = mm(d_ref[j], w_refs[q][rows, :], NT)
            da = part if da is None else da + part
            grad = mm(flipped, d_ref[j]).astype(bf16)
            if j == 2:
                pay_b[q // 2][q % 2, :norm_rows, :] = grad
            else:
                pay_a[q % 2][q // 2, rows, :] = grad
        da_ref[:, spot] = da.astype(bf16)
        gain = None
        for i, x_ref in enumerate(x_refs):
            rows = slice(i * tok, (i + 1) * tok)
            part = x_ref[:, spot].astype(f32) * root_ref[rows, :] * da[rows]
            part = jnp.sum(part, axis=0, keepdims=True)
            gain = part if gain is None else gain + part
        extra_ref[...] = jnp.zeros(extra_ref.shape, f32)
        for k in range(norm_rows // LANES):
            lanes = slice(k * LANES, (k + 1) * LANES)
            row, lane = k * LANES // width, k * LANES % width
            extra_ref[row : row + 1, lane : lane + LANES] = gain[:, lanes]
            two = norm_rows + k * LANES
            row, lane = two // width, two % width
            spot_two = pl.ds(pl.multiple_of(block * norm_rows + k * LANES, LANES), LANES)
            extra_ref[row : row + 1, lane : lane + LANES] = gain_two_ref[0:1, spot_two]
        for r in range(2):
            flat = 2 * norm_rows + r * LANES
            row, lane = flat // width, flat % width
            turned = jnp.broadcast_to(hg_ref[r : r + 1, :], (8, LANES))
            turned = pltpu.roll(turned, (n_fsdp - block) * head_rows, 1)
            extra_ref[row : row + 1, lane : lane + LANES] = turned[:1]
        pay_b[q // 2][q % 2, norm_rows:, :] = extra_ref[...].astype(bf16)


def finish_kernel(sizes, c_ref, *refs):
    n_ctx, norm_rows = sizes
    pay_refs, out_refs = refs[:n_ctx], refs[n_ctx : 2 * n_ctx]
    qkv_ref, out_ref = refs[2 * n_ctx :]
    c = c_ref[0]
    width = pay_refs[0].shape[1]
    piece_rows = out_refs[0].shape[0]
    for q in range(n_ctx):
        block = jnp.bitwise_xor(c, q)
        for j in range(3):
            rows = slice(j * norm_rows, (j + 1) * norm_rows)
            qkv_ref[j, :, at_block(block, width)] = pay_refs[q][rows, :].astype(f32)
        spot = pl.ds(pl.multiple_of(block * piece_rows, piece_rows), piece_rows)
        out_ref[spot, :] = out_refs[q][...].astype(f32)


def dispatch_kernel(picks_ref, scale_ref, *refs):
    piece_refs, dy_ref, all_ref = refs[:-2], refs[-2], refs[-1]
    tok = piece_refs[0].shape[0]

    @pl.when(pl.program_id(0) == 0)
    def _():
        for q, piece_ref in enumerate(piece_refs):
            all_ref[q * tok : (q + 1) * tok, :] = piece_ref[...]

    dy_ref[0] = (mm(picks_ref[0], all_ref[...]) * scale_ref[0]).astype(bf16)


def hidden_kernel(picks_ref, dy_ref, wg_ref, wu_ref, wd_ref, *refs):
    piece_refs, (rows_ref, hid_ref, dg_ref, du_ref, all_ref) = refs[:-5], refs[-5:]
    tok = piece_refs[0].shape[0]
    first = pl.program_id(1) == 0

    @pl.when(first & (pl.program_id(0) == 0))
    def _():
        for q, piece_ref in enumerate(piece_refs):
            all_ref[q * tok : (q + 1) * tok, :] = piece_ref[...]

    @pl.when(first)
    def _():
        rows_ref[0] = mm(picks_ref[0], all_ref[...]).astype(bf16)

    rows = rows_ref[0]
    gate = mm(rows, wg_ref[0])
    up = mm(rows, wu_ref[0])
    d_hid = mm(dy_ref[0], wd_ref[0])
    sig = 1.0 / (1.0 + jnp.exp(-gate))
    act = gate * sig
    hid_ref[0] = (act * up).astype(bf16)
    dg_ref[0] = (d_hid * up * sig * (1.0 + gate * (1.0 - sig))).astype(bf16)
    du_ref[0] = (d_hid * act).astype(bf16)


def body(
    inputs,
    doc_starts,
    routes,
    gate_weights,
    qkv_w,
    out_w,
    norm_gains,
    head_gains,
    gate_up,
    down_t,
    cotangent,
):
    n_ctx, n_fsdp = lax.axis_size("ctx"), lax.axis_size("fsdp")
    c, f = lax.axis_index("ctx"), lax.axis_index("fsdp")
    c_at, f_at = c.astype(jnp.int32).reshape(1), f.astype(jnp.int32).reshape(1)
    tok_rows, model_width = inputs.shape[1:]
    norm_rows, head_rows = norm_gains.shape[0], head_gains.shape[0]
    head_dim = head_rows * n_fsdp
    own_width = model_width // n_ctx
    top_count = routes.shape[2]
    hidden_units = down_t.shape[2]
    local_experts = gate_up.shape[1]
    experts_all = local_experts * n_fsdp
    capacity = tok_rows * top_count * 5 // (experts_all * 4)
    slots = -(-n_fsdp * capacity // 16) * 16
    stream_len = doc_starts.shape[1]
    q_rows = min(512, stream_len)
    half_dim = head_dim // 2
    tokens = n_fsdp * tok_rows
    order = folded_order(n_ctx)

    x_low = inputs[0]
    x_rows = x_low.astype(f32)
    cot_low = cotangent[0]
    cot_rows = cot_low.astype(f32)

    weights = gate_weights[0].T.reshape(-1)
    high = lax.reduce_precision(weights, 8, 7)
    middle = lax.reduce_precision(weights - high, 8, 7)
    gap = jnp.zeros((LANES - head_rows,), bf16)
    small = jnp.concatenate(
        [
            norm_gains.T.reshape(-1),
            head_gains[:, 0],
            gap,
            head_gains[:, 1],
            gap,
            routes[0].T.reshape(-1).astype(bf16),
            high.astype(bf16),
            middle.astype(bf16),
            (weights - high - middle).astype(bf16),
        ]
    )
    extra_rows = -(-small.shape[0] // (16 * own_width)) * 16
    small = jnp.pad(small, (0, extra_rows * own_width - small.shape[0]))
    qkv_own = lax.dynamic_slice_in_dim(qkv_w, c * own_width, own_width, axis=2)
    qkv_own = qkv_own.transpose(1, 0, 2).reshape(3 * norm_rows, own_width)
    qkv_own = jnp.concatenate([qkv_own, small.reshape(extra_rows, own_width)], axis=0)
    qkv_pieces = gather_fsdp(qkv_own)

    x_pieces = gather_ctx(x_low)
    x_pieces = [x_pieces[q] for q in order]

    units = n_ctx * n_fsdp
    out_rows = out_w.shape[0] // n_ctx
    flat = lambda ci, fi: ci * n_fsdp + fi
    to_heads = [(flat(u % n_ctx, u // n_ctx), flat(u // n_fsdp, u % n_fsdp)) for u in range(units)]
    out_piece = lax.dynamic_slice_in_dim(out_w, c * out_rows, out_rows, axis=0)
    out_piece = lax.ppermute(after(out_piece, *x_pieces), ("ctx", "fsdp"), to_heads)
    split = model_width * 11 // (16 * LANES) * LANES
    out_far = gather_far(after(out_piece, qkv_pieces[-1]))
    out_pieces = gather_near(out_far)

    cot_far = gather_far(after(cot_low, *out_far))
    gate_up_all = lax.all_gather(gate_up.transpose(1, 0, 2), "ctx", axis=1, tiled=True)
    down_all = lax.all_gather(
        down_t.transpose(1, 0, 2), "ctx", axis=1, tiled=True
    )

    places = jnp.arange(stream_len, dtype=jnp.int32)
    blocks = jnp.repeat(jnp.asarray(order, jnp.int32), tok_rows)
    spots = (c ^ blocks) * tok_rows + places % tok_rows
    starts = doc_starts[0]
    reach = spots[:, None] >= places[None, :]
    doc_ids = jnp.sum(jnp.where(reach, starts[None, :], 0), axis=1)
    begins = jnp.max(jnp.where(reach & (starts[None, :] == 1), places[None, :], 0), axis=1)
    relative = spots - begins
    frequency = jnp.exp(jnp.arange(half_dim, dtype=f32) * (-2.0 / head_dim) * math.log(ROPE_BASE))
    angles = relative.astype(f32)[:, None] * frequency[None, :]
    cosine = jnp.cos(angles)
    cosine = jnp.concatenate([cosine, cosine], axis=1)
    sine = jnp.sin(angles)
    sine = jnp.concatenate([-sine, sine], axis=1)
    doc_q, doc_k = doc_ids[:, None], doc_ids[None, :]

    act = jax.ShapeDtypeStruct((stream_len, own_width), bf16)
    wide = jax.ShapeDtypeStruct((stream_len, own_width), f32)
    a1, q_proj, k_proj, q_low, k_low, v_low, attn_low, gains, heads = pl.pallas_call(
        functools.partial(
            attend_kernel, (n_ctx, n_fsdp, head_dim, head_rows, norm_rows, q_rows)
        ),
        in_specs=[SMEM] + [VMEM] * (n_ctx + n_fsdp + 4),
        out_specs=[VMEM] * 9,
        out_shape=[
            jax.ShapeDtypeStruct((stream_len, model_width), bf16),
            wide,
            wide,
            act,
            act,
            act,
            act,
            jax.ShapeDtypeStruct((2, model_width), f32),
            jax.ShapeDtypeStruct((2, head_dim), f32),
        ],
        compiler_params=params(48),
        cost_estimate=cost(1),
        name="attend",
    )(f_at, *x_pieces, *qkv_pieces, cosine, sine, doc_q, doc_k)
    out_own, mixed_heads = pl.pallas_call(
        out_kernel,
        in_specs=[SMEM] + [VMEM] * (n_fsdp + 1),
        out_specs=[VMEM] * 2,
        out_shape=[
            jax.ShapeDtypeStruct((own_width, model_width), bf16),
            jax.ShapeDtypeStruct((stream_len, model_width), bf16),
        ],
        compiler_params=params(40),
        cost_estimate=cost(1),
        name="out",
    )(f_at, attn_low, *out_pieces)
    h_one = x_rows + scatter_ctx(mixed_heads.reshape(n_ctx, tok_rows, model_width))
    a2_f32, norm_two_back = jax.vjp(rms_scale, h_one, gains[1])
    a2_low = a2_f32.astype(bf16)
    a2_pieces = gather_fsdp(a2_low)
    cot_pieces = gather_near([after(piece, a2_low) for piece in cot_far])

    extras = jnp.stack([piece[3 * norm_rows :].reshape(-1) for piece in qkv_pieces]).astype(f32)
    route_at = 2 * norm_rows + 2 * LANES
    count = tok_rows * top_count
    spread = extras[:, route_at : route_at + 4 * count].reshape(n_fsdp, 4, top_count, tok_rows)
    spread = spread.transpose(1, 2, 0, 3).reshape(4, top_count, tokens)
    own = (f * local_experts + jnp.arange(local_experts, dtype=jnp.int32)).astype(f32)
    chosen = spread[0][None] == own[:, None, None]
    token_weight = spread[1] + spread[2] + spread[3]
    member = jnp.any(chosen, axis=1)
    weight = jnp.sum(jnp.where(chosen, token_weight[None], 0.0), axis=1)
    token_ids = jnp.arange(tokens, dtype=jnp.int32)
    before = (token_ids[:, None] < token_ids[None, :]).astype(bf16)
    rank = mm(member.astype(bf16), before).astype(jnp.int32)
    place = jnp.where(member, rank, -1)
    slot_ids = jnp.arange(slots, dtype=jnp.int32)
    picks = place[:, None, :] == slot_ids[None, :, None]
    scale = jnp.sum(jnp.where(picks, weight[:, None, :], 0.0), axis=2, keepdims=True)
    picks = picks.astype(bf16)
    tile = 512
    per_expert = lambda *shape: pl.BlockSpec((1,) + shape, lambda e, j: (e, 0, 0))
    whole = lambda *shape: pl.BlockSpec(shape, lambda *_: (0,) * len(shape))
    column = lambda rows_of, shift: pl.BlockSpec((1, rows_of, tile), lambda e, j: (e, 0, j + shift))
    piece_specs = [whole(tok_rows, model_width)] * n_fsdp
    row_shape = jax.ShapeDtypeStruct((local_experts, slots, model_width), bf16)
    gathered = [pltpu.VMEM((tokens, model_width), bf16)]
    dy = pl.pallas_call(
        dispatch_kernel,
        grid=(local_experts,),
        in_specs=[
            pl.BlockSpec((1, slots, tokens), lambda e: (e, 0, 0)),
            pl.BlockSpec((1, slots, 1), lambda e: (e, 0, 0)),
        ]
        + piece_specs,
        out_specs=pl.BlockSpec((1, slots, model_width), lambda e: (e, 0, 0)),
        out_shape=row_shape,
        scratch_shapes=gathered,
        compiler_params=params(40),
        cost_estimate=cost(5),
        name="dispatch",
    )(picks, scale, *cot_pieces)
    hid_shape = jax.ShapeDtypeStruct((local_experts, slots, hidden_units), bf16)
    rows, hidden_low, gate_grad, up_grad = pl.pallas_call(
        hidden_kernel,
        grid=(local_experts, hidden_units // tile),
        in_specs=[
            per_expert(slots, tokens),
            per_expert(slots, model_width),
            column(model_width, 0),
            column(model_width, hidden_units // tile),
            column(model_width, 0),
        ]
        + piece_specs,
        out_specs=[per_expert(slots, model_width)] + [column(slots, 0)] * 3,
        out_shape=[
            row_shape,
            hid_shape,
            hid_shape,
            hid_shape,
        ],
        scratch_shapes=gathered,
        compiler_params=params(48),
        cost_estimate=cost(20),
        name="hidden",
    )(picks, dy, gate_up_all, gate_up_all, down_all, *a2_pieces)

    pair_grad = jnp.concatenate([gate_grad, up_grad], axis=2)

    token_blocks = lambda values: split_blocks(values.reshape(n_fsdp, tok_rows, model_width), split)
    dxe = jnp.einsum("erk,edk->erd", pair_grad, gate_up_all, preferred_element_type=f32).astype(bf16)
    grads_back = jnp.einsum("est,esd->td", picks, dxe, preferred_element_type=f32).astype(bf16)
    dx_first = scatter_first(*token_blocks(grads_back))
    down_part = jnp.einsum(
        "erd,erf->edf", after(dy, grads_back), hidden_low, preferred_element_type=f32
    ).astype(bf16)
    down_grad = lax.psum_scatter(down_part, "ctx", scatter_dimension=1, tiled=True).astype(f32)
    pair_part = jnp.einsum(
        "erd,erk->edk", after(rows, grads_back), pair_grad, preferred_element_type=f32
    ).astype(bf16)
    gate_up_grad = lax.psum_scatter(pair_part, "ctx", scatter_dimension=1, tiled=True).astype(f32)
    da2 = jnp.concatenate(scatter_second(dx_first, pair_part), axis=1)
    made = jnp.einsum(
        "erf,edf->erd", after(hidden_low, grads_back), down_all, preferred_element_type=f32
    )
    made = (scale * made.astype(bf16).astype(f32)).astype(bf16)
    mixed = jnp.einsum("est,esd->td", picks, made, preferred_element_type=f32).astype(bf16)
    mixed_first = scatter_first(*token_blocks(mixed))

    dh_part, gain_two_grad = norm_two_back(da2)
    dh_one = cot_rows + dh_part
    dattn_pieces = gather_ctx(dh_one.astype(bf16))
    dattn_pieces = [dattn_pieces[q] for q in order]
    proj_grad, head_grads = pl.pallas_call(
        functools.partial(attend_back_kernel, (n_ctx, head_dim, q_rows)),
        in_specs=[VMEM] * (n_ctx + 11),
        out_specs=[VMEM] * 2,
        out_shape=[
            jax.ShapeDtypeStruct((3, stream_len, own_width), bf16),
            jax.ShapeDtypeStruct((2, head_dim), f32),
        ],
        scratch_shapes=[pltpu.VMEM((stream_len, own_width), bf16)],
        compiler_params=params(56),
        cost_estimate=cost(500),
        name="attend_back",
    )(*dattn_pieces, out_own, after(q_low, *mixed_first[0], *mixed_first[1:]), k_low, v_low, q_proj, k_proj, cosine, sine, doc_q, doc_k, heads)
    dattn = jnp.concatenate(dattn_pieces, axis=0)
    out_part = mm(attn_low, dattn, TN).astype(bf16)
    out_blocks = jnp.stack(
        [
            lax.dynamic_slice_in_dim(out_part, (f ^ q) * out_rows, out_rows, axis=0)
            for q in range(n_fsdp)
        ]
    )
    out_first_sums = scatter_first(*split_blocks(out_blocks, split))
    out_parts = scatter_second(out_first_sums, proj_grad)
    out_sum = jnp.concatenate(out_parts, axis=1)
    half_stack = jax.ShapeDtypeStruct((n_fsdp // 2, 2 * norm_rows, own_width), bf16)
    pair_shape = jax.ShapeDtypeStruct((2, norm_rows + extra_rows, own_width), bf16)
    even_a, odd_a, *pairs_b, da1 = pl.pallas_call(
        functools.partial(project_back_kernel, (n_ctx, n_fsdp, head_rows, norm_rows)),
        in_specs=[SMEM] + [VMEM] * (n_ctx + n_fsdp + 4),
        out_specs=[VMEM] * (n_fsdp // 2 + 3),
        out_shape=[half_stack] * 2
        + [pair_shape] * (n_fsdp // 2)
        + [jax.ShapeDtypeStruct((stream_len, model_width), bf16)],
        scratch_shapes=[
            pltpu.VMEM((stream_len, 1), f32),
            pltpu.VMEM((extra_rows, own_width), f32),
        ],
        compiler_params=params(56),
        cost_estimate=cost(500),
        name="project_back",
    )(f_at, *x_pieces, *qkv_pieces, a1, after(proj_grad, *out_first_sums[0], out_first_sums[2]), head_grads, gain_two_grad[None])
    payload_first = scatter_first(even_a, odd_a, pairs_b)
    da1 = scatter_ctx(da1.reshape(n_ctx, tok_rows, model_width))
    out_sum = lax.ppermute(out_sum.astype(bf16), ("ctx", "fsdp"), [(b, a) for a, b in to_heads])
    out_ends = gather_ctx(out_sum)
    payload_parts = scatter_second(payload_first, *out_parts, da1, down_grad)
    qkv_sum = jnp.concatenate(payload_parts, axis=0)
    _, norm_one_back = jax.vjp(lambda x: rms_scale(x, gains[0]), x_rows)
    inputs_grad = dh_one + norm_one_back(da1)[0]
    mixed_parts = scatter_second(mixed_first, *payload_parts)
    ends = gather_ctx(qkv_sum.astype(bf16))
    qkv_grad, out_grad = pl.pallas_call(
        functools.partial(finish_kernel, (n_ctx, norm_rows)),
        in_specs=[SMEM] + [VMEM] * (2 * n_ctx),
        out_specs=[VMEM] * 2,
        out_shape=[
            jax.ShapeDtypeStruct((3, norm_rows, model_width), f32),
            jax.ShapeDtypeStruct((norm_rows, model_width), f32),
        ],
        compiler_params=params(40),
        cost_estimate=cost(1),
        name="finish",
    )(c_at, *ends, *out_ends)
    gate_up_grad = after(gate_up_grad, out_grad)
    h_one = after(h_one, out_grad, gate_up_grad)
    block_out = (h_one + jnp.concatenate(mixed_parts, axis=1)).astype(bf16)
    extras = sum(piece[3 * norm_rows :].astype(f32) for piece in ends).reshape(-1)
    norm_grad = extras[: 2 * norm_rows].reshape(2, norm_rows).T
    head_grad = extras[2 * norm_rows : route_at].reshape(2, LANES)[:, :head_rows].T
    return (
        block_out[None],
        inputs_grad[None],
        qkv_grad.transpose(1, 0, 2),
        out_grad,
        norm_grad,
        head_grad,
        gate_up_grad.transpose(1, 0, 2),
        down_grad.transpose(1, 0, 2),
    )


def solution(mesh):
    return jax.shard_map(
        body,
        mesh=mesh,
        in_specs=(
            P("fsdp", "ctx", None),
            P("fsdp", None),
            P("fsdp", "ctx", None),
            P("fsdp", "ctx", None),
            P("fsdp", None, None),
            P("fsdp", None),
            P("fsdp", None),
            P("fsdp", None),
            P("ctx", "fsdp", None),
            P("ctx", "fsdp", None),
            P("fsdp", "ctx", None),
        ),
        out_specs=(
            P("fsdp", "ctx", None),
            P("fsdp", "ctx", None),
            P("fsdp", None, None),
            P("fsdp", None),
            P("fsdp", None),
            P("fsdp", None),
            P("ctx", "fsdp", None),
            P("ctx", "fsdp", None),
        ),
        check_vma=False,
    )
```

time: 821 us -> 737 us (0.90)
  matrix products: 169 us -> 79.9 us
  Pallas kernels: 10.1 us -> 94.6 us
  starting transfers between devices: 210 us -> 175 us
  waiting for transfers between devices: 291 us -> 266 us
  other arithmetic: 67.7 us -> 47.4 us
    dot_general x20 -> x5, matrix products: 138 us -> 50.3 us  [the longest x1 21.4 us: body(): jnp.einsum('erd,erk->edk', after(rows, grads_back), pair_grad, preferred_...]
    pallas_call x2 -> x7, Pallas kernels: 10.1 us -> 94.6 us  [the longest x1 33.3 us: body(): pl.pallas_call(hidden_kernel, grid=(local_experts, hidden_units // tile),...]
    ppermute x86 -> x76, starting transfers between devices: 207 us -> 173 us  [swap(): return lax.ppermute(value, axis, [(i, i ^ mask) for i in range(size)])]
    ppermute x86 -> x76, waiting for transfers between devices: 289 us -> 265 us  [swap(): return lax.ppermute(value, axis, [(i, i ^ mask) for i in range(size)])]
    add x7 -> x15, other arithmetic: 1.28 us -> 14.2 us  [the longest x4 6.07 us: scatter_second(): total_a + swap(after(sums_a[i + 1], *others), 'fsdp', m).astype(f32)]
    dynamic_update_slice x8 -> x0, other arithmetic: 10.2 us -> none  [the longest x4 6.9 us: body(): lax.dynamic_update_slice_in_dim(qkv_grad, piece.astype(f32), (c ^ q) * ow...]
    squeeze x0 -> x7, local copies, waits for them, and re-layouts: none -> 10.1 us  [the longest x3 5.05 us: split_blocks(): parts_b = [pairs[i, :, :, size:] for i in range(pairs.shape[0])]]
    transpose x1, other arithmetic: 9.23 us -> 0.01 us  [body(): spread = spread.transpose(1, 2, 0, 3).reshape(4, top_count, tokens)]
  transfers between devices with their start and end apart: 92 -> 82, of which waited for: 32 -> 21; matrix products, arithmetic and copies ran while one was open for 28% -> 14% of each run, Pallas kernels for 1% -> 8%
where the time goes in v3:
time: 737 us; the launch traced here: 729 us
  waiting for transfers between devices  266 us (36%)
  starting transfers between devices  175 us (24%)
  Pallas kernels  94.6 us (13%)
  matrix products  79.9 us (11%)
  local copies, waits for them, and re-layouts  49.3 us (7%)
  other arithmetic  47.4 us (6%)
  between operations  15.5 us (2%)
    ppermute x76, waiting for transfers between devices, swap(): return lax.ppermute(value, axis, [(i, i ^ mask) for i in range(size)])  265 us
    ppermute x76, starting transfers between devices, swap(): return lax.ppermute(value, axis, [(i, i ^ mask) for i in range(size)])  173 us
    pallas_call x1, Pallas kernels, body(): pl.pallas_call(hidden_kernel, grid=(local_experts, hidden_units // tile),...  33.3 us
    unnamed x221, local copies, waits for them, and re-layouts  28.9 us
    dot_general x1, matrix products, body(): jnp.einsum('erd,erk->edk', after(rows, grads_back), pair_grad, preferred_...  21.4 us
    pallas_call x1, Pallas kernels, body(): pl.pallas_call(functools.partial(attend_back_kernel, (n_ctx, head_dim, q_...  18.6 us
    dot_general x1, matrix products, body(): jnp.einsum('erk,edk->erd', pair_grad, gate_up_all, preferred_element_type...  18.4 us
    dot_general x1, matrix products, body(): jnp.einsum('est,esd->td', picks, made, preferred_element_type=f32)  17.5 us
  transfers between devices with their start and end apart: 82, of which 21 were waited for; matrix products, arithmetic and copies ran while one was open for 14% of the time, Pallas kernels for 8%

profile of v3, /device:TPU:0, one launch (start us, length us, event | category | flops | bytes accessed | tf_op | source)
XLA Modules:
  0.0 728.6 jit_solution(7501311456472136096)
XLA Ops:
  17.3 15.8 %collective-permute-done.refs_1_ = bf16[128,2048]{1,0:T(8,128)(2,1)S(1)} collective-permute-done((bf16[128,2048]{1,0:T(8,128)(2,1)S(1)}, bf16[128,2048]{1,0:T(8,128)(2,1)S(1)}, u32[]{:S(2)}, u32[]{:S(2)}) %collective-permute-start) | collective-permute-done | bytes 524320 | tf_op jit(solution)/shard_map/ppermute | solution.py:46
  37.0 13.7 %collective-permute-done.4.refs_6_ = bf16[784,512]{1,0:T(8,128)(2,1)} collective-permute-done((bf16[784,512]{1,0:T(8,128)(2,1)S(1)}, bf16[784,512]{1,0:T(8,128)(2,1)}, u32[]{:S(2)}, u32[]{:S(2)}) %collective-permute-start.4) | collective-permute-done | bytes 802848 | tf_op jit(solution)/shard_map/ppermute | solution.py:46
  52.1 31.0 %collective-permute-done.6.refs_8_ = bf16[784,512]{1,0:T(8,128)(2,1)} collective-permute-done((bf16[784,512]{1,0:T(8,128)(2,1)S(1)}, bf16[784,512]{1,0:T(8,128)(2,1)}, u32[]{:S(2)}, u32[]{:S(2)}) %collective-permute-start.6) | collective-permute-done | bytes 802848 | tf_op jit(solution)/shard_map/ppermute | solution.py:46
  90.7 14.7 %collective-permute-start.12 = (bf16[64,2048]{1,0:T(8,128)(2,1)S(1)}, bf16[64,2048]{1,0:T(8,128)(2,1)}, u32[]{:S(2)}, u32[]{:S(2)}) collective-permute-start(bf16[64,2048]{1,0:T(8,128)(2,1)S(1)} %collective-permute-done.10.refs_0_), channel_id=1, source_target_pairs={{0,2},{1,3},{2,0},{3,1},{4,6},{5,7},{6,4},{7,5},{8,10},{9,11},{10,... | collective-permute-start | bytes 786440 | tf_op jit(solution)/shard_map/ppermute | solution.py:46
  118.0 8.2 %collective-permute-done.14.refs_4_ = bf16[64,2048]{1,0:T(8,128)(2,1)} collective-permute-done((bf16[64,2048]{1,0:T(8,128)(2,1)S(1)}, bf16[64,2048]{1,0:T(8,128)(2,1)}, u32[]{:S(2)}, u32[]{:S(2)}) %collective-permute-start.14) | collective-permute-done | bytes 262176 | tf_op jit(solution)/shard_map/ppermute | solution.py:46
  132.3 11.9 %attend.1 = (bf16[512,2048]{1,0:T(8,128)(2,1)}, f32[512,512]{1,0:T(8,128)}, f32[512,512]{1,0:T(8,128)}, bf16[512,512]{1,0:T(8,128)(2,1)S(1)}, bf16[512,512]{1,0:...) custom-call(s32[1]{0:T(128)} %bitcast.1.f_ref, ...), custom_call_target="tpu_custom_call" | custom-call | flops 1000000000 | tf_op jit(solution)/shard_map/attend/pallas_call | solution.py:470
  162.0 18.3 %collective-permute-done.19 = bf16[1,128,2048]{2,1,0:T(8,128)(2,1)S(1)} collective-permute-done((bf16[1,128,2048]{2,1,0:T(8,128)(2,1)S(1)}, bf16[1,128,2048]{2,1,0:T(8,128)(2,1)S(1)}, u32[]{:S(2)}, u32[]{:S(2)}) %collective-permute-start.19) | collective-permute-done | bytes 524320 | tf_op jit(solution)/shard_map/ppermute | solution.py:46
  183.6 22.9 %collective-permute-done.23.refs_4_ = bf16[128,2048]{1,0:T(8,128)(2,1)S(1)} collective-permute-done((bf16[128,2048]{1,0:T(8,128)(2,1)}, bf16[128,2048]{1,0:T(8,128)(2,1)S(1)}, u32[]{:S(2)}, u32[]{:S(2)}) %collective-permute-start.23) | collective-permute-done | bytes 524320 | tf_op jit(solution)/shard_map/ppermute | solution.py:46
  224.0 8.5 %collective-permute-done.22.refs_3_ = bf16[128,2048]{1,0:T(8,128)(2,1)S(1)} collective-permute-done((bf16[128,2048]{1,0:T(8,128)(2,1)S(1)}, bf16[128,2048]{1,0:T(8,128)(2,1)S(1)}, u32[]{:S(2)}, u32[]{:S(2)}) %collective-permute-start.22) | collective-permute-done | bytes 524320 | tf_op jit(solution)/shard_map/ppermute | solution.py:46
  235.4 10.4 %collective-permute-done.30.refs_4_ = bf16[128,2048]{1,0:T(8,128)(2,1)} collective-permute-done((bf16[128,2048]{1,0:T(8,128)(2,1)S(1)}, bf16[128,2048]{1,0:T(8,128)(2,1)}, u32[]{:S(2)}, u32[]{:S(2)}) %collective-permute-start.30) | collective-permute-done | bytes 524320 | tf_op jit(solution)/shard_map/ppermute | solution.py:46
  266.9 10.7 %collective-permute-done.31.refs_5_ = bf16[128,2048]{1,0:T(8,128)(2,1)} collective-permute-done((bf16[128,2048]{1,0:T(8,128)(2,1)}, bf16[128,2048]{1,0:T(8,128)(2,1)}, u32[]{:S(2)}, u32[]{:S(2)}) %collective-permute-start.31) | collective-permute-done | bytes 524320 | tf_op jit(solution)/shard_map/ppermute | solution.py:46
  277.6 10.3 %collective-permute-done.33.refs_7_ = bf16[128,2048]{1,0:T(8,128)(2,1)} collective-permute-done((bf16[128,2048]{1,0:T(8,128)(2,1)}, bf16[128,2048]{1,0:T(8,128)(2,1)}, u32[]{:S(2)}, u32[]{:S(2)}) %collective-permute-start.33) | collective-permute-done | bytes 524320 | tf_op jit(solution)/shard_map/ppermute | solution.py:46
  287.9 33.3 %hidden.1 = (bf16[3,432,2048]{2,1,0:T(8,128)(2,1)}, bf16[3,432,1024]{2,1,0:T(8,128)(2,1)}, bf16[3,432,1024]{2,1,0:T(8,128)(2,1)}, bf16[3,432,1024]{2,1,0:T(8,128)(2,1)}) custom-call(bf16[3,432,1024]{2,1,0:T(8,128)(2,1)} %copy-done.2, bf16[3,432,2048]{2,1,0:T(8,128)(2,1)} %copy-done.6, bf16[3,2048,2048]{2,1,0:T(8,128)(2,1)} %all-gather.3.cloned.1.call-done.wg_ref.wu_ref, ...), custom_call_target="tpu_custom_call" | custom-call | flops 20000000000 | tf_op jit(solution)/shard_map/hidden/pallas_call | solution.py:550
  324.2 18.4 %fusion.80 = bf16[3,432,2048]{2,1,0:T(8,128)(2,1)} fusion(bf16[3,432,2048]{2,1,0:T(8,128)(2,1)S(1)} %constant_dynamic-update-slice_fusion, bf16[3,2048,2048]{2,1,0:T(8,128)(2,1)} %all-gather.3.cloned.1.call-done.wg_ref.wu_ref), kind=kOutput, calls=%fused_computation.234 | convolution fusion | flops 10871635968 | bytes 35782656 | tf_op jit(solution)/shard_map/erk,edk->erd/dot_general | solution.py:577
  342.6 11.2 %bitcast_convert_fusion.1 = bf16[1024,2048]{1,0:T(8,128)(2,1)} fusion(bf16[3,432,2048]{2,1,0:T(8,128)(2,1)} %fusion.80, s32[3,1024]{1,0:T(4,128)S(1)} %fusion.23), kind=kOutput, calls=%fused_computation.3 | convolution fusion | flops 5439242240 | bytes 9515008 | tf_op jit(solution)/shard_map/est,esd->td/dot_general | solution.py:578
  353.8 9.8 %convolution_convert_fusion.1 = bf16[3,2048,1024]{2,1,0:T(8,128)(2,1)} fusion(bf16[3,432,2048]{2,1,0:T(8,128)(2,1)S(1)} %bitcast.363, bf16[3,432,1024]{2,1,0:T(8,128)(2,1)S(1)} %copy-done.89), kind=kOutput, calls=%fused_computation.4 | convolution fusion | flops 5442109440 | bytes 20545536 | tf_op jit(solution)/shard_map/erd,erf->edf/dot_general | solution.py:580
  372.4 21.4 %convolution_convert_fusion = bf16[3,2048,2048]{2,1,0:T(8,128)(2,1)} fusion(bf16[3,432,2048]{2,1,0:T(8,128)(2,1)} %get-tuple-element.78, bf16[3,432,2048]{2,1,0:T(8,128)(2,1)} %copy-done.58), kind=kOutput, calls=%fused_computation | convolution fusion | flops 10884218880 | bytes 35782656 | tf_op jit(solution)/shard_map/erd,erk->edk/dot_general | solution.py:584
  393.9 17.5 %bitcast_convert_fusion = bf16[1024,2048]{1,0:T(8,128)(2,1)} fusion(bf16[3,432,1024]{2,1,0:T(8,128)(2,1)} %get-tuple-element.86, bf16[3,2048,1024]{2,1,0:T(8,128)(2,1)} %all-gather.5.cloned.1.call-done.wd_ref, f32[3,432]{1,0:T(4,128)S(1)} %select_reduce_fusion, s32[3,1024]{1,0:T(4,128)} %copy-done.76), kind=kOutput, calls=%fused_computation.2 | convolution fusion | flops 10885677056 | bytes 19448896 | tf_op jit(solution)/shard_map/est,esd->td/dot_general | solution.py:593
  428.0 8.0 %collective-permute-done.35 = bf16[128,1408]{1,0:T(8,128)(2,1)S(1)} collective-permute-done((bf16[128,1408]{1,0:T(8,128)(2,1)S(1)}, bf16[128,1408]{1,0:T(8,128)(2,1)S(1)}, u32[]{:S(2)}, u32[]{:S(2)}) %collective-permute-start.35) | collective-permute-done | bytes 360480 | tf_op jit(solution)/shard_map/ppermute | solution.py:46
  438.1 8.4 %collective-permute-done.36 = bf16[128,1408]{1,0:T(8,128)(2,1)S(1)} collective-permute-done((bf16[128,1408]{1,0:T(8,128)(2,1)S(1)}, bf16[128,1408]{1,0:T(8,128)(2,1)S(1)}, u32[]{:S(2)}, u32[]{:S(2)}) %collective-permute-start.36) | collective-permute-done | bytes 360480 | tf_op jit(solution)/shard_map/ppermute | solution.py:46
  452.3 23.2 %collective-permute-done.47 = bf16[2,128,640]{2,1,0:T(8,128)(2,1)} collective-permute-done((bf16[2,128,640]{2,1,0:T(8,128)(2,1)}, bf16[2,128,640]{2,1,0:T(8,128)(2,1)}, u32[]{:S(2)}, u32[]{:S(2)}) %collective-permute-start.47) | collective-permute-done | bytes 327712 | tf_op jit(solution)/shard_map/ppermute | solution.py:46
  493.1 18.6 %attend_back.1 = (bf16[3,512,512]{2,1,0:T(8,128)(2,1)}, f32[2,128]{1,0:T(2,128)}) custom-call(bf16[128,2048]{1,0:T(8,128)(2,1)} %copy-done.63, bf16[128,2048]{1,0:T(8,128)(2,1)} %copy-done.93, bf16[128,2048]{1,0:T(8,128)(2,1)} %copy-done.94, bf16[128,2048]{1,0:T(8,128)(2,1)} %copy-done.95, bf16[512,2048]{1,0:T(8,128)(2,1)} %copy-done.35, ...), custom_call_target="tpu_custom_call" | custom-call | flops 499999997952 | tf_op jit(solution)/shard_map/attend_back/pallas_call | solution.py:600
  516.5 15.1 %project_back.1 = (bf16[4,512,512]{2,1,0:T(8,128)(2,1)}, bf16[4,512,512]{2,1,0:T(8,128)(2,1)}, bf16[2,272,512]{2,1,0:T(8,128)(2,1)}, bf16[2,272,512]{2,1,0:T(8,1...) custom-call(s32[1]{0:T(128)} %bitcast.1.f_ref, ...), custom_call_target="tpu_custom_call" | custom-call | flops 499999997952 | tf_op jit(solution)/shard_map/project_back/pallas_call | solution.py:626
  545.2 8.2 %collective-permute-done.55 = bf16[64,1408]{1,0:T(8,128)(2,1)S(1)} collective-permute-done((bf16[64,1408]{1,0:T(8,128)(2,1)S(1)}, bf16[64,1408]{1,0:T(8,128)(2,1)S(1)}, u32[]{:S(2)}, u32[]{:S(2)}) %collective-permute-start.55) | collective-permute-done | bytes 180256 | tf_op jit(solution)/shard_map/ppermute | solution.py:46
  559.7 11.5 %collective-permute-done.63 = bf16[2,272,512]{2,1,0:T(8,128)(2,1)S(1)} collective-permute-done((bf16[2,272,512]{2,1,0:T(8,128)(2,1)}, bf16[2,272,512]{2,1,0:T(8,128)(2,1)S(1)}, u32[]{:S(2)}, u32[]{:S(2)}) %collective-permute-start.63) | collective-permute-done | bytes 557088 | tf_op jit(solution)/shard_map/ppermute | solution.py:46
  571.2 22.6 %collective-permute-done.64 = bf16[2,272,512]{2,1,0:T(8,128)(2,1)S(1)} collective-permute-done((bf16[2,272,512]{2,1,0:T(8,128)(2,1)S(1)}, bf16[2,272,512]{2,1,0:T(8,128)(2,1)S(1)}, u32[]{:S(2)}, u32[]{:S(2)}) %collective-permute-start.64) | collective-permute-done | bytes 557088 | tf_op jit(solution)/shard_map/ppermute | solution.py:46
  596.9 10.5 %collective-permute-start.60 = (bf16[512,512]{1,0:T(8,128)(2,1)}, bf16[512,512]{1,0:T(8,128)(2,1)S(1)}, u32[]{:S(2)}, u32[]{:S(2)}) collective-permute-start(bf16[512,512]{1,0:T(8,128)(2,1)} %get-tuple-element.104), channel_id=1, source_target_pairs={{0,2},{1,3},{2,0},{3,1},{4,6},{5,7},{6,4},{7,5},{8,10},{9,11},{10,... | collective-permute-start | bytes 1572872 | tf_op jit(solution)/shard_map/ppermute | solution.py:46
  612.3 34.5 %collective-permute-start.72 = (bf16[64,2048]{1,0:T(8,128)(2,1)S(1)}, bf16[64,2048]{1,0:T(8,128)(2,1)}, u32[]{:S(2)}, u32[]{:S(2)}) collective-permute-start(bf16[64,2048]{1,0:T(8,128)(2,1)S(1)} %collective-permute-done.70.refs_4_), channel_id=1, source_target_pairs={{0,16},{8,24},{16,0},{24,8},{1,17},{9,25},{17,1},{25,9},{2,18},{10... | collective-permute-start | bytes 786440 | tf_op jit(solution)/shard_map/ppermute | solution.py:46
  654.6 17.7 %collective-permute-start.77 = (bf16[128,640]{1,0:T(8,128)(2,1)S(1)}, bf16[128,640]{1,0:T(8,128)(2,1)S(1)}, u32[]{:S(2)}, u32[]{:S(2)}) collective-permute-start(bf16[128,640]{1,0:T(8,128)(2,1)S(1)} %copy-done.72), channel_id=1, source_target_pairs={{0,1},{1,0},{2,3},{3,2},{4,5},{5,4},{6,7},{7,6},{8,9},{9,8},{10,11... | collective-permute-start | bytes 491528 | tf_op jit(solution)/shard_map/ppermute | solution.py:46
  679.8 10.6 %collective-permute-done.68.refs_2_ = bf16[784,512]{1,0:T(8,128)(2,1)S(1)} collective-permute-done((bf16[784,512]{1,0:T(8,128)(2,1)S(1)}, bf16[784,512]{1,0:T(8,128)(2,1)S(1)}, u32[]{:S(2)}, u32[]{:S(2)}) %collective-permute-start.68) | collective-permute-done | bytes 802848 | tf_op jit(solution)/shard_map/ppermute | solution.py:46
  695.2 7.9 %collective-permute-done.75 = bf16[128,1408]{1,0:T(8,128)(2,1)S(1)} collective-permute-done((bf16[128,1408]{1,0:T(8,128)(2,1)S(1)}, bf16[128,1408]{1,0:T(8,128)(2,1)S(1)}, u32[]{:S(2)}, u32[]{:S(2)}) %collective-permute-start.75) | collective-permute-done | bytes 360480 | tf_op jit(solution)/shard_map/ppermute | solution.py:46
  711.6 9.2 %convert_element_type.635 = f32[3,512,2048]{2,1,0:T(8,128)} convert(bf16[3,512,2048]{2,1,0:T(8,128)(2,1)} %reduce-scatter.5.cloned.1.call-done) | non-fusion elementwise | flops 3145728 | bytes 18874368 | tf_op jit(solution)/shard_map/convert_element_type | solution.py:587
  (457 shorter events, 218.9 us)
Async XLA Ops:
  7.2 280.7 %all-gather.5.cloned.1.call-start = ((), (), s32[]{:S(2)}) async-start(), calls=%async_computation.3 | async-start | bytes 15728640 | tf_op jit(solution)/shard_map/all_gather | solution.py:448
  7.9 280.0 %all-gather.3.cloned.1.call-start = ((), (), s32[]{:S(2)}) async-start(), calls=%async_computation.2 | async-start | bytes 31457280 | tf_op jit(solution)/shard_map/all_gather | solution.py:447
  8.7 588.2 %reduce-scatter.3.cloned.1.call-start = ((), (), s32[]{:S(2)}) async-start(), calls=%async_computation.4 | async-start | bytes 15728640 | tf_op jit(solution)/shard_map/reduce_scatter | solution.py:583
  14.3 36.3 %collective-permute-start.4 = (bf16[784,512]{1,0:T(8,128)(2,1)S(1)}, bf16[784,512]{1,0:T(8,128)(2,1)}, u32[]{:S(2)}, u32[]{:S(2)}) collective-permute-start(bf16[784,512]{1,0:T(8,128)(2,1)S(1)} %pad_maximum_fusion.1.refs_4_), channel_id=1, source_target_pairs={{0,2},{1,3},{2,0},{3,1},{4,6},{5,7},{6,4},{7,5},{8,10},{9,11},{10,... | collective-permute-start | bytes 2408456 | tf_op jit(solution)/shard_map/ppermute | solution.py:46
  14.4 68.8 %collective-permute-start.6 = (bf16[784,512]{1,0:T(8,128)(2,1)S(1)}, bf16[784,512]{1,0:T(8,128)(2,1)}, u32[]{:S(2)}, u32[]{:S(2)}) collective-permute-start(bf16[784,512]{1,0:T(8,128)(2,1)S(1)} %pad_maximum_fusion.1.refs_4_), channel_id=1, source_target_pairs={{0,4},{1,5},{2,6},{3,7},{4,0},{5,1},{6,2},{7,3},{8,12},{9,13},{10,... | collective-permute-start | bytes 2408456 | tf_op jit(solution)/shard_map/ppermute | solution.py:46
  33.1 72.3 %collective-permute-start.3 = (bf16[784,512]{1,0:T(8,128)(2,1)S(1)}, bf16[784,512]{1,0:T(8,128)(2,1)}, u32[]{:S(2)}, u32[]{:S(2)}) collective-permute-start(bf16[784,512]{1,0:T(8,128)(2,1)S(1)} %pad_maximum_fusion.1.refs_4_), channel_id=1, source_target_pairs={{0,1},{1,0},{2,3},{3,2},{4,5},{5,4},{6,7},{7,6},{8,9},{9,8},{10,11... | collective-permute-start | bytes 2408456 | tf_op jit(solution)/shard_map/ppermute | solution.py:46
  34.5 50.1 %collective-permute-start.2 = (bf16[128,2048]{1,0:T(8,128)(2,1)S(1)}, bf16[128,2048]{1,0:T(8,128)(2,1)S(1)}, u32[]{:S(2)}, u32[]{:S(2)}) collective-permute-start(bf16[128,2048]{1,0:T(8,128)(2,1)S(1)} %collective-permute-done.refs_1_), channel_id=1, source_target_pairs={{0,8},{8,0},{16,24},{24,16},{1,9},{9,1},{17,25},{25,17},{2,10},{10... | collective-permute-start | bytes 1572872 | tf_op jit(solution)/shard_map/ppermute | solution.py:46
  34.5 56.2 %collective-permute-start.9 = (bf16[784,512]{1,0:T(8,128)(2,1)}, bf16[784,512]{1,0:T(8,128)(2,1)}, u32[]{:S(2)}, u32[]{:S(2)}) collective-permute-start(bf16[784,512]{1,0:T(8,128)(2,1)} %collective-permute-done.8.refs_10_), channel_id=1, source_target_pairs={{0,1},{1,0},{2,3},{3,2},{4,5},{5,4},{6,7},{7,6},{8,9},{9,8},{10,11... | collective-permute-start | bytes 2408456 | tf_op jit(solution)/shard_map/ppermute | solution.py:46
  50.7 58.1 %collective-permute-start.5 = (bf16[784,512]{1,0:T(8,128)(2,1)}, bf16[784,512]{1,0:T(8,128)(2,1)}, u32[]{:S(2)}, u32[]{:S(2)}) collective-permute-start(bf16[784,512]{1,0:T(8,128)(2,1)} %collective-permute-done.4.refs_6_), channel_id=1, source_target_pairs={{0,1},{1,0},{2,3},{3,2},{4,5},{5,4},{6,7},{7,6},{8,9},{9,8},{10,11... | collective-permute-start | bytes 2408456 | tf_op jit(solution)/shard_map/ppermute | solution.py:46
  83.1 48.1 %collective-permute-start.7 = (bf16[784,512]{1,0:T(8,128)(2,1)}, bf16[784,512]{1,0:T(8,128)(2,1)}, u32[]{:S(2)}, u32[]{:S(2)}) collective-permute-start(bf16[784,512]{1,0:T(8,128)(2,1)} %collective-permute-done.6.refs_8_), channel_id=1, source_target_pairs={{0,1},{1,0},{2,3},{3,2},{4,5},{5,4},{6,7},{7,6},{8,9},{9,8},{10,11... | collective-permute-start | bytes 2408456 | tf_op jit(solution)/shard_map/ppermute | solution.py:46
  108.8 36.1 %collective-permute-start.11 = (bf16[64,2048]{1,0:T(8,128)(2,1)S(1)}, bf16[64,2048]{1,0:T(8,128)(2,1)S(1)}, u32[]{:S(2)}, u32[]{:S(2)}) collective-permute-start(bf16[64,2048]{1,0:T(8,128)(2,1)S(1)} %collective-permute-done.10.refs_0_), channel_id=1, source_target_pairs={{0,1},{1,0},{2,3},{3,2},{4,5},{5,4},{6,7},{7,6},{8,9},{9,8},{10,11... | collective-permute-start | bytes 786440 | tf_op jit(solution)/shard_map/ppermute | solution.py:46
  159.3 47.3 %collective-permute-start.23 = (bf16[128,2048]{1,0:T(8,128)(2,1)}, bf16[128,2048]{1,0:T(8,128)(2,1)S(1)}, u32[]{:S(2)}, u32[]{:S(2)}) collective-permute-start(bf16[128,2048]{1,0:T(8,128)(2,1)} %bitcast.23.refs_0_), channel_id=1, source_target_pairs={{0,4},{1,5},{2,6},{3,7},{4,0},{5,1},{6,2},{7,3},{8,12},{9,13},{10,... | collective-permute-start | bytes 1572872 | tf_op jit(solution)/shard_map/ppermute | solution.py:46
  161.9 47.9 %collective-permute-start.21 = (bf16[128,2048]{1,0:T(8,128)(2,1)}, bf16[128,2048]{1,0:T(8,128)(2,1)S(1)}, u32[]{:S(2)}, u32[]{:S(2)}) collective-permute-start(bf16[128,2048]{1,0:T(8,128)(2,1)} %bitcast.23.refs_0_), channel_id=1, source_target_pairs={{0,2},{1,3},{2,0},{3,1},{4,6},{5,7},{6,4},{7,5},{8,10},{9,11},{10,... | collective-permute-start | bytes 1572872 | tf_op jit(solution)/shard_map/ppermute | solution.py:46
  207.4 38.4 %collective-permute-start.30 = (bf16[128,2048]{1,0:T(8,128)(2,1)S(1)}, bf16[128,2048]{1,0:T(8,128)(2,1)}, u32[]{:S(2)}, u32[]{:S(2)}) collective-permute-start(bf16[128,2048]{1,0:T(8,128)(2,1)S(1)} %multiply_convert_fusion.4.refs_0_), channel_id=1, source_target_pairs={{0,4},{1,5},{2,6},{3,7},{4,0},{5,1},{6,2},{7,3},{8,12},{9,13},{10,... | collective-permute-start | bytes 1572872 | tf_op jit(solution)/shard_map/ppermute | solution.py:46
  209.8 37.4 %collective-permute-start.32 = (bf16[128,2048]{1,0:T(8,128)(2,1)S(1)}, bf16[128,2048]{1,0:T(8,128)(2,1)}, u32[]{:S(2)}, u32[]{:S(2)}) collective-permute-start(bf16[128,2048]{1,0:T(8,128)(2,1)S(1)} %multiply_convert_fusion.4.refs_0_), channel_id=1, source_target_pairs={{0,6},{1,7},{2,4},{3,5},{4,2},{5,3},{6,0},{7,1},{8,14},{9,15},{10,... | collective-permute-start | bytes 1572872 | tf_op jit(solution)/shard_map/ppermute | solution.py:46
  247.2 40.7 %collective-permute-start.33 = (bf16[128,2048]{1,0:T(8,128)(2,1)}, bf16[128,2048]{1,0:T(8,128)(2,1)}, u32[]{:S(2)}, u32[]{:S(2)}) collective-permute-start(bf16[128,2048]{1,0:T(8,128)(2,1)} %collective-permute-done.32.refs_6_), channel_id=1, source_target_pairs={{0,1},{1,0},{2,3},{3,2},{4,5},{5,4},{6,7},{7,6},{8,9},{9,8},{10,11... | collective-permute-start | bytes 1572872 | tf_op jit(solution)/shard_map/ppermute | solution.py:46
  363.7 347.9 %reduce-scatter.5.cloned.1.call-start = ((), (), s32[]{:S(2)}) async-start(), calls=%async_computation.5 | async-start | bytes 31457280 | tf_op jit(solution)/shard_map/reduce_scatter | solution.py:587
  365.2 51.5 %collective-permute-start.34 = (bf16[4,128,1408]{2,1,0:T(8,128)(2,1)S(1)}, bf16[4,128,1408]{2,1,0:T(8,128)(2,1)S(1)}, u32[]{:S(2)}, u32[]{:S(2)}) collective-permute-start(bf16[4,128,1408]{2,1,0:T(8,128)(2,1)S(1)} %slice_bitcast_fusion.1), channel_id=1, source_target_pairs={{0,1},{1,0},{2,3},{3,2},{4,5},{5,4},{6,7},{7,6},{8,9},{9,8},{10,11... | collective-permute-start | bytes 4325384 | tf_op jit(solution)/shard_map/ppermute | solution.py:46
  368.1 45.9 %collective-permute-start.38 = (bf16[2,128,640]{2,1,0:T(8,128)(2,1)}, bf16[2,128,640]{2,1,0:T(8,128)(2,1)S(1)}, u32[]{:S(2)}, u32[]{:S(2)}) collective-permute-start(bf16[2,128,640]{2,1,0:T(8,128)(2,1)} %get-tuple-element.140), channel_id=1, source_target_pairs={{0,2},{1,3},{2,0},{3,1},{4,6},{5,7},{6,4},{7,5},{8,10},{9,11},{10,... | collective-permute-start | bytes 983048 | tf_op jit(solution)/shard_map/ppermute | solution.py:46
  368.7 45.3 %collective-permute-start.39 = (bf16[2,128,640]{2,1,0:T(8,128)(2,1)}, bf16[2,128,640]{2,1,0:T(8,128)(2,1)}, u32[]{:S(2)}, u32[]{:S(2)}) collective-permute-start(bf16[2,128,640]{2,1,0:T(8,128)(2,1)} %get-tuple-element.142), channel_id=1, source_target_pairs={{0,4},{1,5},{2,6},{3,7},{4,0},{5,1},{6,2},{7,3},{8,12},{9,13},{10,... | collective-permute-start | bytes 983048 | tf_op jit(solution)/shard_map/ppermute | solution.py:46
  370.7 43.3 %collective-permute-start.40 = (bf16[2,128,640]{2,1,0:T(8,128)(2,1)S(1)}, bf16[2,128,640]{2,1,0:T(8,128)(2,1)}, u32[]{:S(2)}, u32[]{:S(2)}) collective-permute-start(bf16[2,128,640]{2,1,0:T(8,128)(2,1)S(1)} %get-tuple-element.141), channel_id=1, source_target_pairs={{0,6},{1,7},{2,4},{3,5},{4,2},{5,3},{6,0},{7,1},{8,14},{9,15},{10,... | collective-permute-start | bytes 983048 | tf_op jit(solution)/shard_map/ppermute | solution.py:46
  424.7 50.7 %collective-permute-start.47 = (bf16[2,128,640]{2,1,0:T(8,128)(2,1)}, bf16[2,128,640]{2,1,0:T(8,128)(2,1)}, u32[]{:S(2)}, u32[]{:S(2)}) collective-permute-start(bf16[2,128,640]{2,1,0:T(8,128)(2,1)} %get-tuple-element.139), channel_id=1, source_target_pairs={{0,4},{1,5},{2,6},{3,7},{4,0},{5,1},{6,2},{7,3},{8,12},{9,13},{10,... | collective-permute-start | bytes 983048 | tf_op jit(solution)/shard_map/ppermute | solution.py:46
  436.1 39.4 %collective-permute-start.48 = (bf16[2,128,640]{2,1,0:T(8,128)(2,1)S(1)}, bf16[2,128,640]{2,1,0:T(8,128)(2,1)}, u32[]{:S(2)}, u32[]{:S(2)}) collective-permute-start(bf16[2,128,640]{2,1,0:T(8,128)(2,1)S(1)} %get-tuple-element.138), channel_id=1, source_target_pairs={{0,6},{1,7},{2,4},{3,5},{4,2},{5,3},{6,0},{7,1},{8,14},{9,15},{10,... | collective-permute-start | bytes 983048 | tf_op jit(solution)/shard_map/ppermute | solution.py:46
  535.5 58.6 %collective-permute-start.53 = (bf16[4,512,512]{2,1,0:T(8,128)(2,1)S(1)}, bf16[4,512,512]{2,1,0:T(8,128)(2,1)S(1)}, u32[]{:S(2)}, u32[]{:S(2)}) collective-permute-start(bf16[4,512,512]{2,1,0:T(8,128)(2,1)S(1)} %copy-done.90), channel_id=1, source_target_pairs={{0,1},{1,0},{2,3},{3,2},{4,5},{5,4},{6,7},{7,6},{8,9},{9,8},{10,11... | collective-permute-start | bytes 6291464 | tf_op jit(solution)/shard_map/ppermute | solution.py:46
  553.4 40.4 %collective-permute-start.64 = (bf16[2,272,512]{2,1,0:T(8,128)(2,1)S(1)}, bf16[2,272,512]{2,1,0:T(8,128)(2,1)S(1)}, u32[]{:S(2)}, u32[]{:S(2)}) collective-permute-start(bf16[2,272,512]{2,1,0:T(8,128)(2,1)S(1)} %copy-done.92), channel_id=1, source_target_pairs={{0,4},{1,5},{2,6},{3,7},{4,0},{5,1},{6,2},{7,3},{8,12},{9,13},{10,... | collective-permute-start | bytes 1671176 | tf_op jit(solution)/shard_map/ppermute | solution.py:46
  553.4 40.4 %collective-permute-start.65 = (bf16[2,272,512]{2,1,0:T(8,128)(2,1)S(1)}, bf16[2,272,512]{2,1,0:T(8,128)(2,1)S(1)}, u32[]{:S(2)}, u32[]{:S(2)}) collective-permute-start(bf16[2,272,512]{2,1,0:T(8,128)(2,1)S(1)} %copy-done.91), channel_id=1, source_target_pairs={{0,6},{1,7},{2,4},{3,5},{4,2},{5,3},{6,0},{7,1},{8,14},{9,15},{10,... | collective-permute-start | bytes 1671176 | tf_op jit(solution)/shard_map/ppermute | solution.py:46
  596.9 50.1 %collective-permute-start.60 = (bf16[512,512]{1,0:T(8,128)(2,1)}, bf16[512,512]{1,0:T(8,128)(2,1)S(1)}, u32[]{:S(2)}, u32[]{:S(2)}) collective-permute-start(bf16[512,512]{1,0:T(8,128)(2,1)} %get-tuple-element.104), channel_id=1, source_target_pairs={{0,2},{1,3},{2,0},{3,1},{4,6},{5,7},{6,4},{7,5},{8,10},{9,11},{10,... | collective-permute-start | bytes 1572872 | tf_op jit(solution)/shard_map/ppermute | solution.py:46
  607.3 44.1 %collective-permute-start.61 = (bf16[512,512]{1,0:T(8,128)(2,1)}, bf16[512,512]{1,0:T(8,128)(2,1)S(1)}, u32[]{:S(2)}, u32[]{:S(2)}) collective-permute-start(bf16[512,512]{1,0:T(8,128)(2,1)} %get-tuple-element.105), channel_id=1, source_target_pairs={{0,4},{1,5},{2,6},{3,7},{4,0},{5,1},{6,2},{7,3},{8,12},{9,13},{10,... | collective-permute-start | bytes 1572872 | tf_op jit(solution)/shard_map/ppermute | solution.py:46
  608.2 43.2 %collective-permute-start.62 = (bf16[512,512]{1,0:T(8,128)(2,1)}, bf16[512,512]{1,0:T(8,128)(2,1)S(1)}, u32[]{:S(2)}, u32[]{:S(2)}) collective-permute-start(bf16[512,512]{1,0:T(8,128)(2,1)} %get-tuple-element.106), channel_id=1, source_target_pairs={{0,6},{1,7},{2,4},{3,5},{4,2},{5,3},{6,0},{7,1},{8,14},{9,15},{10,... | collective-permute-start | bytes 1572872 | tf_op jit(solution)/shard_map/ppermute | solution.py:46
  609.7 37.1 %collective-permute-start.66 = (bf16[272,512]{1,0:T(8,128)(2,1)S(1)}, bf16[272,512]{1,0:T(8,128)(2,1)S(1)}, u32[]{:S(2)}, u32[]{:S(2)}) collective-permute-start(bf16[272,512]{1,0:T(8,128)(2,1)S(1)} %fusion.61), channel_id=1, source_target_pairs={{0,1},{1,0},{2,3},{3,2},{4,5},{5,4},{6,7},{7,6},{8,9},{9,8},{10,11... | collective-permute-start | bytes 835592 | tf_op jit(solution)/shard_map/ppermute | solution.py:46
  612.3 63.2 %collective-permute-start.72 = (bf16[64,2048]{1,0:T(8,128)(2,1)S(1)}, bf16[64,2048]{1,0:T(8,128)(2,1)}, u32[]{:S(2)}, u32[]{:S(2)}) collective-permute-start(bf16[64,2048]{1,0:T(8,128)(2,1)S(1)} %collective-permute-done.70.refs_4_), channel_id=1, source_target_pairs={{0,16},{8,24},{16,0},{24,8},{1,17},{9,25},{17,1},{25,9},{2,18},{10... | collective-permute-start | bytes 786440 | tf_op jit(solution)/shard_map/ppermute | solution.py:46
  653.0 37.5 %collective-permute-start.68 = (bf16[784,512]{1,0:T(8,128)(2,1)S(1)}, bf16[784,512]{1,0:T(8,128)(2,1)S(1)}, u32[]{:S(2)}, u32[]{:S(2)}) collective-permute-start(bf16[784,512]{1,0:T(8,128)(2,1)S(1)} %pad_maximum_fusion.2.refs_0_), channel_id=1, source_target_pairs={{0,16},{8,24},{16,0},{24,8},{1,17},{9,25},{17,1},{25,9},{2,18},{10... | collective-permute-start | bytes 2408456 | tf_op jit(solution)/shard_map/ppermute | solution.py:46
  (149 other events, 3205.8 us)
Sparse Core Ops, SparseCore 0:
  9.6 96.2 all-gather.4
  107.4 169.0 all-gather.2
  363.8 107.0 reduce-scatter.2
  473.3 214.9 reduce-scatter.4

commit v4 on v3

--- a/solution.py
+++ b/solution.py
@@ -338,7 +338,7 @@
 
     @pl.when(pl.program_id(0) == 0)
     def _():
-        for q, piece_ref in enumerate(piece_refs):
+        for q, piece_ref in enumerate(reversed(piece_refs)):
             all_ref[q * tok : (q + 1) * tok, :] = piece_ref[...]
 
     dy_ref[0] = (mm(picks_ref[0], all_ref[...]) * scale_ref[0]).astype(bf16)
@@ -367,6 +367,25 @@
     hid_ref[0] = (act * up).astype(bf16)
     dg_ref[0] = (d_hid * up * sig * (1.0 + gate * (1.0 - sig))).astype(bf16)
     du_ref[0] = (d_hid * act).astype(bf16)
+
+
+def widen_kernel(from_ref, to_ref):
+    to_ref[...] = from_ref[...].astype(f32)
+
+
+def widen(values):
+    count, rows, columns = values.shape
+    block = pl.BlockSpec((1, min(rows, 256), columns), lambda i, j: (i, j, 0))
+    return pl.pallas_call(
+        widen_kernel,
+        grid=(count, rows // min(rows, 256)),
+        in_specs=[block],
+        out_specs=block,
+        out_shape=jax.ShapeDtypeStruct(values.shape, f32),
+        compiler_params=params(24),
+        cost_estimate=cost(5),
+        name="widen",
+    )(values)
 
 
 def body(
@@ -545,7 +564,7 @@
         compiler_params=params(40),
         cost_estimate=cost(5),
         name="dispatch",
-    )(picks, scale, *cot_pieces)
+    )(picks, scale, *reversed(cot_pieces))
     hid_shape = jax.ShapeDtypeStruct((local_experts, slots, hidden_units), bf16)
     rows, hidden_low, gate_grad, up_grad = pl.pallas_call(
         hidden_kernel,
@@ -574,20 +593,18 @@
     pair_grad = jnp.concatenate([gate_grad, up_grad], axis=2)
 
     token_blocks = lambda values: split_blocks(values.reshape(n_fsdp, tok_rows, model_width), split)
-    dxe = jnp.einsum("erk,edk->erd", pair_grad, gate_up_all, preferred_element_type=f32).astype(bf16)
+    down_part = jnp.einsum("erd,erf->edf", dy, hidden_low, preferred_element_type=f32).astype(bf16)
+    down_grad = widen(lax.psum_scatter(down_part, "ctx", scatter_dimension=1, tiled=True))
+    dxe = jnp.einsum("erk,edk->erd", after(pair_grad, down_part), gate_up_all, preferred_element_type=f32).astype(bf16)
     grads_back = jnp.einsum("est,esd->td", picks, dxe, preferred_element_type=f32).astype(bf16)
     dx_first = scatter_first(*token_blocks(grads_back))
-    down_part = jnp.einsum(
-        "erd,erf->edf", after(dy, grads_back), hidden_low, preferred_element_type=f32
-    ).astype(bf16)
-    down_grad = lax.psum_scatter(down_part, "ctx", scatter_dimension=1, tiled=True).astype(f32)
     pair_part = jnp.einsum(
         "erd,erk->edk", after(rows, grads_back), pair_grad, preferred_element_type=f32
     ).astype(bf16)
-    gate_up_grad = lax.psum_scatter(pair_part, "ctx", scatter_dimension=1, tiled=True).astype(f32)
+    gate_up_grad = widen(lax.psum_scatter(pair_part, "ctx", scatter_dimension=1, tiled=True))
     da2 = jnp.concatenate(scatter_second(dx_first, pair_part), axis=1)
     made = jnp.einsum(
-        "erf,edf->erd", after(hidden_low, grads_back), down_all, preferred_element_type=f32
+        "erf,edf->erd", after(hidden_low, *dx_first[0], *dx_first[1:]), down_all, preferred_element_type=f32
     )
     made = (scale * made.astype(bf16).astype(f32)).astype(bf16)
     mixed = jnp.einsum("est,esd->td", picks, made, preferred_element_type=f32).astype(bf16)
@@ -595,7 +612,7 @@
 
     dh_part, gain_two_grad = norm_two_back(da2)
     dh_one = cot_rows + dh_part
-    dattn_pieces = gather_ctx(dh_one.astype(bf16))
+    dattn_pieces = gather_ctx(after(dh_one.astype(bf16), mixed))
     dattn_pieces = [dattn_pieces[q] for q in order]
     proj_grad, head_grads = pl.pallas_call(
         functools.partial(attend_back_kernel, (n_ctx, head_dim, q_rows)),
@@ -609,7 +626,7 @@
         compiler_params=params(56),
         cost_estimate=cost(500),
         name="attend_back",
-    )(*dattn_pieces, out_own, after(q_low, *mixed_first[0], *mixed_first[1:]), k_low, v_low, q_proj, k_proj, cosine, sine, doc_q, doc_k, heads)
+    )(*dattn_pieces, out_own, q_low, k_low, v_low, q_proj, k_proj, cosine, sine, doc_q, doc_k, heads)
     dattn = jnp.concatenate(dattn_pieces, axis=0)
     out_part = mm(attn_low, dattn, TN).astype(bf16)
     out_blocks = jnp.stack(
@@ -619,8 +636,6 @@
         ]
     )
     out_first_sums = scatter_first(*split_blocks(out_blocks, split))
-    out_parts = scatter_second(out_first_sums, proj_grad)
-    out_sum = jnp.concatenate(out_parts, axis=1)
     half_stack = jax.ShapeDtypeStruct((n_fsdp // 2, 2 * norm_rows, own_width), bf16)
     pair_shape = jax.ShapeDtypeStruct((2, norm_rows + extra_rows, own_width), bf16)
     even_a, odd_a, *pairs_b, da1 = pl.pallas_call(
@@ -635,19 +650,21 @@
             pltpu.VMEM((extra_rows, own_width), f32),
         ],
         compiler_params=params(56),
-        cost_estimate=cost(500),
+        cost_estimate=cost(10),
         name="project_back",
-    )(f_at, *x_pieces, *qkv_pieces, a1, after(proj_grad, *out_first_sums[0], out_first_sums[2]), head_grads, gain_two_grad[None])
-    payload_first = scatter_first(even_a, odd_a, pairs_b)
+    )(f_at, *x_pieces, *qkv_pieces, a1, proj_grad, head_grads, gain_two_grad[None])
+    ready = (*mixed_first[0], *mixed_first[1:], *out_first_sums[0], *out_first_sums[1:])
+    payload_first = scatter_first(even_a, after(odd_a, *ready), pairs_b)
     da1 = scatter_ctx(da1.reshape(n_ctx, tok_rows, model_width))
+    payload_parts = scatter_second(payload_first, down_grad)
+    qkv_sum = jnp.concatenate(payload_parts, axis=0)
+    out_parts = scatter_second(out_first_sums, *payload_parts)
+    out_sum = jnp.concatenate(out_parts, axis=1)
     out_sum = lax.ppermute(out_sum.astype(bf16), ("ctx", "fsdp"), [(b, a) for a, b in to_heads])
     out_ends = gather_ctx(out_sum)
-    payload_parts = scatter_second(payload_first, *out_parts, da1, down_grad)
-    qkv_sum = jnp.concatenate(payload_parts, axis=0)
     _, norm_one_back = jax.vjp(lambda x: rms_scale(x, gains[0]), x_rows)
     inputs_grad = dh_one + norm_one_back(da1)[0]
-    mixed_parts = scatter_second(mixed_first, *payload_parts)
-    ends = gather_ctx(qkv_sum.astype(bf16))
+    ends = gather_ctx(after(qkv_sum.astype(bf16), da1))
     qkv_grad, out_grad = pl.pallas_call(
         functools.partial(finish_kernel, (n_ctx, norm_rows)),
         in_specs=[SMEM] + [VMEM] * (2 * n_ctx),
@@ -660,8 +677,8 @@
         cost_estimate=cost(1),
         name="finish",
     )(c_at, *ends, *out_ends)
-    gate_up_grad = after(gate_up_grad, out_grad)
-    h_one = after(h_one, out_grad, gate_up_grad)
+    mixed_first[0][0] = after(mixed_first[0][0], gate_up_grad)
+    mixed_parts = scatter_second(mixed_first, *payload_parts)
     block_out = (h_one + jnp.concatenate(mixed_parts, axis=1)).astype(bf16)
     extras = sum(piece[3 * norm_rows :].astype(f32) for piece in ends).reshape(-1)
     norm_grad = extras[: 2 * norm_rows].reshape(2, norm_rows).T

time: 737 us -> 719 us (0.976)
  starting transfers between devices: 175 us -> 113 us
  waiting for transfers between devices: 266 us -> 314 us
  other arithmetic: 47.4 us -> 35.1 us
  Pallas kernels: 94.6 us -> 104 us
    ppermute x76, starting transfers between devices: 173 us -> 111 us  [swap(): return lax.ppermute(value, axis, [(i, i ^ mask) for i in range(size)])]
    ppermute x76, waiting for transfers between devices: 265 us -> 313 us  [swap(): return lax.ppermute(value, axis, [(i, i ^ mask) for i in range(size)])]
    convert_element_type x2 -> x1, other arithmetic: 10.7 us -> 1.56 us  [body(): dattn_pieces = gather_ctx(after(dh_one.astype(bf16), mixed))]
    pallas_call x0 -> x2, Pallas kernels: none -> 8.97 us  [widen(): pl.pallas_call(widen_kernel, grid=(count, rows // min(rows, 256)), in_spe...]
    unnamed x221 -> x203, local copies, waits for them, and re-layouts: 28.9 us -> 31.1 us
  transfers between devices with their start and end apart: 82 -> 82, of which waited for: 21 -> 27; matrix products, arithmetic and copies ran while one was open for 14% -> 18% of each run, Pallas kernels for 8% -> 10%
where the time goes in v4:
time: 719 us; the launch traced here: 715 us
  waiting for transfers between devices  314 us (44%)
  starting transfers between devices  113 us (16%)
  Pallas kernels  104 us (14%)
  matrix products  80 us (11%)
  local copies, waits for them, and re-layouts  52.9 us (7%)
  other arithmetic  35.1 us (5%)
  between operations  15.6 us (2%)
    ppermute x76, waiting for transfers between devices, swap(): return lax.ppermute(value, axis, [(i, i ^ mask) for i in range(size)])  313 us
    ppermute x76, starting transfers between devices, swap(): return lax.ppermute(value, axis, [(i, i ^ mask) for i in range(size)])  111 us
    pallas_call x1, Pallas kernels, body(): pl.pallas_call(hidden_kernel, grid=(local_experts, hidden_units // tile),...  35.2 us
    unnamed x203, local copies, waits for them, and re-layouts  31.1 us
    dot_general x1, matrix products, body(): jnp.einsum('erk,edk->erd', after(pair_grad, down_part), gate_up_all, pref...  20.5 us
    dot_general x1, matrix products, body(): jnp.einsum('est,esd->td', picks, made, preferred_element_type=f32)  17.7 us
    dot_general x1, matrix products, body(): jnp.einsum('erd,erk->edk', after(rows, grads_back), pair_grad, preferred_...  17.3 us
    pallas_call x1, Pallas kernels, body(): pl.pallas_call(functools.partial(attend_back_kernel, (n_ctx, head_dim, q_...  16.9 us
  transfers between devices with their start and end apart: 82, of which 27 were waited for; matrix products, arithmetic and copies ran while one was open for 18% of the time, Pallas kernels for 10%

profile of v4, /device:TPU:0, one launch (start us, length us, event | category | flops | bytes accessed | tf_op | source)
XLA Modules:
  0.0 715.2 jit_solution(13307260946664195919)
XLA Ops:
  17.3 15.8 %collective-permute-done.refs_1_ = bf16[128,2048]{1,0:T(8,128)(2,1)S(1)} collective-permute-done((bf16[128,2048]{1,0:T(8,128)(2,1)S(1)}, bf16[128,2048]{1,0:T(8,128)(2,1)S(1)}, u32[]{:S(2)}, u32[]{:S(2)}) %collective-permute-start) | collective-permute-done | bytes 524320 | tf_op jit(solution)/shard_map/ppermute | solution.py:46
  37.0 13.7 %collective-permute-done.4.refs_6_ = bf16[784,512]{1,0:T(8,128)(2,1)} collective-permute-done((bf16[784,512]{1,0:T(8,128)(2,1)S(1)}, bf16[784,512]{1,0:T(8,128)(2,1)}, u32[]{:S(2)}, u32[]{:S(2)}) %collective-permute-start.4) | collective-permute-done | bytes 802848 | tf_op jit(solution)/shard_map/ppermute | solution.py:46
  52.1 31.0 %collective-permute-done.6.refs_8_ = bf16[784,512]{1,0:T(8,128)(2,1)} collective-permute-done((bf16[784,512]{1,0:T(8,128)(2,1)S(1)}, bf16[784,512]{1,0:T(8,128)(2,1)}, u32[]{:S(2)}, u32[]{:S(2)}) %collective-permute-start.6) | collective-permute-done | bytes 802848 | tf_op jit(solution)/shard_map/ppermute | solution.py:46
  90.4 15.1 %collective-permute-start.12 = (bf16[64,2048]{1,0:T(8,128)(2,1)S(1)}, bf16[64,2048]{1,0:T(8,128)(2,1)}, u32[]{:S(2)}, u32[]{:S(2)}) collective-permute-start(bf16[64,2048]{1,0:T(8,128)(2,1)S(1)} %collective-permute-done.10.refs_0_), channel_id=1, source_target_pairs={{0,2},{1,3},{2,0},{3,1},{4,6},{5,7},{6,4},{7,5},{8,10},{9,11},{10,... | collective-permute-start | bytes 786440 | tf_op jit(solution)/shard_map/ppermute | solution.py:46
  108.8 6.0 collective-permute-start.11
  118.0 8.2 %collective-permute-done.14.refs_4_ = bf16[64,2048]{1,0:T(8,128)(2,1)} collective-permute-done((bf16[64,2048]{1,0:T(8,128)(2,1)S(1)}, bf16[64,2048]{1,0:T(8,128)(2,1)}, u32[]{:S(2)}, u32[]{:S(2)}) %collective-permute-start.14) | collective-permute-done | bytes 262176 | tf_op jit(solution)/shard_map/ppermute | solution.py:46
  132.3 11.9 %attend.1 = (bf16[512,2048]{1,0:T(8,128)(2,1)}, f32[512,512]{1,0:T(8,128)}, f32[512,512]{1,0:T(8,128)}, bf16[512,512]{1,0:T(8,128)(2,1)S(1)}, bf16[512,512]{1,0:...) custom-call(s32[1]{0:T(128)} %bitcast.f_ref, ...), custom_call_target="tpu_custom_call" | custom-call | flops 1000000000 | tf_op jit(solution)/shard_map/attend/pallas_call | solution.py:489
  162.0 18.3 %collective-permute-done.19 = bf16[1,128,2048]{2,1,0:T(8,128)(2,1)S(1)} collective-permute-done((bf16[1,128,2048]{2,1,0:T(8,128)(2,1)S(1)}, bf16[1,128,2048]{2,1,0:T(8,128)(2,1)S(1)}, u32[]{:S(2)}, u32[]{:S(2)}) %collective-permute-start.19) | collective-permute-done | bytes 524320 | tf_op jit(solution)/shard_map/ppermute | solution.py:46
  183.8 22.8 %collective-permute-done.22.refs_3_ = bf16[128,2048]{1,0:T(8,128)(2,1)S(1)} collective-permute-done((bf16[128,2048]{1,0:T(8,128)(2,1)}, bf16[128,2048]{1,0:T(8,128)(2,1)S(1)}, u32[]{:S(2)}, u32[]{:S(2)}) %collective-permute-start.22) | collective-permute-done | bytes 524320 | tf_op jit(solution)/shard_map/ppermute | solution.py:46
  223.9 8.6 %collective-permute-done.25.refs_4_ = bf16[128,2048]{1,0:T(8,128)(2,1)S(1)} collective-permute-done((bf16[128,2048]{1,0:T(8,128)(2,1)S(1)}, bf16[128,2048]{1,0:T(8,128)(2,1)S(1)}, u32[]{:S(2)}, u32[]{:S(2)}) %collective-permute-start.25) | collective-permute-done | bytes 524320 | tf_op jit(solution)/shard_map/ppermute | solution.py:46
  235.4 10.6 %collective-permute-done.30.refs_4_ = bf16[128,2048]{1,0:T(8,128)(2,1)} collective-permute-done((bf16[128,2048]{1,0:T(8,128)(2,1)}, bf16[128,2048]{1,0:T(8,128)(2,1)}, u32[]{:S(2)}, u32[]{:S(2)}) %collective-permute-start.30) | collective-permute-done | bytes 524320 | tf_op jit(solution)/shard_map/ppermute | solution.py:46
  257.2 7.5 %dispatch.1.dy_ref = bf16[3,432,2048]{2,1,0:T(8,128)(2,1)S(1)} custom-call(bf16[3,432,1024]{2,1,0:T(8,128)(2,1)S(1)} %fusion.7.picks_ref, f32[3,432,1]{2,1,0:T(8,128)S(1)} %copy-done.14, bf16[128,2048]{1,0:T(8,128)(2,1)S(1)} %copy-done.33, bf16[128,2048]{1,0:T(8,128)(2,1)S(1)} %copy-done.27, bf16[128,2048]{1,0:T(8,128)(2,1)S(1)} %copy-done.35, ...), custom_call_target="tpu_custom_call" | custom-call | flops 5000000000 | tf_op jit(solution)/shard_map/dispatch/pallas_call | solution.py:553
  267.2 10.5 %collective-permute-done.31.refs_5_ = bf16[128,2048]{1,0:T(8,128)(2,1)} collective-permute-done((bf16[128,2048]{1,0:T(8,128)(2,1)}, bf16[128,2048]{1,0:T(8,128)(2,1)}, u32[]{:S(2)}, u32[]{:S(2)}) %collective-permute-start.31) | collective-permute-done | bytes 524320 | tf_op jit(solution)/shard_map/ppermute | solution.py:46
  277.6 10.3 %collective-permute-done.33.refs_7_ = bf16[128,2048]{1,0:T(8,128)(2,1)} collective-permute-done((bf16[128,2048]{1,0:T(8,128)(2,1)}, bf16[128,2048]{1,0:T(8,128)(2,1)}, u32[]{:S(2)}, u32[]{:S(2)}) %collective-permute-start.33) | collective-permute-done | bytes 524320 | tf_op jit(solution)/shard_map/ppermute | solution.py:46
  287.9 35.2 %hidden.1 = (bf16[3,432,2048]{2,1,0:T(8,128)(2,1)}, bf16[3,432,1024]{2,1,0:T(8,128)(2,1)}, bf16[3,432,1024]{2,1,0:T(8,128)(2,1)}, bf16[3,432,1024]{2,1,0:T(8,128)(2,1)}) custom-call(bf16[3,432,1024]{2,1,0:T(8,128)(2,1)} %copy-done.6, bf16[3,432,2048]{2,1,0:T(8,128)(2,1)} %copy-done.8, bf16[3,2048,2048]{2,1,0:T(8,128)(2,1)} %all-gather.3.cloned.1.call-done.wg_ref.wu_ref, ...), custom_call_target="tpu_custom_call" | custom-call | flops 20000000000 | tf_op jit(solution)/shard_map/hidden/pallas_call | solution.py:569
  323.1 11.4 %convolution_convert_fusion.1 = bf16[3,2048,1024]{2,1,0:T(8,128)(2,1)} fusion(bf16[3,432,2048]{2,1,0:T(8,128)(2,1)S(1)} %copy-done.9, bf16[3,432,1024]{2,1,0:T(8,128)(2,1)} %get-tuple-element.78), kind=kOutput, calls=%fused_computation.4 | convolution fusion | flops 5442109440 | bytes 20545536 | tf_op jit(solution)/shard_map/erd,erf->edf/dot_general | solution.py:596
  338.4 20.5 %fusion.73 = bf16[3,432,2048]{2,1,0:T(8,128)(2,1)} fusion(bf16[3,432,2048]{2,1,0:T(8,128)(2,1)S(1)} %constant_dynamic-update-slice_fusion, bf16[3,2048,2048]{2,1,0:T(8,128)(2,1)} %all-gather.3.cloned.1.call-done.wg_ref.wu_ref), kind=kOutput, calls=%fused_computation.229 | convolution fusion | flops 10871635968 | bytes 35782656 | tf_op jit(solution)/shard_map/erk,edk->erd/dot_general | solution.py:598
  359.0 11.3 %bitcast_convert_fusion.1 = bf16[1024,2048]{1,0:T(8,128)(2,1)} fusion(bf16[3,432,2048]{2,1,0:T(8,128)(2,1)} %fusion.73, s32[3,1024]{1,0:T(4,128)S(1)} %fusion.23), kind=kOutput, calls=%fused_computation.3 | convolution fusion | flops 5439242240 | bytes 9515008 | tf_op jit(solution)/shard_map/est,esd->td/dot_general | solution.py:599
  380.0 17.3 %convolution_convert_fusion = bf16[3,2048,2048]{2,1,0:T(8,128)(2,1)} fusion(bf16[3,432,2048]{2,1,0:T(8,128)(2,1)S(1)} %bitcast.423, bf16[3,432,2048]{2,1,0:T(8,128)(2,1)S(1)} %constant_dynamic-update-slice_fusion), kind=kOutput, calls=%fused_computation | convolution fusion | flops 10884218880 | bytes 35782656 | tf_op jit(solution)/shard_map/erd,erk->edk/dot_general | solution.py:601
  404.2 10.6 %collective-permute-done.42 = bf16[128,640]{1,0:T(8,128)(2,1)S(1)} collective-permute-done((bf16[128,640]{1,0:T(8,128)(2,1)S(1)}, bf16[128,640]{1,0:T(8,128)(2,1)S(1)}, u32[]{:S(2)}, u32[]{:S(2)}) %collective-permute-start.42) | collective-permute-done | bytes 163872 | tf_op jit(solution)/shard_map/ppermute | solution.py:46
  421.8 17.7 %bitcast_convert_fusion = bf16[1024,2048]{1,0:T(8,128)(2,1)} fusion(bf16[3,432,1024]{2,1,0:T(8,128)(2,1)} %get-tuple-element.78, bf16[3,2048,1024]{2,1,0:T(8,128)(2,1)} %all-gather.5.cloned.1.call-done.wd_ref, f32[3,432]{1,0:T(4,128)S(1)} %select_reduce_fusion, s32[3,1024]{1,0:T(4,128)S(1)} %fusion.23), kind=kOutput, calls=%fused_computation.2 | convolution fusion | flops 10885677056 | bytes 19448896 | tf_op jit(solution)/shard_map/est,esd->td/dot_general | solution.py:610
  439.5 9.6 %collective-permute-done.40 = bf16[128,1408]{1,0:T(8,128)(2,1)S(1)} collective-permute-done((bf16[128,1408]{1,0:T(8,128)(2,1)}, bf16[128,1408]{1,0:T(8,128)(2,1)S(1)}, u32[]{:S(2)}, u32[]{:S(2)}) %collective-permute-start.40) | collective-permute-done | bytes 360480 | tf_op jit(solution)/shard_map/ppermute | solution.py:46
  459.3 6.3 collective-permute-done.43.refs_1_
  469.3 13.3 %collective-permute-done.47 = bf16[2,128,640]{2,1,0:T(8,128)(2,1)S(1)} collective-permute-done((bf16[2,128,640]{2,1,0:T(8,128)(2,1)S(1)}, bf16[2,128,640]{2,1,0:T(8,128)(2,1)S(1)}, u32[]{:S(2)}, u32[]{:S(2)}) %collective-permute-start.47) | collective-permute-done | bytes 327712 | tf_op jit(solution)/shard_map/ppermute | solution.py:46
  495.5 16.9 %attend_back.1 = (bf16[3,512,512]{2,1,0:T(8,128)(2,1)}, f32[2,128]{1,0:T(2,128)}) custom-call(bf16[128,2048]{1,0:T(8,128)(2,1)} %copy-done.64, bf16[128,2048]{1,0:T(8,128)(2,1)} %copy-done.84, bf16[128,2048]{1,0:T(8,128)(2,1)} %copy-done.85, bf16[128,2048]{1,0:T(8,128)(2,1)} %copy-done.86, bf16[512,2048]{1,0:T(8,128)(2,1)} %copy-done.39, ...), custom_call_target="tpu_custom_call" | custom-call | flops 499999997952 | tf_op jit(solution)/shard_map/attend_back/pallas_call | solution.py:617
  512.4 15.2 %project_back.1 = (bf16[4,512,512]{2,1,0:T(8,128)(2,1)}, bf16[4,512,512]{2,1,0:T(8,128)(2,1)}, bf16[2,272,512]{2,1,0:T(8,128)(2,1)}, bf16[2,272,512]{2,1,0:T(8,1...) custom-call(s32[1]{0:T(128)} %bitcast.f_ref, ...), custom_call_target="tpu_custom_call" | custom-call | flops 10000000000 | tf_op jit(solution)/shard_map/project_back/pallas_call | solution.py:641
  540.8 11.9 %collective-permute-done.59 = bf16[2,272,512]{2,1,0:T(8,128)(2,1)S(1)} collective-permute-done((bf16[2,272,512]{2,1,0:T(8,128)(2,1)S(1)}, bf16[2,272,512]{2,1,0:T(8,128)(2,1)S(1)}, u32[]{:S(2)}, u32[]{:S(2)}) %collective-permute-start.59) | collective-permute-done | bytes 557088 | tf_op jit(solution)/shard_map/ppermute | solution.py:46
  552.7 28.7 %collective-permute-done.58 = bf16[2,272,512]{2,1,0:T(8,128)(2,1)S(1)} collective-permute-done((bf16[2,272,512]{2,1,0:T(8,128)(2,1)S(1)}, bf16[2,272,512]{2,1,0:T(8,128)(2,1)S(1)}, u32[]{:S(2)}, u32[]{:S(2)}) %collective-permute-start.58) | collective-permute-done | bytes 557088 | tf_op jit(solution)/shard_map/ppermute | solution.py:46
  595.7 12.2 %collective-permute-done.56 = bf16[512,512]{1,0:T(8,128)(2,1)S(1)} collective-permute-done((bf16[512,512]{1,0:T(8,128)(2,1)S(1)}, bf16[512,512]{1,0:T(8,128)(2,1)S(1)}, u32[]{:S(2)}, u32[]{:S(2)}) %collective-permute-start.56) | collective-permute-done | bytes 524320 | tf_op jit(solution)/shard_map/ppermute | solution.py:46
  607.9 26.7 %collective-permute-done.55 = bf16[512,512]{1,0:T(8,128)(2,1)S(1)} collective-permute-done((bf16[512,512]{1,0:T(8,128)(2,1)S(1)}, bf16[512,512]{1,0:T(8,128)(2,1)S(1)}, u32[]{:S(2)}, u32[]{:S(2)}) %collective-permute-start.55) | collective-permute-done | bytes 524320 | tf_op jit(solution)/shard_map/ppermute | solution.py:46
  657.7 10.2 %collective-permute-done.66 = bf16[1,128,2048]{2,1,0:T(8,128)(2,1)S(1)} collective-permute-done((bf16[1,128,2048]{2,1,0:T(8,128)(2,1)S(1)}, bf16[1,128,2048]{2,1,0:T(8,128)(2,1)S(1)}, u32[]{:S(2)}, u32[]{:S(2)}) %collective-permute-start.66) | collective-permute-done | bytes 524320 | tf_op jit(solution)/shard_map/ppermute | solution.py:46
  694.8 8.6 %collective-permute-done.62 = bf16[128,1408]{1,0:T(8,128)(2,1)} collective-permute-done((bf16[128,1408]{1,0:T(8,128)(2,1)}, bf16[128,1408]{1,0:T(8,128)(2,1)}, u32[]{:S(2)}, u32[]{:S(2)}) %collective-permute-start.62) | collective-permute-done | bytes 360480 | tf_op jit(solution)/shard_map/ppermute | solution.py:46
  (438 shorter events, 225.6 us)
Async XLA Ops:
  7.2 280.8 %all-gather.5.cloned.1.call-start = ((), (), s32[]{:S(2)}) async-start(), calls=%async_computation.3 | async-start | bytes 15728640 | tf_op jit(solution)/shard_map/all_gather | solution.py:467
  7.9 280.0 %all-gather.3.cloned.1.call-start = ((), (), s32[]{:S(2)}) async-start(), calls=%async_computation.2 | async-start | bytes 31457280 | tf_op jit(solution)/shard_map/all_gather | solution.py:466
  8.7 573.0 %reduce-scatter.5.cloned.1.call-start = ((), (), s32[]{:S(2)}) async-start(), calls=%async_computation.5 | async-start | bytes 15728640 | tf_op jit(solution)/shard_map/reduce_scatter | solution.py:597
  14.3 36.3 %collective-permute-start.4 = (bf16[784,512]{1,0:T(8,128)(2,1)S(1)}, bf16[784,512]{1,0:T(8,128)(2,1)}, u32[]{:S(2)}, u32[]{:S(2)}) collective-permute-start(bf16[784,512]{1,0:T(8,128)(2,1)S(1)} %pad_maximum_fusion.1.refs_4_), channel_id=1, source_target_pairs={{0,2},{1,3},{2,0},{3,1},{4,6},{5,7},{6,4},{7,5},{8,10},{9,11},{10,... | collective-permute-start | bytes 2408456 | tf_op jit(solution)/shard_map/ppermute | solution.py:46
  14.4 68.8 %collective-permute-start.6 = (bf16[784,512]{1,0:T(8,128)(2,1)S(1)}, bf16[784,512]{1,0:T(8,128)(2,1)}, u32[]{:S(2)}, u32[]{:S(2)}) collective-permute-start(bf16[784,512]{1,0:T(8,128)(2,1)S(1)} %pad_maximum_fusion.1.refs_4_), channel_id=1, source_target_pairs={{0,4},{1,5},{2,6},{3,7},{4,0},{5,1},{6,2},{7,3},{8,12},{9,13},{10,... | collective-permute-start | bytes 2408456 | tf_op jit(solution)/shard_map/ppermute | solution.py:46
  33.1 72.3 %collective-permute-start.3 = (bf16[784,512]{1,0:T(8,128)(2,1)S(1)}, bf16[784,512]{1,0:T(8,128)(2,1)}, u32[]{:S(2)}, u32[]{:S(2)}) collective-permute-start(bf16[784,512]{1,0:T(8,128)(2,1)S(1)} %pad_maximum_fusion.1.refs_4_), channel_id=1, source_target_pairs={{0,1},{1,0},{2,3},{3,2},{4,5},{5,4},{6,7},{7,6},{8,9},{9,8},{10,11... | collective-permute-start | bytes 2408456 | tf_op jit(solution)/shard_map/ppermute | solution.py:46
  34.5 50.1 %collective-permute-start.2 = (bf16[128,2048]{1,0:T(8,128)(2,1)S(1)}, bf16[128,2048]{1,0:T(8,128)(2,1)S(1)}, u32[]{:S(2)}, u32[]{:S(2)}) collective-permute-start(bf16[128,2048]{1,0:T(8,128)(2,1)S(1)} %collective-permute-done.refs_1_), channel_id=1, source_target_pairs={{0,8},{8,0},{16,24},{24,16},{1,9},{9,1},{17,25},{25,17},{2,10},{10... | collective-permute-start | bytes 1572872 | tf_op jit(solution)/shard_map/ppermute | solution.py:46
  34.5 55.8 %collective-permute-start.9 = (bf16[784,512]{1,0:T(8,128)(2,1)}, bf16[784,512]{1,0:T(8,128)(2,1)}, u32[]{:S(2)}, u32[]{:S(2)}) collective-permute-start(bf16[784,512]{1,0:T(8,128)(2,1)} %collective-permute-done.8.refs_10_), channel_id=1, source_target_pairs={{0,1},{1,0},{2,3},{3,2},{4,5},{5,4},{6,7},{7,6},{8,9},{9,8},{10,11... | collective-permute-start | bytes 2408456 | tf_op jit(solution)/shard_map/ppermute | solution.py:46
  50.7 58.1 %collective-permute-start.5 = (bf16[784,512]{1,0:T(8,128)(2,1)}, bf16[784,512]{1,0:T(8,128)(2,1)}, u32[]{:S(2)}, u32[]{:S(2)}) collective-permute-start(bf16[784,512]{1,0:T(8,128)(2,1)} %collective-permute-done.4.refs_6_), channel_id=1, source_target_pairs={{0,1},{1,0},{2,3},{3,2},{4,5},{5,4},{6,7},{7,6},{8,9},{9,8},{10,11... | collective-permute-start | bytes 2408456 | tf_op jit(solution)/shard_map/ppermute | solution.py:46
  83.1 48.1 %collective-permute-start.7 = (bf16[784,512]{1,0:T(8,128)(2,1)}, bf16[784,512]{1,0:T(8,128)(2,1)}, u32[]{:S(2)}, u32[]{:S(2)}) collective-permute-start(bf16[784,512]{1,0:T(8,128)(2,1)} %collective-permute-done.6.refs_8_), channel_id=1, source_target_pairs={{0,1},{1,0},{2,3},{3,2},{4,5},{5,4},{6,7},{7,6},{8,9},{9,8},{10,11... | collective-permute-start | bytes 2408456 | tf_op jit(solution)/shard_map/ppermute | solution.py:46
  108.8 36.1 %collective-permute-start.11 = (bf16[64,2048]{1,0:T(8,128)(2,1)S(1)}, bf16[64,2048]{1,0:T(8,128)(2,1)S(1)}, u32[]{:S(2)}, u32[]{:S(2)}) collective-permute-start(bf16[64,2048]{1,0:T(8,128)(2,1)S(1)} %collective-permute-done.10.refs_0_), channel_id=1, source_target_pairs={{0,1},{1,0},{2,3},{3,2},{4,5},{5,4},{6,7},{7,6},{8,9},{9,8},{10,11... | collective-permute-start | bytes 786440 | tf_op jit(solution)/shard_map/ppermute | solution.py:46
  159.3 47.2 %collective-permute-start.22 = (bf16[128,2048]{1,0:T(8,128)(2,1)}, bf16[128,2048]{1,0:T(8,128)(2,1)S(1)}, u32[]{:S(2)}, u32[]{:S(2)}) collective-permute-start(bf16[128,2048]{1,0:T(8,128)(2,1)} %bitcast.25.refs_7_), channel_id=1, source_target_pairs={{0,4},{1,5},{2,6},{3,7},{4,0},{5,1},{6,2},{7,3},{8,12},{9,13},{10,... | collective-permute-start | bytes 1572872 | tf_op jit(solution)/shard_map/ppermute | solution.py:46
  161.9 47.9 %collective-permute-start.24 = (bf16[128,2048]{1,0:T(8,128)(2,1)}, bf16[128,2048]{1,0:T(8,128)(2,1)S(1)}, u32[]{:S(2)}, u32[]{:S(2)}) collective-permute-start(bf16[128,2048]{1,0:T(8,128)(2,1)} %bitcast.25.refs_7_), channel_id=1, source_target_pairs={{0,2},{1,3},{2,0},{3,1},{4,6},{5,7},{6,4},{7,5},{8,10},{9,11},{10,... | collective-permute-start | bytes 1572872 | tf_op jit(solution)/shard_map/ppermute | solution.py:46
  207.5 38.6 %collective-permute-start.30 = (bf16[128,2048]{1,0:T(8,128)(2,1)}, bf16[128,2048]{1,0:T(8,128)(2,1)}, u32[]{:S(2)}, u32[]{:S(2)}) collective-permute-start(bf16[128,2048]{1,0:T(8,128)(2,1)} %multiply_convert_fusion.4.refs_0_), channel_id=1, source_target_pairs={{0,4},{1,5},{2,6},{3,7},{4,0},{5,1},{6,2},{7,3},{8,12},{9,13},{10,... | collective-permute-start | bytes 1572872 | tf_op jit(solution)/shard_map/ppermute | solution.py:46
  209.9 37.6 %collective-permute-start.32 = (bf16[128,2048]{1,0:T(8,128)(2,1)}, bf16[128,2048]{1,0:T(8,128)(2,1)}, u32[]{:S(2)}, u32[]{:S(2)}) collective-permute-start(bf16[128,2048]{1,0:T(8,128)(2,1)} %multiply_convert_fusion.4.refs_0_), channel_id=1, source_target_pairs={{0,6},{1,7},{2,4},{3,5},{4,2},{5,3},{6,0},{7,1},{8,14},{9,15},{10,... | collective-permute-start | bytes 1572872 | tf_op jit(solution)/shard_map/ppermute | solution.py:46
  233.4 33.8 %collective-permute-start.27 = (bf16[128,2048]{1,0:T(8,128)(2,1)}, bf16[128,2048]{1,0:T(8,128)(2,1)}, u32[]{:S(2)}, u32[]{:S(2)}) collective-permute-start(bf16[128,2048]{1,0:T(8,128)(2,1)} %multiply_convert_fusion.4.refs_0_), channel_id=1, source_target_pairs={{0,1},{1,0},{2,3},{3,2},{4,5},{5,4},{6,7},{7,6},{8,9},{9,8},{10,11... | collective-permute-start | bytes 1572872 | tf_op jit(solution)/shard_map/ppermute | solution.py:46
  234.1 33.1 %collective-permute-start.29 = (bf16[128,2048]{1,0:T(8,128)(2,1)}, bf16[128,2048]{1,0:T(8,128)(2,1)}, u32[]{:S(2)}, u32[]{:S(2)}) collective-permute-start(bf16[128,2048]{1,0:T(8,128)(2,1)} %collective-permute-done.28.refs_2_), channel_id=1, source_target_pairs={{0,1},{1,0},{2,3},{3,2},{4,5},{5,4},{6,7},{7,6},{8,9},{9,8},{10,11... | collective-permute-start | bytes 1572872 | tf_op jit(solution)/shard_map/ppermute | solution.py:46
  246.1 31.6 %collective-permute-start.31 = (bf16[128,2048]{1,0:T(8,128)(2,1)}, bf16[128,2048]{1,0:T(8,128)(2,1)}, u32[]{:S(2)}, u32[]{:S(2)}) collective-permute-start(bf16[128,2048]{1,0:T(8,128)(2,1)} %collective-permute-done.30.refs_4_), channel_id=1, source_target_pairs={{0,1},{1,0},{2,3},{3,2},{4,5},{5,4},{6,7},{7,6},{8,9},{9,8},{10,11... | collective-permute-start | bytes 1572872 | tf_op jit(solution)/shard_map/ppermute | solution.py:46
  247.5 40.4 %collective-permute-start.33 = (bf16[128,2048]{1,0:T(8,128)(2,1)}, bf16[128,2048]{1,0:T(8,128)(2,1)}, u32[]{:S(2)}, u32[]{:S(2)}) collective-permute-start(bf16[128,2048]{1,0:T(8,128)(2,1)} %collective-permute-done.32.refs_6_), channel_id=1, source_target_pairs={{0,1},{1,0},{2,3},{3,2},{4,5},{5,4},{6,7},{7,6},{8,9},{9,8},{10,11... | collective-permute-start | bytes 1572872 | tf_op jit(solution)/shard_map/ppermute | solution.py:46
  334.6 352.1 %reduce-scatter.3.cloned.1.call-start = ((), (), s32[]{:S(2)}) async-start(), calls=%async_computation.4 | async-start | bytes 31457280 | tf_op jit(solution)/shard_map/reduce_scatter | solution.py:604
  379.2 35.7 %collective-permute-start.34 = (bf16[4,128,1408]{2,1,0:T(8,128)(2,1)}, bf16[4,128,1408]{2,1,0:T(8,128)(2,1)S(1)}, u32[]{:S(2)}, u32[]{:S(2)}) collective-permute-start(bf16[4,128,1408]{2,1,0:T(8,128)(2,1)} %slice_bitcast_fusion.1), channel_id=1, source_target_pairs={{0,1},{1,0},{2,3},{3,2},{4,5},{5,4},{6,7},{7,6},{8,9},{9,8},{10,11... | collective-permute-start | bytes 4325384 | tf_op jit(solution)/shard_map/ppermute | solution.py:46
  468.7 59.0 %collective-permute-start.38 = (bf16[4,128,1408]{2,1,0:T(8,128)(2,1)}, bf16[4,128,1408]{2,1,0:T(8,128)(2,1)}, u32[]{:S(2)}, u32[]{:S(2)}) collective-permute-start(bf16[4,128,1408]{2,1,0:T(8,128)(2,1)} %slice_bitcast_fusion), channel_id=1, source_target_pairs={{0,1},{1,0},{2,3},{3,2},{4,5},{5,4},{6,7},{7,6},{8,9},{9,8},{10,11... | collective-permute-start | bytes 4325384 | tf_op jit(solution)/shard_map/ppermute | solution.py:46
  488.7 44.3 %collective-permute-start.49 = (bf16[4,64,1408]{2,1,0:T(8,128)(2,1)}, bf16[4,64,1408]{2,1,0:T(8,128)(2,1)}, u32[]{:S(2)}, u32[]{:S(2)}) collective-permute-start(bf16[4,64,1408]{2,1,0:T(8,128)(2,1)} %slice_bitcast_fusion.2), channel_id=1, source_target_pairs={{0,1},{1,0},{2,3},{3,2},{4,5},{5,4},{6,7},{7,6},{8,9},{9,8},{10,11... | collective-permute-start | bytes 2162696 | tf_op jit(solution)/shard_map/ppermute | solution.py:46
  491.1 39.9 %collective-permute-start.52 = (bf16[2,64,640]{2,1,0:T(8,128)(2,1)}, bf16[2,64,640]{2,1,0:T(8,128)(2,1)}, u32[]{:S(2)}, u32[]{:S(2)}) collective-permute-start(bf16[2,64,640]{2,1,0:T(8,128)(2,1)} %get-tuple-element.149), channel_id=1, source_target_pairs={{0,6},{1,7},{2,4},{3,5},{4,2},{5,3},{6,0},{7,1},{8,14},{9,15},{10,... | collective-permute-start | bytes 491528 | tf_op jit(solution)/shard_map/ppermute | solution.py:46
  492.3 38.7 %collective-permute-start.51 = (bf16[2,64,640]{2,1,0:T(8,128)(2,1)}, bf16[2,64,640]{2,1,0:T(8,128)(2,1)}, u32[]{:S(2)}, u32[]{:S(2)}) collective-permute-start(bf16[2,64,640]{2,1,0:T(8,128)(2,1)} %get-tuple-element.150), channel_id=1, source_target_pairs={{0,4},{1,5},{2,6},{3,7},{4,0},{5,1},{6,2},{7,3},{8,12},{9,13},{10,... | collective-permute-start | bytes 491528 | tf_op jit(solution)/shard_map/ppermute | solution.py:46
  492.3 38.7 %collective-permute-start.50 = (bf16[2,64,640]{2,1,0:T(8,128)(2,1)}, bf16[2,64,640]{2,1,0:T(8,128)(2,1)}, u32[]{:S(2)}, u32[]{:S(2)}) collective-permute-start(bf16[2,64,640]{2,1,0:T(8,128)(2,1)} %get-tuple-element.148), channel_id=1, source_target_pairs={{0,2},{1,3},{2,0},{3,1},{4,6},{5,7},{6,4},{7,5},{8,10},{9,11},{10,... | collective-permute-start | bytes 491528 | tf_op jit(solution)/shard_map/ppermute | solution.py:46
  534.5 54.9 %collective-permute-start.53 = (bf16[4,512,512]{2,1,0:T(8,128)(2,1)}, bf16[4,512,512]{2,1,0:T(8,128)(2,1)}, u32[]{:S(2)}, u32[]{:S(2)}) collective-permute-start(bf16[4,512,512]{2,1,0:T(8,128)(2,1)} %get-tuple-element.99), channel_id=1, source_target_pairs={{0,1},{1,0},{2,3},{3,2},{4,5},{5,4},{6,7},{7,6},{8,9},{9,8},{10,11... | collective-permute-start | bytes 6291464 | tf_op jit(solution)/shard_map/ppermute | solution.py:46
  536.2 45.2 %collective-permute-start.58 = (bf16[2,272,512]{2,1,0:T(8,128)(2,1)S(1)}, bf16[2,272,512]{2,1,0:T(8,128)(2,1)S(1)}, u32[]{:S(2)}, u32[]{:S(2)}) collective-permute-start(bf16[2,272,512]{2,1,0:T(8,128)(2,1)S(1)} %copy-done.82), channel_id=1, source_target_pairs={{0,4},{1,5},{2,6},{3,7},{4,0},{5,1},{6,2},{7,3},{8,12},{9,13},{10,... | collective-permute-start | bytes 1671176 | tf_op jit(solution)/shard_map/ppermute | solution.py:46
  536.8 44.6 %collective-permute-start.57 = (bf16[2,272,512]{2,1,0:T(8,128)(2,1)S(1)}, bf16[2,272,512]{2,1,0:T(8,128)(2,1)S(1)}, u32[]{:S(2)}, u32[]{:S(2)}) collective-permute-start(bf16[2,272,512]{2,1,0:T(8,128)(2,1)S(1)} %copy-done.81), channel_id=1, source_target_pairs={{0,2},{1,3},{2,0},{3,1},{4,6},{5,7},{6,4},{7,5},{8,10},{9,11},{10,... | collective-permute-start | bytes 1671176 | tf_op jit(solution)/shard_map/ppermute | solution.py:46
  540.7 96.2 %collective-permute-start.65 = (bf16[2,128,2048]{2,1,0:T(8,128)(2,1)}, bf16[2,128,2048]{2,1,0:T(8,128)(2,1)}, u32[]{:S(2)}, u32[]{:S(2)}) collective-permute-start(bf16[2,128,2048]{2,1,0:T(8,128)(2,1)} %bitcast.100), channel_id=1, source_target_pairs={{0,8},{8,0},{16,24},{24,16},{1,9},{9,1},{17,25},{25,17},{2,10},{10... | collective-permute-start | bytes 3145736 | tf_op jit(solution)/shard_map/ppermute | solution.py:46
  592.2 42.4 %collective-permute-start.55 = (bf16[512,512]{1,0:T(8,128)(2,1)S(1)}, bf16[512,512]{1,0:T(8,128)(2,1)S(1)}, u32[]{:S(2)}, u32[]{:S(2)}) collective-permute-start(bf16[512,512]{1,0:T(8,128)(2,1)S(1)} %get-tuple-element.101), channel_id=1, source_target_pairs={{0,4},{1,5},{2,6},{3,7},{4,0},{5,1},{6,2},{7,3},{8,12},{9,13},{10,... | collective-permute-start | bytes 1572872 | tf_op jit(solution)/shard_map/ppermute | solution.py:46
  592.2 42.4 %collective-permute-start.54 = (bf16[512,512]{1,0:T(8,128)(2,1)S(1)}, bf16[512,512]{1,0:T(8,128)(2,1)S(1)}, u32[]{:S(2)}, u32[]{:S(2)}) collective-permute-start(bf16[512,512]{1,0:T(8,128)(2,1)S(1)} %get-tuple-element.100), channel_id=1, source_target_pairs={{0,2},{1,3},{2,0},{3,1},{4,6},{5,7},{6,4},{7,5},{8,10},{9,11},{10,... | collective-permute-start | bytes 1572872 | tf_op jit(solution)/shard_map/ppermute | solution.py:46
  (140 other events, 3188.3 us)
Sparse Core Ops, SparseCore 0:
  9.6 96.2 all-gather.4
  107.4 169.0 all-gather.2
  334.7 97.4 reduce-scatter.4
  453.7 179.9 reduce-scatter.2
